TPU v7x, 256 devices: a whole 4x4x8 slice. The times are simulated.
256 devices in a mesh: seq: 32 (over x, z), ch: 8 (over y, core).
Axes of the slice: x: 4, y: 4, z: 8, core: 2. Of those that a mesh axis runs over, the one named last changes fastest.
Arguments:
- signal: bfloat16 [8192, 2048], P('seq', 'ch'), may hold values from -6 to 6
- conv_taps: float32 [2, 4, 2048], P(None, None, 'ch'), may hold values from -3 to 3
- dilations: int32 [2], replicated, may hold values from 1 to 16, as said below
- decays: float32 [2, 2048], P(None, 'ch'), may hold values from 0.96 to 1
- retention: float32 [8192], P('seq'), may hold values from 0.5 to 1
- readout: float32 [2, 2048], P(None, 'ch'), may hold values from -4 to 4
- skip_gain: float32 [2048], P('ch'), may hold values from 0.5 to 1.5
- w_out: bfloat16 [2048, 2048], P('ch'), may hold values from -0.125 to 0.125
- cotangent: bfloat16 [8192, 2048], P('seq', 'ch'), may hold values from -6 to 6
Outputs:
- output: bfloat16 [8192, 2048], P('seq', 'ch')
- grad_signal: bfloat16 [8192, 2048], P('seq', 'ch')
- grad_w_out: float32 [2048, 2048], P('ch', 'seq')
Inputs may be any that keep to these rules, and one draw needn't show every extreme that they name: `dilations`: one of the two equals 16, the other is smaller.
All inputs are finite; a program needn't handle non-finite values.
Results may differ from a plain program's by a relative error of at most 0.0042.
Values may be sent and summed in bfloat16 or wider, within the bound.
No kernel may reach another device: no remote copies, remote signals or barrier semaphores. Data moves between devices by JAX's collectives and lax.ppermute only.
A program may use at most 64 MiB of HBM per device.

v0:
```python
import jax
import jax.numpy as jnp
from jax import lax
from jax.sharding import PartitionSpec as P

K = 4
DMAX = 16


def shifted(block, axis, distance):
    devices = range(lax.axis_size(axis))
    route = [(i - distance, i) for i in devices if i - distance in devices]
    return lax.ppermute(block, axis, route)


def carried_in(value, axis, join, neutral, backward):
    count, mine = (lax.axis_size(axis), lax.axis_index(axis))
    pieces = jax.tree.map(lambda part: lax.all_gather(part, axis), value)
    if backward:
        pieces = jax.tree.map(lambda part: part[::-1], pieces)
        mine = count - 1 - mine
    total = jax.tree.map(
        lambda part, zero: jnp.full_like(part, 0) + jnp.asarray(zero, part.dtype), value, neutral
    )

    def lap(position, total):
        longer = join(total, jax.tree.map(lambda part: part[position], pieces))
        return jax.tree.map(lambda new, old: jnp.where(position < mine, new, old), longer, total)

    return lax.fori_loop(0, count - 1, lap, total)


def for_sending(array):

    def short(part):
        return part.astype(jnp.bfloat16) if part.dtype == jnp.float32 else part

    return jax.tree.map(short, array)


def combine(earlier, later):
    return (earlier[0] * later[0], later[0] * earlier[1] + later[1])


def per_device(
    signal, conv_taps, dilations, decays, retention, readout, skip_gain, w_out, cotangent
):
    rows = signal.shape[0]
    margin = (K - 1) * DMAX
    reach = 2 * margin
    first_gap = dilations[0]
    second_gap = dilations[1]
    earlier_rows = shifted(signal[rows - reach :], "seq", 1)
    extended = jnp.concatenate([earlier_rows, signal], axis=0).astype(jnp.float32)
    padded = jnp.pad(extended, ((margin, 0), (0, 0)))
    first = jnp.zeros(extended.shape, jnp.float32)
    for lag_index in range(K):
        first = first + conv_taps[0, lag_index] * lax.dynamic_slice_in_dim(
            padded, margin - lag_index * first_gap, rows + reach, 0
        )
    driven = jnp.zeros(signal.shape, jnp.float32)
    for lag_index in range(K):
        driven = driven + conv_taps[1, lag_index] * lax.dynamic_slice_in_dim(
            first, reach - lag_index * second_gap, rows, 0
        )
    gamma = jnp.sqrt(1.0 - decays * decays)
    factor = decays[None, :, :] * retention[:, None, None]
    inputs = gamma[None, :, :] * driven[:, None, :]
    running, local_state = lax.associative_scan(combine, (factor, inputs), axis=0)
    unit = jnp.ones(decays.shape, jnp.float32)
    nothing = jnp.zeros(decays.shape, jnp.float32)
    entering = carried_in((running[-1], local_state[-1]), "seq", combine, (unit, nothing), False)[1]
    state = local_state + running * entering[None]
    mixed = (readout[0] * state[:, 0, :] + readout[1] * state[:, 1, :] + skip_gain * driven).astype(
        jnp.bfloat16
    )
    partial_value = jnp.dot(mixed, w_out, preferred_element_type=jnp.float32)
    projected = lax.psum_scatter(partial_value, "ch", scatter_dimension=1, tiled=True)
    output = (signal.astype(jnp.float32) + projected).astype(jnp.bfloat16)
    all_cotangent = lax.all_gather(cotangent, "ch", axis=1, tiled=True)
    grad_mixed = lax.dot_general(
        all_cotangent, w_out, (((1,), (1,)), ((), ())), preferred_element_type=jnp.float32
    )
    weight_part = lax.dot_general(
        mixed, all_cotangent, (((0,), (0,)), ((), ())), preferred_element_type=jnp.float32
    )
    grad_w_out = lax.psum_scatter(weight_part, "seq", scatter_dimension=1, tiled=True)
    emitted = readout[None, :, :] * grad_mixed[:, None, :]
    backward_run, local_passed = lax.associative_scan(
        combine, (factor, factor * emitted), axis=0, reverse=True
    )
    arriving = carried_in(
        (backward_run[0], local_passed[0]), "seq", combine, (unit, nothing), True
    )[1]
    passed = local_passed + backward_run * arriving[None]
    following = jnp.concatenate([passed[1:], arriving[None]], axis=0)
    grad_state = emitted + following
    grad_driven = skip_gain * grad_mixed + (
        gamma[0] * grad_state[:, 0, :] + gamma[1] * grad_state[:, 1, :]
    )
    later_rows = shifted(for_sending(grad_driven[:reach]), "seq", -1)
    ahead = jnp.concatenate([grad_driven, later_rows], axis=0)
    grad_first = jnp.zeros((rows + margin, grad_driven.shape[1]), jnp.float32)
    for lag_index in range(K):
        grad_first = grad_first + conv_taps[1, lag_index] * lax.dynamic_slice_in_dim(
            ahead, lag_index * second_gap, rows + margin, 0
        )
    grad_branch = jnp.zeros(signal.shape, jnp.float32)
    for lag_index in range(K):
        grad_branch = grad_branch + conv_taps[0, lag_index] * lax.dynamic_slice_in_dim(
            grad_first, lag_index * first_gap, rows, 0
        )
    grad_signal = (cotangent.astype(jnp.float32) + grad_branch).astype(jnp.bfloat16)
    return (output, grad_signal, grad_w_out)


def solution(mesh):
    return jax.shard_map(
        per_device,
        mesh=mesh,
        in_specs=(
            P("seq", "ch"),
            P(None, None, "ch"),
            P(),
            P(None, "ch"),
            P("seq"),
            P(None, "ch"),
            P("ch"),
            P("ch", None),
            P("seq", "ch"),
        ),
        out_specs=(P("seq", "ch"), P("seq", "ch"), P("ch", "seq")),
        check_vma=False,
    )
```

profile of v0, /device:TPU:2, one launch (start us, length us, event | category | flops | bytes accessed | tf_op | source)
XLA Modules:
  0.0 720.0 jit_solution(5474295419296595748)
XLA Ops:
  8.8 3.8 collective-permute-start
  27.1 11.6 %all-gather.2.cloned.1.call-done = bf16[256,2048]{1,0:T(8,128)(2,1)} async-done(((bf16[256,256]{1,0:T(8,128)(2,1)}), bf16[256,2048]{1,0:T(8,128)(2,1)}) %all-gather.2.cloned.1.call-update) | async-done | bytes 1048592 | tf_op jit(solution)/shard_map/all_gather | solution.py:80
  41.9 2.9 slice.661
  48.8 2.0 multiply_add_fusion.2
  57.7 1.8 multiply_add_fusion.4
  129.9 3.0 slice.716
  136.7 2.3 pad.245
  140.7 2.6 pad.248
  143.9 1.9 fusion.28
  148.9 1.9 add.552
  152.7 2.5 pad.263
  156.5 1.9 add.560
  208.0 48.8 %all_gather.18 = f32[32,2,256]{2,1,0:T(2,128)S(1)} all-gather(f32[1,2,256]{2,1,0:T(2,128)S(1)} %copy.18), channel_id=1, replica_groups=mesh['seq'=32,'ch'=8] {'seq'}, dimensions={0}, use_global_device_ids=true | all-gather | bytes 67584 | tf_op jit(solution)/shard_map/all_gather | solution.py:18
  257.4 46.9 %all_gather.19 = f32[32,2,256]{2,1,0:T(2,128)S(1)} all-gather(f32[1,2,256]{2,1,0:T(2,128)S(1)} %copy.19), channel_id=1, replica_groups=mesh['seq'=32,'ch'=8] {'seq'}, dimensions={0}, use_global_device_ids=true | all-gather | bytes 67584 | tf_op jit(solution)/shard_map/all_gather | solution.py:18
  304.4 39.0 %while.29 = (s32[]{:T(128)}, f32[2,256]{1,0:T(2,128)}, s32[]{:T(128)}, f32[32,2,256]{2,1,0:T(2,128)S(1)}, f32[32,2,256]{2,1,0:T(2,128)S(1)}, /*index=5*/s32[]{:T(128)}, s32[]{:T(128)}) while((s32[]{:T(128)}, f32[2,256]{1,0:T(2,128)}, s32[]{:T(128)}, f32[32,2,256]{2,1,0:T(2,128)S(1)}, f32[32,2,256]{2,1,0:T(2,128)S(1)}, ...), condition=%wide.region_4.5_spmd.clone, body=%wide.region_3.4_spmd.clone.sunk | while | flops 2052 | bytes 8301 | solution.py:30
  344.7 2.6 rev.14
  347.3 2.6 rev.15
  352.4 1.7 fusion.34
  358.8 47.3 %all_gather.15 = f32[32,2,256]{2,1,0:T(2,128)S(1)} all-gather(f32[1,2,256]{2,1,0:T(2,128)S(1)} %copy.16), channel_id=1, replica_groups=mesh['seq'=32,'ch'=8] {'seq'}, dimensions={0}, use_global_device_ids=true | all-gather | bytes 67584 | tf_op jit(solution)/shard_map/all_gather | solution.py:18
  406.8 47.0 %all_gather.16 = f32[32,2,256]{2,1,0:T(2,128)S(1)} all-gather(f32[1,2,256]{2,1,0:T(2,128)S(1)} %copy.17), channel_id=1, replica_groups=mesh['seq'=32,'ch'=8] {'seq'}, dimensions={0}, use_global_device_ids=true | all-gather | bytes 67584 | tf_op jit(solution)/shard_map/all_gather | solution.py:18
  459.1 1.9 fusion.66
  461.1 4.6 collective-permute-start.1
  470.8 24.0 %reduce-scatter.3.cloned.1.call-done = f32[256,256]{1,0:T(8,128)} async-done(((f32[256,2048]{1,0:T(8,128)}), f32[256,256]{1,0:T(8,128)}) %reduce-scatter.3.cloned.1.call-update) | async-done | bytes 262160 | tf_op jit(solution)/shard_map/reduce_scatter | solution.py:78
  496.4 217.0 %reduce-scatter.5.cloned.1.call-done = f32[256,64]{0,1:T(8,128)} async-done(((f32[256,2048]{0,1:T(8,128)}), f32[256,64]{0,1:T(8,128)}) %reduce-scatter.5.cloned.1.call-update) | async-done | bytes 65552 | tf_op jit(solution)/shard_map/reduce_scatter | solution.py:87
  (484 shorter events, 213.5 us)
Async XLA Ops:
  7.2 31.6 %all-gather.2.cloned.1.call-start = ((), (), s32[]{:S(2)}) async-start(), calls=%async_computation.3 | async-start | bytes 1179648 | tf_op jit(solution)/shard_map/all_gather | solution.py:80
  7.9 486.9 %reduce-scatter.3.cloned.1.call-start = ((), (), s32[]{:S(2)}) async-start(), calls=%async_computation.2 | async-start | bytes 2359296 | tf_op jit(solution)/shard_map/reduce_scatter | solution.py:78
  8.8 13.9 %collective-permute-start = (bf16[96,256]{1,0:T(8,128)(2,1)S(1)}, bf16[96,256]{1,0:T(8,128)(2,1)S(1)}, u32[]{:S(2)}, u32[]{:S(2)}) collective-permute-start(bf16[96,256]{1,0:T(8,128)(2,1)S(1)} %slice.565), channel_id=1, source_target_pairs={{0,8},{8,16},{16,24},{24,32},{32,40},{40,48},{48,56},{56,64},{64,7... | collective-permute-start | bytes 147464 | tf_op jit(solution)/shard_map/ppermute | solution.py:13
  160.4 184.2 %copy-start.2 = (f32[256,2,256]{2,0,1:T(8,128)S(1)}, f32[256,2,256]{2,0,1:T(8,128)}, u32[]{:S(2)}) copy-start(f32[256,2,256]{2,0,1:T(8,128)} %add.552) | copy-start | bytes 1572868
  162.5 184.9 %copy-start.3 = (f32[256,2,256]{2,0,1:T(8,128)S(1)}, f32[256,2,256]{2,0,1:T(8,128)}, u32[]{:S(2)}) copy-start(f32[256,2,256]{2,0,1:T(8,128)} %add.560) | copy-start | bytes 1572868
  197.3 153.0 %copy-start.21 = (f32[7,2,256]{2,0,1:T(8,128)S(1)}, f32[7,2,256]{2,0,1:T(8,128)}, u32[]{:S(2)}) copy-start(f32[7,2,256]{2,0,1:T(8,128)} %slice.624) | copy-start | bytes 43012
  206.0 143.9 %copy-start.61 = (f32[1,2,256]{2,0,1:T(1,128)S(1)}, f32[1,2,256]{2,0,1:T(1,128)}, u32[]{:S(2)}) copy-start(f32[1,2,256]{2,0,1:T(1,128)} %get-tuple-element.311) | copy-start | bytes 6148
  206.0 143.9 %copy-start.62 = (f32[1,2,256]{2,0,1:T(1,128)S(1)}, f32[1,2,256]{2,0,1:T(1,128)}, u32[]{:S(2)}) copy-start(f32[1,2,256]{2,0,1:T(1,128)} %get-tuple-element.312) | copy-start | bytes 6148
  206.0 143.9 %copy-start.63 = (f32[1,2,256]{2,0,1:T(1,128)S(1)}, f32[1,2,256]{2,0,1:T(1,128)}, u32[]{:S(2)}) copy-start(f32[1,2,256]{2,0,1:T(1,128)} %get-tuple-element.313) | copy-start | bytes 6148
  206.0 143.9 %copy-start.64 = (f32[1,2,256]{2,0,1:T(1,128)S(1)}, f32[1,2,256]{2,0,1:T(1,128)}, u32[]{:S(2)}) copy-start(f32[1,2,256]{2,0,1:T(1,128)} %get-tuple-element.314) | copy-start | bytes 6148
  206.0 144.0 %copy-start.28 = (f32[2,2,256]{2,0,1:T(2,128)S(1)}, f32[2,2,256]{2,0,1:T(2,128)}, u32[]{:S(2)}) copy-start(f32[2,2,256]{2,0,1:T(2,128)} %get-tuple-element.352) | copy-start | bytes 12292
  206.0 144.1 %copy-start.27 = (f32[2,2,256]{2,0,1:T(2,128)S(1)}, f32[2,2,256]{2,0,1:T(2,128)}, u32[]{:S(2)}) copy-start(f32[2,2,256]{2,0,1:T(2,128)} %get-tuple-element.351) | copy-start | bytes 12292
  206.0 144.1 %copy-start.23 = (f32[3,2,256]{2,0,1:T(4,128)S(1)}, f32[3,2,256]{2,0,1:T(4,128)}, u32[]{:S(2)}) copy-start(f32[3,2,256]{2,0,1:T(4,128)} %slice.622) | copy-start | bytes 18436
  206.0 144.1 %copy-start.24 = (f32[3,2,256]{2,0,1:T(4,128)S(1)}, f32[3,2,256]{2,0,1:T(4,128)}, u32[]{:S(2)}) copy-start(f32[3,2,256]{2,0,1:T(4,128)} %slice.605) | copy-start | bytes 18436
  206.0 144.2 %copy-start.60 = (f32[1,2,256]{2,0,1:T(1,128)S(1)}, f32[1,2,256]{2,0,1:T(1,128)}, u32[]{:S(2)}) copy-start(f32[1,2,256]{2,0,1:T(1,128)} %slice.744) | copy-start | bytes 6148
  206.1 144.2 %copy-start.59 = (f32[1,2,256]{2,0,1:T(1,128)S(1)}, f32[1,2,256]{2,0,1:T(1,128)}, u32[]{:S(2)}) copy-start(f32[1,2,256]{2,0,1:T(1,128)} %slice.770) | copy-start | bytes 6148
  206.1 144.3 %copy-start.22 = (f32[7,2,256]{2,0,1:T(8,128)S(1)}, f32[7,2,256]{2,0,1:T(8,128)}, u32[]{:S(2)}) copy-start(f32[7,2,256]{2,0,1:T(8,128)} %slice.599) | copy-start | bytes 43012
  206.1 144.3 %copy-start.58 = (f32[1,2,256]{2,0,1:T(1,128)S(1)}, f32[1,2,256]{2,0,1:T(1,128)}, u32[]{:S(2)}) copy-start(f32[1,2,256]{2,0,1:T(1,128)} %slice.743) | copy-start | bytes 6148
  206.7 143.9 %copy-start.57 = (f32[1,2,256]{2,0,1:T(1,128)S(1)}, f32[1,2,256]{2,0,1:T(1,128)}, u32[]{:S(2)}) copy-start(f32[1,2,256]{2,0,1:T(1,128)} %slice.769) | copy-start | bytes 6148
  206.7 144.0 %copy-start.18 = (f32[15,2,256]{2,0,1:T(8,128)S(1)}, f32[15,2,256]{2,0,1:T(8,128)}, u32[]{:S(2)}) copy-start(f32[15,2,256]{2,0,1:T(8,128)} %slice.593) | copy-start | bytes 92164
  206.7 144.0 %copy-start.56 = (f32[1,2,256]{2,0,1:T(1,128)S(1)}, f32[1,2,256]{2,0,1:T(1,128)}, u32[]{:S(2)}) copy-start(f32[1,2,256]{2,0,1:T(1,128)} %slice.742) | copy-start | bytes 6148
  356.1 100.2 %copy-start.19 = (f32[2,256]{1,0:T(2,128)S(1)}, f32[2,256]{1,0:T(2,128)}, u32[]{:S(2)}) copy-start(f32[2,256]{1,0:T(2,128)} %get-tuple-element.192) | copy-start | bytes 6148
  459.0 254.4 %reduce-scatter.5.cloned.1.call-start = ((), (), s32[]{:S(2)}) async-start(), calls=%async_computation.4 | async-start | bytes 2162688 | tf_op jit(solution)/shard_map/reduce_scatter | solution.py:87
  461.1 8.4 %collective-permute-start.1 = (bf16[96,256]{1,0:T(8,128)(2,1)S(1)}, bf16[96,256]{1,0:T(8,128)(2,1)S(1)}, u32[]{:S(2)}, u32[]{:S(2)}) collective-permute-start(bf16[96,256]{1,0:T(8,128)(2,1)S(1)} %slice.995), channel_id=1, source_target_pairs={{8,0},{16,8},{24,16},{32,24},{40,32},{48,40},{56,48},{64,56},{72,6... | collective-permute-start | bytes 147464 | tf_op jit(solution)/shard_map/ppermute | solution.py:13
  (52 other events, 529.1 us)
Sparse Core Ops, SparseCore 0:
  9.8 28.8 all-gather.1
  459.2 35.5 reduce-scatter.2
  499.2 214.1 reduce-scatter.4
where the time goes:
time: 727 us; the launch traced here: 720 us
  waiting for transfers between devices  253 us (35%)
  blocking collectives  190 us (26%)
  local copies, waits for them, and re-layouts  138 us (19%)
  other arithmetic  99.4 us (14%)
  between operations  24.3 us (3%)
  starting transfers between devices  8.53 us (1%)
    reduce_scatter x1, waiting for transfers between devices, per_device(): lax.psum_scatter(weight_part, 'seq', scatter_dimension=1, tiled=True)  217 us
    all_gather x4, blocking collectives, carried_in(): pieces = jax.tree.map(lambda part: lax.all_gather(part, axis), value)  190 us
    slice x56, local copies, waits for them, and re-layouts, per_device(): lax.associative_scan(combine, (factor, factor * emitted), axis=0, reverse...  65 us
    slice x51, local copies, waits for them, and re-layouts, per_device(): lax.associative_scan(combine, (factor, inputs), axis=0)  42.5 us
    select_n x62, other arithmetic, lap(): jnp.where(position < mine, new, old)  39.5 us
    add x27, other arithmetic, combine(): return (earlier[0] * later[0], later[0] * earlier[1] + later[1])  26.1 us
    reduce_scatter x1, waiting for transfers between devices, per_device(): lax.psum_scatter(partial_value, 'ch', scatter_dimension=1, tiled=True)  24 us
  transfers between devices with their start and end apart: 5, of which 3 were waited for; matrix products, arithmetic and copies ran while one was open for 2% of the time, Pallas kernels for 0%

commit v1 on v0

v1 whole, which is shorter than its diff:
```python
import functools
import jax
import jax.numpy as jnp
from jax import lax
from jax.experimental import pallas as pl
from jax.experimental.pallas import tpu as pltpu
from jax.sharding import PartitionSpec as P

K = 4
DMAX = 16
MARGIN = (K - 1) * DMAX
REACH = 2 * MARGIN
SEGS = 8
LANES = 128
ZSIZE = 8
F32 = jnp.float32
BF16 = jnp.bfloat16


def spread_rows(row):
    return jnp.transpose(jnp.broadcast_to(row, (LANES, row.shape[1])))


def row_of(value, index):
    return value[index : index + 1]


def power(value, exponent):
    while exponent > 1:
        value = value * value
        exponent //= 2
    return value


def halves(count):
    return [(half, slice(half * LANES, (half + 1) * LANES)) for half in range(count // LANES)]


def lanes_of(ref, which, cols):
    return ref[which : which + 1, cols]


def fill_copies(pay_ref, rows):
    tile = jnp.concatenate(rows, axis=0)
    for copy in range(pay_ref.shape[0] // 8):
        pay_ref[8 * copy : 8 * copy + 8, :] = tile


def forward_local(
    dil_ref, halo_ref, sig_ref, taps_ref, dec_ref, ret_ref,
    drv_ref, pay_ref, segh_ref, segp_ref,
    ext_ref, first_ref, rb_ref,
):
    rows, width = sig_ref.shape
    steps = rows // SEGS
    rb_ref[...] = spread_rows(ret_ref[...])
    ends = [[None] * 2 for _ in range(2)]
    prods = [[None] * 2 for _ in range(2)]
    for half, cols in halves(width):
        ext_ref[0:REACH, :] = halo_ref[:, cols].astype(F32)
        ext_ref[REACH : REACH + rows, :] = sig_ref[:, cols].astype(F32)
        total = jnp.zeros((rows + MARGIN, LANES), F32)
        for k in range(K):
            total = total + taps_ref[0, k : k + 1, cols] * ext_ref[
                pl.ds(MARGIN - k * dil_ref[0], rows + MARGIN), :
            ]
        first_ref[...] = total
        total = jnp.zeros((rows, LANES), F32)
        for k in range(K):
            total = total + taps_ref[1, k : k + 1, cols] * first_ref[
                pl.ds(MARGIN - k * dil_ref[1], rows), :
            ]
        drv_ref[half] = total
        decay = [lanes_of(dec_ref, p, cols) for p in range(2)]
        gamma = [jnp.sqrt(1.0 - d * d) for d in decay]
        state = [jnp.zeros((SEGS, LANES), F32) for _ in range(2)]
        kept = jnp.ones((SEGS, LANES), F32)
        for i in range(steps):
            r = rb_ref[pl.ds(i, SEGS, stride=steps), :]
            u = drv_ref[half, pl.ds(i, SEGS, stride=steps), :]
            kept = kept * r
            for p in range(2):
                state[p] = (decay[p] * r) * state[p] + gamma[p] * u
        for p in range(2):
            seg = kept * power(decay[p], steps)
            segh_ref[half, p] = state[p]
            segp_ref[half, p] = seg
            end = row_of(state[p], 0)
            prod = row_of(seg, 0)
            for s in range(1, SEGS):
                end = row_of(seg, s) * end + row_of(state[p], s)
                prod = prod * row_of(seg, s)
            ends[p][half] = end
            prods[p][half] = prod
    fill_copies(pay_ref, ends[0] + ends[1] + prods[0] + prods[1])


def forward_final(
    me_ref, got_ref, drv_ref, segh_ref, segp_ref, dec_ref, ret_ref, ro_ref, skip_ref, cot_ref,
    mixed_ref, w0_ref, w1_ref, w2_ref, w3_ref,
    rb_ref, mix_ref,
):
    rows, width = mixed_ref.shape
    steps = rows // SEGS
    me = me_ref[0]
    count = got_ref.shape[0] // 8
    rb_ref[...] = spread_rows(ret_ref[...])
    entering = jnp.zeros((4, LANES), F32)
    for i in range(count - 1):
        longer = got_ref[8 * i + 4 : 8 * i + 8, :] * entering + got_ref[8 * i : 8 * i + 4, :]
        entering = jnp.where(i < me, longer, entering)
    for half, cols in halves(width):
        decay = [lanes_of(dec_ref, p, cols) for p in range(2)]
        gamma = [jnp.sqrt(1.0 - d * d) for d in decay]
        readout = [lanes_of(ro_ref, p, cols) for p in range(2)]
        skip = skip_ref[0:1, cols]
        state = []
        for p in range(2):
            here = row_of(entering, 2 * p + half)
            starts = [here]
            for s in range(SEGS - 1):
                here = segp_ref[half, p, s : s + 1, :] * here + segh_ref[half, p, s : s + 1, :]
                starts.append(here)
            state.append(jnp.concatenate(starts, axis=0))
        for i in range(steps):
            r = rb_ref[pl.ds(i, SEGS, stride=steps), :]
            u = drv_ref[half, pl.ds(i, SEGS, stride=steps), :]
            for p in range(2):
                state[p] = (decay[p] * r) * state[p] + gamma[p] * u
            mix_ref[half, pl.ds(i, SEGS, stride=steps), :] = (
                readout[0] * state[0] + readout[1] * state[1] + skip * u
            )
        mixed_ref[:, cols] = mix_ref[half].astype(BF16)
    flipped = jnp.transpose(
        jnp.concatenate([mix_ref[half] for half, _ in halves(width)], axis=1)
    ).astype(BF16)
    parts = (w0_ref, w1_ref, w2_ref, w3_ref)
    block = cot_ref.shape[1] // 4
    for d, part in enumerate(parts):
        start = pl.multiple_of(lax.rem(me // ZSIZE + d, 4) * block, block)
        part[...] = jnp.dot(
            flipped, cot_ref[:, pl.ds(start, block)], preferred_element_type=F32
        ).astype(part.dtype)


def backward_local(
    cot_ref, wout_ref, segp_ref, dec_ref, ret_ref, ro_ref, skip_ref,
    gm_ref, pay_ref, segw_ref, halo_ref,
    rb_ref, gd_ref,
):
    rows = cot_ref.shape[0]
    width = wout_ref.shape[0]
    steps = rows // SEGS
    rb_ref[...] = spread_rows(ret_ref[...])
    grad_mixed = lax.dot_general(
        cot_ref[...], wout_ref[...], (((1,), (1,)), ((), ())), preferred_element_type=F32
    )
    ends = [[None] * 2 for _ in range(2)]
    prods = [[None] * 2 for _ in range(2)]
    for half, cols in halves(width):
        gm_ref[half] = grad_mixed[:, cols]
        decay = [lanes_of(dec_ref, p, cols) for p in range(2)]
        gamma = [jnp.sqrt(1.0 - d * d) for d in decay]
        readout = [lanes_of(ro_ref, p, cols) for p in range(2)]
        skip = skip_ref[0:1, cols]
        passed = [jnp.zeros((SEGS, LANES), F32) for _ in range(2)]
        for i in reversed(range(steps)):
            r = rb_ref[pl.ds(i, SEGS, stride=steps), :]
            g = gm_ref[half, pl.ds(i, SEGS, stride=steps), :]
            for p in range(2):
                passed[p] = (decay[p] * r) * (readout[p] * g + passed[p])
        inits = []
        for p in range(2):
            segw_ref[half, p] = passed[p]
            here = jnp.zeros((1, LANES), F32)
            starts = [here]
            prod = segp_ref[half, p, 0:1, :]
            for s in reversed(range(1, SEGS)):
                here = row_of(passed[p], s) + segp_ref[half, p, s : s + 1, :] * here
                prod = prod * segp_ref[half, p, s : s + 1, :]
                starts.append(here)
            ends[p][half] = row_of(passed[p], 0) + segp_ref[half, p, 0:1, :] * here
            prods[p][half] = prod
            inits.append(jnp.concatenate(starts[::-1], axis=0))
        for i in reversed(range(steps)):
            r = rb_ref[pl.ds(i, SEGS, stride=steps), :]
            g = gm_ref[half, pl.ds(i, SEGS, stride=steps), :]
            total = None
            for p in range(2):
                grad_state = readout[p] * g + inits[p]
                inits[p] = (decay[p] * r) * grad_state
                term = gamma[p] * grad_state
                total = term if total is None else total + term
            gd_ref[pl.ds(i, SEGS, stride=steps), :] = skip * g + total
        halo_ref[:, cols] = gd_ref[0:REACH, :].astype(BF16)
    fill_copies(pay_ref, ends[0] + ends[1] + prods[0] + prods[1])


def backward_final(
    me_ref, dil_ref, got_ref, gm_ref, segw_ref, segp_ref, halo_ref, ret_ref, next_ref,
    dec_ref, ro_ref, skip_ref, taps_ref, cot_ref,
    out_ref,
    rb_ref, rn_ref, ahead_ref, far_ref, first_ref,
):
    rows, width = cot_ref.shape
    steps = rows // SEGS
    me = me_ref[0]
    count = got_ref.shape[0] // 8
    rb_ref[...] = spread_rows(ret_ref[...])
    rn_ref[...] = spread_rows(next_ref[...])
    arriving = jnp.zeros((4, LANES), F32)
    beyond = jnp.zeros((4, LANES), F32)
    for i in reversed(range(1, count)):
        prod = got_ref[8 * i + 4 : 8 * i + 8, :]
        own = got_ref[8 * i : 8 * i + 4, :]
        longer = prod * arriving + own
        beyond = jnp.where(i > me + 1, longer, beyond)
        arriving = jnp.where(i > me, longer, arriving)
    kept = jnp.ones((SEGS, LANES), F32)
    for i in range(steps):
        kept = kept * rn_ref[pl.ds(i, SEGS, stride=steps), :]
    for half, cols in halves(width):
        decay = [lanes_of(dec_ref, p, cols) for p in range(2)]
        gamma = [jnp.sqrt(1.0 - d * d) for d in decay]
        readout = [lanes_of(ro_ref, p, cols) for p in range(2)]
        skip = skip_ref[0:1, cols]
        here_at, far_at = [], []
        for p in range(2):
            here = row_of(arriving, 2 * p + half)
            far = row_of(beyond, 2 * p + half)
            seg = kept * power(decay[p], steps)
            starts, fars = [here], [far]
            for s in reversed(range(1, SEGS)):
                here = segw_ref[half, p, s : s + 1, :] + segp_ref[half, p, s : s + 1, :] * here
                far = row_of(seg, s) * far
                starts.append(here)
                fars.append(far)
            here_at.append(jnp.concatenate(starts[::-1], axis=0))
            far_at.append(jnp.concatenate(fars[::-1], axis=0))
        for i in reversed(range(steps)):
            r = rb_ref[pl.ds(i, SEGS, stride=steps), :]
            rn = rn_ref[pl.ds(i, SEGS, stride=steps), :]
            g = gm_ref[half, pl.ds(i, SEGS, stride=steps), :]
            total = far_total = None
            for p in range(2):
                grad_state = readout[p] * g + here_at[p]
                here_at[p] = (decay[p] * r) * grad_state
                term = gamma[p] * grad_state
                total = term if total is None else total + term
                term = gamma[p] * far_at[p]
                far_total = term if far_total is None else far_total + term
                far_at[p] = (decay[p] * rn) * far_at[p]
            ahead_ref[pl.ds(i, SEGS, stride=steps), :] = skip * g + total
            far_ref[pl.ds(i, SEGS, stride=steps), :] = far_total
        ahead_ref[rows : rows + REACH, :] = halo_ref[:, cols].astype(F32) + far_ref[0:REACH, :]
        total = jnp.zeros((rows + MARGIN, LANES), F32)
        for k in range(K):
            total = total + taps_ref[1, k : k + 1, cols] * ahead_ref[
                pl.ds(k * dil_ref[1], rows + MARGIN), :
            ]
        first_ref[...] = total
        total = jnp.zeros((rows, LANES), F32)
        for k in range(K):
            total = total + taps_ref[0, k : k + 1, cols] * first_ref[pl.ds(k * dil_ref[0], rows), :]
        out_ref[:, cols] = (cot_ref[:, cols].astype(F32) + total).astype(BF16)


def near_sum(a_ref, b_ref, c_ref, d_ref, out_ref):
    total = (a_ref[...].astype(F32) + b_ref[...].astype(F32)) + (
        c_ref[...].astype(F32) + d_ref[...].astype(F32)
    )
    rows, width = total.shape
    wide = width // ZSIZE
    for z in range(ZSIZE):
        piece = total[:, z * wide : (z + 1) * wide]
        out_ref[z] = jnp.concatenate([piece[: rows // 2], piece[rows // 2 :]], axis=1).astype(BF16)


def far_sum(in_ref, out_ref):
    total = in_ref[0].astype(F32)
    for z in range(1, ZSIZE):
        total = total + in_ref[z].astype(F32)
    wide = total.shape[1] // 2
    out_ref[...] = jnp.concatenate([total[:, :wide], total[:, wide:]], axis=0)


def call(kernel, outs, smem, scratch, name):
    def run(*args):
        specs = [
            pl.BlockSpec(memory_space=pltpu.SMEM if i < smem else pltpu.VMEM)
            for i in range(len(args))
        ]
        return pl.pallas_call(
            kernel,
            out_shape=tuple(jax.ShapeDtypeStruct(shape, dtype) for shape, dtype in outs),
            in_specs=specs,
            out_specs=tuple(pl.BlockSpec(memory_space=pltpu.VMEM) for _ in outs),
            scratch_shapes=[pltpu.VMEM(shape, F32) for shape in scratch],
            compiler_params=pltpu.CompilerParams(vmem_limit_bytes=40 * 2**20),
            name=name,
        )(*args)

    return run


def shifted(block, distance):
    devices = range(lax.axis_size("seq"))
    return lax.ppermute(
        block, "seq", [(i - distance, i) for i in devices if i - distance in devices]
    )


def along_x(block, distance):
    size = lax.axis_size("seq")
    return lax.ppermute(
        block, "seq", [(i, (i + distance * ZSIZE) % size) for i in range(size)]
    )


def per_device(
    signal, conv_taps, dilations, decays, retention, readout, skip_gain, w_out, cotangent
):
    rows, width = signal.shape
    count = lax.axis_size("seq")
    xsize = count // ZSIZE
    me = lax.axis_index("seq").astype(jnp.int32).reshape(1)
    ret = retention.reshape(1, rows)
    skip = skip_gain.reshape(1, width)
    nh = width // LANES

    halo = shifted(signal[rows - REACH :], 1)
    ret_next = shifted(ret, -1)
    all_cot = lax.all_gather(cotangent, "ch", axis=1, tiled=True)

    seg = ((nh, 2, SEGS, LANES), F32)
    tall = ((nh, rows, LANES), F32)
    pay = ((count * 8, LANES), F32)
    driven, payload, segh, segp = call(
        forward_local, [tall, pay, seg, seg], 1,
        [(rows + REACH, LANES), (rows + MARGIN, LANES), (rows, LANES)], "forward_local",
    )(dilations, halo, signal, conv_taps, decays, ret)
    got = lax.all_to_all(payload, "seq", 0, 0, tiled=True)

    block = all_cot.shape[1] // xsize
    mixed, w0, w1, w2, w3 = call(
        forward_final, [((rows, width), BF16)] + [((width, block), BF16)] * 4, 1,
        [(rows, LANES), (nh, rows, LANES)], "forward_final",
    )(me, got, driven, segh, segp, decays, ret, readout, skip, all_cot)
    w1, w2, w3 = along_x(w1, 1), along_x(w2, 2), along_x(w3, 3)

    partial = jnp.dot(mixed, w_out, preferred_element_type=F32)
    projected = lax.psum_scatter(partial, "ch", scatter_dimension=1, tiled=True)
    output = (signal.astype(F32) + projected).astype(BF16)

    grad_mixed, bpay, segw, bhalo = call(
        backward_local, [tall, pay, seg, ((REACH, width), BF16)], 0,
        [(rows, LANES), (rows, LANES)], "backward_local",
    )(all_cot, w_out, segp, decays, ret, readout, skip)
    later = shifted(bhalo, -1)
    bgot = lax.all_to_all(bpay, "seq", 0, 0, tiled=True)

    groups = [[x * ZSIZE + z for z in range(ZSIZE)] for x in range(xsize)]
    wide = block // ZSIZE
    (near,) = call(near_sum, [((ZSIZE, width // 2, 2 * wide), BF16)], 0, [], "near_sum")(
        w0, w1, w2, w3
    )
    far = lax.all_to_all(near, "seq", 0, 0, axis_index_groups=groups, tiled=True)
    (grad_w_out,) = call(far_sum, [((width, wide), F32)], 0, [], "far_sum")(far)

    (grad_signal,) = call(
        backward_final, [((rows, width), BF16)], 2,
        [(rows, LANES), (rows, LANES), (rows + REACH, LANES), (rows, LANES), (rows + MARGIN, LANES)],
        "backward_final",
    )(
        me, dilations, bgot, grad_mixed, segw, segp, later, ret, ret_next,
        decays, readout, skip, conv_taps, cotangent,
    )
    return (output, grad_signal, grad_w_out)


def solution(mesh):
    return jax.shard_map(
        per_device,
        mesh=mesh,
        in_specs=(
            P("seq", "ch"),
            P(None, None, "ch"),
            P(),
            P(None, "ch"),
            P("seq"),
            P(None, "ch"),
            P("ch"),
            P("ch", None),
            P("seq", "ch"),
        ),
        out_specs=(P("seq", "ch"), P("seq", "ch"), P("ch", "seq")),
        check_vma=False,
    )
```

time: 727 us -> 106 us (0.15)
  waiting for transfers between devices: 253 us -> 26.4 us
  blocking collectives: 190 us -> 0 us
  local copies, waits for them, and re-layouts: 138 us -> 17.8 us
  other arithmetic: 99.4 us -> 1.63 us
  starting transfers between devices: 8.53 us -> 35.8 us
  between operations: 24.3 us -> 14.2 us
  Pallas kernels: 0 us -> 7.66 us
    reduce_scatter x2 -> x1, waiting for transfers between devices: 241 us -> 0.01 us  [per_device(): projected = lax.psum_scatter(partial, 'ch', scatter_dimension=1, tiled=True)]
    all_gather x4 -> x0, blocking collectives: 190 us -> none  [carried_in(): pieces = jax.tree.map(lambda part: lax.all_gather(part, axis), value)]
    slice x117 -> x1, local copies, waits for them, and re-layouts: 114 us -> 0.81 us  [per_device(): halo = shifted(signal[rows - REACH:], 1)]
    add x66 -> x0, other arithmetic: 40.8 us -> none  [the longest x27 26.1 us: combine(): return (earlier[0] * later[0], later[0] * earlier[1] + later[1])]
    select_n x62 -> x0, other arithmetic: 39.5 us -> none  [lap(): jnp.where(position < mine, new, old)]
    all_to_all x0 -> x3, starting transfers between devices: none -> 18.6 us  [the longest x1 9.01 us: per_device(): got = lax.all_to_all(payload, 'seq', 0, 0, tiled=True)]
    all_to_all x0 -> x3, waiting for transfers between devices: none -> 17.4 us  [the longest x1 9.14 us: per_device(): got = lax.all_to_all(payload, 'seq', 0, 0, tiled=True)]
    pad x56 -> x0, local copies, waits for them, and re-layouts: 16.7 us -> none  [the longest x28 13 us: per_device(): lax.associative_scan(combine, (factor, factor * emitted), axis=0, reverse...]
  transfers between devices with their start and end apart: 5 -> 11, of which waited for: 3 -> 4; matrix products, arithmetic and copies ran while one was open for 2% -> 1% of each run, Pallas kernels for 0% -> 6%
where the time goes in v1:
time: 106 us; the launch traced here: 105 us
  starting transfers between devices  35.8 us (34%)
  waiting for transfers between devices  26.4 us (25%)
  local copies, waits for them, and re-layouts  17.8 us (17%)
  between operations  14.2 us (13%)
  Pallas kernels  7.66 us (7%)
  matrix products  1.78 us (2%)
  other arithmetic  1.63 us (2%)
    unnamed x59, local copies, waits for them, and re-layouts  17 us
    ppermute x3, starting transfers between devices, shifted(): lax.ppermute(block, 'seq', [(i - distance, i) for i in devices if i - dis...  13 us
    all_to_all x1, waiting for transfers between devices, per_device(): got = lax.all_to_all(payload, 'seq', 0, 0, tiled=True)  9.14 us
    all_to_all x1, starting transfers between devices, per_device(): got = lax.all_to_all(payload, 'seq', 0, 0, tiled=True)  9.01 us
    ppermute x3, waiting for transfers between devices, shifted(): lax.ppermute(block, 'seq', [(i - distance, i) for i in devices if i - dis...  8.27 us
    all_to_all x1, waiting for transfers between devices, per_device(): bgot = lax.all_to_all(bpay, 'seq', 0, 0, tiled=True)  8.26 us
    pallas_call x6, Pallas kernels, run(): pl.pallas_call(kernel, out_shape=tuple((jax.ShapeDtypeStruct(shape, dtype...  7.66 us
    all_to_all x1, starting transfers between devices, per_device(): bgot = lax.all_to_all(bpay, 'seq', 0, 0, tiled=True)  6.14 us
  transfers between devices with their start and end apart: 11, of which 4 were waited for; matrix products, arithmetic and copies ran while one was open for 1% of the time, Pallas kernels for 6%

profile of v1, /device:TPU:2, one launch (start us, length us, event | category | flops | bytes accessed | tf_op | source)
XLA Modules:
  0.0 105.2 jit_solution(12172139341949242813)
XLA Ops:
  7.9 0.8 slice.3
  8.7 3.8 %collective-permute-start = (bf16[96,256]{1,0:T(8,128)(2,1)S(1)}, bf16[96,256]{1,0:T(8,128)(2,1)S(1)}, u32[]{:S(2)}, u32[]{:S(2)}) collective-permute-start(bf16[96,256]{1,0:T(8,128)(2,1)S(1)} %slice.3), channel_id=1, source_target_pairs={{0,8},{8,16},{16,24},{24,32},{32,40},{40,48},{48,56},{56,64},{64,7... | collective-permute-start | bytes 147464 | tf_op jit(solution)/shard_map/ppermute | solution.py:308
  12.5 6.0 %collective-permute-done.halo_ref = bf16[96,256]{1,0:T(8,128)(2,1)S(1)} collective-permute-done((bf16[96,256]{1,0:T(8,128)(2,1)S(1)}, bf16[96,256]{1,0:T(8,128)(2,1)S(1)}, u32[]{:S(2)}, u32[]{:S(2)}) %collective-permute-start) | collective-permute-done | bytes 49184 | tf_op jit(solution)/shard_map/ppermute | solution.py:308
  18.5 0.9 copy-done.3
  20.1 0.7 copy-done.11
  22.1 1.7 %forward_local.1 = (f32[2,256,128]{2,1,0:T(8,128)S(1)}, f32[256,128]{1,0:T(8,128)}, f32[2,2,8,128]{3,2,1,0:T(8,128)S(1)}, f32[2,2,8,128]{3,2,1,0:T(8,128)S(1)}) custom-call(s32[2]{0:T(128)S(1)} %copy-done.25, bf16[96,256]{1,0:T(8,128)(2,1)S(1)} %collective-permute-done.halo_ref, bf16[256,256]{1,0:T(8,128)(2,1)S(1)} %copy-done.3, ...), custom_call_target="tpu_custom_call" | custom-call | tf_op jit(solution)/shard_map/forward_local/pallas_call | solution.py:293
  23.8 9.0 %all-to-all-start = ((f32[32,8,128]{2,1,0:T(8,128)}), f32[32,8,128]{2,1,0:T(8,128)S(1)}, u32[]{:S(2)}, u32[]{:S(2)}) async-start(f32[32,8,128]{2,1,0:T(8,128)} %bitcast.2), calls=%async_computation | async-start | bytes 262144 | tf_op jit(solution)/shard_map/all_to_all | solution.py:342
  32.9 9.1 %all-to-all-done = f32[32,8,128]{2,1,0:T(8,128)S(1)} async-done(((f32[32,8,128]{2,1,0:T(8,128)}), f32[32,8,128]{2,1,0:T(8,128)S(1)}, u32[]{:S(2)}, u32[]{:S(2)}) %all-to-all-start) | async-done | bytes 131104 | tf_op jit(solution)/shard_map/all_to_all | solution.py:342
  42.1 1.2 %copy-done.1 = bf16[256,2048]{1,0:T(8,128)(2,1)S(1)} copy-done((bf16[256,2048]{1,0:T(8,128)(2,1)S(1)}, bf16[256,2048]{1,0:T(8,128)(2,1)}, u32[]{:S(2)}) %copy-start.1) | copy-done | bytes 1048600
  46.0 1.7 %forward_final.1 = (bf16[256,256]{1,0:T(8,128)(2,1)S(1)}, bf16[256,512]{1,0:T(8,128)(2,1)S(1)}, bf16[256,512]{1,0:T(8,128)(2,1)}, bf16[256,512]{1,0:T(8,128)(2,1)}, bf16[256,512]{1,0:T(8,128)(2,1)}) custom-call(s32[1]{0:T(128)} %bitcast.me_ref, f32[256,128]{1,0:T(8,128)S(1)} %bitcast.10, f32[2,256,128]{2,1,0:T(8,128)S(1)} %get-tuple-element.17.drv_ref, ...), custom_call_target="tpu_custom_call" | custom-call | tf_op jit(solution)/shard_map/forward_final/pallas_call | solution.py:293
  47.7 1.8 %fusion = f32[256,2048]{1,0:T(8,128)} fusion(bf16[256,256]{1,0:T(8,128)(2,1)S(1)} %get-tuple-element.20, bf16[256,2048]{1,0:T(8,128)(2,1)S(1)} %copy-done), kind=kOutput, calls=%fused_computation.1 | convolution fusion | flops 268435456 | bytes 3276800 | tf_op jit(solution)/shard_map/dot_general | solution.py:351
  49.6 0.8 collective-permute-start.3
  50.3 2.8 %collective-permute-start.4 = (bf16[256,512]{1,0:T(8,128)(2,1)}, bf16[256,512]{1,0:T(8,128)(2,1)S(1)}, u32[]{:S(2)}, u32[]{:S(2)}) collective-permute-start(bf16[256,512]{1,0:T(8,128)(2,1)} %get-tuple-element.27), channel_id=1, source_target_pairs={{0,128},{8,136},{16,144},{24,152},{32,160},{40,168},{48,176},{56,1... | collective-permute-start | bytes 786440 | tf_op jit(solution)/shard_map/ppermute | solution.py:315
  56.4 1.0 backward_local.1
  59.2 6.1 %all-to-all-start.1 = ((f32[32,8,128]{2,1,0:T(8,128)}), f32[32,8,128]{2,1,0:T(8,128)S(1)}, u32[]{:S(2)}, u32[]{:S(2)}) async-start(f32[32,8,128]{2,1,0:T(8,128)} %bitcast.11), calls=%async_computation.2 | async-start | bytes 262144 | tf_op jit(solution)/shard_map/all_to_all | solution.py:360
  65.4 0.9 near_sum.1
  66.3 8.3 %all-to-all-done.1 = f32[32,8,128]{2,1,0:T(8,128)S(1)} async-done(((f32[32,8,128]{2,1,0:T(8,128)}), f32[32,8,128]{2,1,0:T(8,128)S(1)}, u32[]{:S(2)}, u32[]{:S(2)}) %all-to-all-start.1) | async-done | bytes 131104 | tf_op jit(solution)/shard_map/all_to_all | solution.py:360
  74.6 3.4 %all-to-all-start.2 = ((bf16[8,128,128]{2,1,0:T(8,128)(2,1)}), bf16[8,128,128]{2,1,0:T(8,128)(2,1)S(1)}, u32[]{:S(2)}, u32[]{:S(2)}) async-start(bf16[8,128,128]{2,1,0:T(8,128)(2,1)} %near_sum.1), calls=%async_computation.3 | async-start | bytes 524288 | tf_op jit(solution)/shard_map/all_to_all | solution.py:367
  78.0 5.9 %collective-permute-start.1 = (bf16[96,256]{1,0:T(8,128)(2,1)S(1)}, bf16[96,256]{1,0:T(8,128)(2,1)S(1)}, u32[]{:S(2)}, u32[]{:S(2)}) collective-permute-start(bf16[96,256]{1,0:T(8,128)(2,1)S(1)} %copy-done.28), channel_id=1, source_target_pairs={{8,0},{16,8},{24,16},{32,24},{40,32},{48,40},{56,48},{64,56},{72,6... | collective-permute-start | bytes 147464 | tf_op jit(solution)/shard_map/ppermute | solution.py:308
  83.9 3.4 %collective-permute-start.2 = (f32[1,256]{1,0:T(1,128)}, f32[1,256]{1,0:T(1,128)S(1)}, u32[]{:S(2)}, u32[]{:S(2)}) collective-permute-start(f32[1,256]{1,0:T(1,128)} %bitcast.12), channel_id=1, source_target_pairs={{8,0},{16,8},{24,16},{32,24},{40,32},{48,40},{56,48},{64,56},{72,6... | collective-permute-start | bytes 3080 | tf_op jit(solution)/shard_map/ppermute | solution.py:308
  87.3 2.3 %collective-permute-done.2.next_ref = f32[1,256]{1,0:T(1,128)S(1)} collective-permute-done((f32[1,256]{1,0:T(1,128)}, f32[1,256]{1,0:T(1,128)S(1)}, u32[]{:S(2)}, u32[]{:S(2)}) %collective-permute-start.2) | collective-permute-done | bytes 1056 | tf_op jit(solution)/shard_map/ppermute | solution.py:308
  93.7 2.2 %backward_final.1 = bf16[256,256]{1,0:T(8,128)(2,1)} custom-call(s32[1]{0:T(128)} %bitcast.me_ref, s32[2]{0:T(128)S(1)} %copy-done.26, f32[256,128]{1,0:T(8,128)S(1)} %bitcast.9, f32[2,256,128]{2,1,0:T(8,128)S(1)} %get-tuple-element.22.gm_ref, f32[2,2,8,128]{3,2,1,0:T(8,128)S(1)} %copy-done.21, f32[2,2,8,128]{3,2,1,0:T(8,128)S(1)} %get-tuple-element.19.segp_ref, ...), custom_call_target="tpu_custom_call" | custom-call | tf_op jit(solution)/shard_map/backward_final/pallas_call | solution.py:293
  96.0 0.7 copy.12
  96.7 1.6 %add_convert_fusion = bf16[256,256]{1,0:T(8,128)(2,1)} fusion(f32[256,256]{1,0:T(8,128)} %reduce-scatter.2.cloned.1.call-done, bf16[256,256]{1,0:T(8,128)(2,1)S(1)} %copy-done.4), kind=kLoop, calls=%fused_computation | loop fusion | flops 196608 | bytes 524288 | tf_op jit(solution)/shard_map/convert_element_type | solution.py:353
  (68 shorter events, 14.9 us)
Async XLA Ops:
  7.2 40.6 %copy-start = (bf16[256,2048]{1,0:T(8,128)(2,1)S(1)}, bf16[256,2048]{1,0:T(8,128)(2,1)}, u32[]{:S(2)}) copy-start(bf16[256,2048]{1,0:T(8,128)(2,1)} %wout_ref.1) | copy-start | bytes 3145732
  7.2 34.9 %all-gather.2.cloned.1.call-start = ((), (), s32[]{:S(2)}) async-start(), calls=%async_computation.4 | async-start | bytes 1179648 | tf_op jit(solution)/shard_map/all_gather | solution.py:333
  8.7 9.8 %collective-permute-start = (bf16[96,256]{1,0:T(8,128)(2,1)S(1)}, bf16[96,256]{1,0:T(8,128)(2,1)S(1)}, u32[]{:S(2)}, u32[]{:S(2)}) collective-permute-start(bf16[96,256]{1,0:T(8,128)(2,1)S(1)} %slice.3), channel_id=1, source_target_pairs={{0,8},{8,16},{16,24},{24,32},{32,40},{40,48},{48,56},{56,64},{64,7... | collective-permute-start | bytes 147464 | tf_op jit(solution)/shard_map/ppermute | solution.py:308
  18.5 0.9 copy-start.3
  19.4 0.7 copy-start.7
  20.1 0.7 copy-start.11
  23.8 18.2 %all-to-all-start = ((f32[32,8,128]{2,1,0:T(8,128)}), f32[32,8,128]{2,1,0:T(8,128)S(1)}, u32[]{:S(2)}, u32[]{:S(2)}) async-start(f32[32,8,128]{2,1,0:T(8,128)} %bitcast.2), calls=%async_computation | async-start | bytes 262144 | tf_op jit(solution)/shard_map/all_to_all | solution.py:342
  32.9 63.9 %reduce-scatter.2.cloned.1.call-start = ((), (), s32[]{:S(2)}) async-start(), calls=%async_computation.5 | async-start | bytes 2359296 | tf_op jit(solution)/shard_map/reduce_scatter | solution.py:352
  42.1 1.2 %copy-start.1 = (bf16[256,2048]{1,0:T(8,128)(2,1)S(1)}, bf16[256,2048]{1,0:T(8,128)(2,1)}, u32[]{:S(2)}) copy-start(bf16[256,2048]{1,0:T(8,128)(2,1)} %all-gather.2.cloned.1.call-done.cot_ref) | copy-start | bytes 3145732
  47.7 5.9 %copy-start.2 = (bf16[256,2048]{1,0:T(8,128)(2,1)S(1)}, bf16[256,2048]{1,0:T(8,128)(2,1)}, u32[]{:S(2)}) copy-start(bf16[256,2048]{1,0:T(8,128)(2,1)} %all-gather.2.cloned.1.call-done.cot_ref) | copy-start | bytes 3145732
  49.6 15.8 %collective-permute-start.3 = (bf16[256,512]{1,0:T(8,128)(2,1)}, bf16[256,512]{1,0:T(8,128)(2,1)S(1)}, u32[]{:S(2)}, u32[]{:S(2)}) collective-permute-start(bf16[256,512]{1,0:T(8,128)(2,1)} %get-tuple-element.26), channel_id=1, source_target_pairs={{0,64},{8,72},{16,80},{24,88},{32,96},{40,104},{48,112},{56,120},{... | collective-permute-start | bytes 786440 | tf_op jit(solution)/shard_map/ppermute | solution.py:315
  50.3 15.0 %collective-permute-start.4 = (bf16[256,512]{1,0:T(8,128)(2,1)}, bf16[256,512]{1,0:T(8,128)(2,1)S(1)}, u32[]{:S(2)}, u32[]{:S(2)}) collective-permute-start(bf16[256,512]{1,0:T(8,128)(2,1)} %get-tuple-element.27), channel_id=1, source_target_pairs={{0,128},{8,136},{16,144},{24,152},{32,160},{40,168},{48,176},{56,1... | collective-permute-start | bytes 786440 | tf_op jit(solution)/shard_map/ppermute | solution.py:315
  53.1 36.5 %copy-start.5 = (bf16[256,256]{1,0:T(8,128)(2,1)S(1)}, bf16[256,256]{1,0:T(8,128)(2,1)}, u32[]{:S(2)}) copy-start(bf16[256,256]{1,0:T(8,128)(2,1)} %cot_ref.1) | copy-start | bytes 393220
  53.1 12.3 %collective-permute-start.5 = (bf16[256,512]{1,0:T(8,128)(2,1)}, bf16[256,512]{1,0:T(8,128)(2,1)S(1)}, u32[]{:S(2)}, u32[]{:S(2)}) collective-permute-start(bf16[256,512]{1,0:T(8,128)(2,1)} %get-tuple-element.28), channel_id=1, source_target_pairs={{0,192},{8,200},{16,208},{24,216},{32,224},{40,232},{48,240},{56,2... | collective-permute-start | bytes 786440 | tf_op jit(solution)/shard_map/ppermute | solution.py:315
  53.7 0.7 copy-start.9
  59.2 37.5 %copy-start.4 = (bf16[256,256]{1,0:T(8,128)(2,1)S(1)}, bf16[256,256]{1,0:T(8,128)(2,1)}, u32[]{:S(2)}) copy-start(bf16[256,256]{1,0:T(8,128)(2,1)} %sig_ref.1) | copy-start | bytes 393220
  59.2 18.8 %copy-start.28 = (bf16[96,256]{1,0:T(8,128)(2,1)S(1)}, bf16[96,256]{1,0:T(8,128)(2,1)}, u32[]{:S(2)}) copy-start(bf16[96,256]{1,0:T(8,128)(2,1)} %copy-done.27) | copy-start | bytes 147460
  59.2 30.4 %copy-start.21 = (f32[2,2,8,128]{3,2,1,0:T(8,128)S(1)}, f32[2,2,8,128]{3,2,1,0:T(8,128)}, u32[]{:S(2)}) copy-start(f32[2,2,8,128]{3,2,1,0:T(8,128)} %copy-done.20) | copy-start | bytes 49156
  59.2 15.4 %all-to-all-start.1 = ((f32[32,8,128]{2,1,0:T(8,128)}), f32[32,8,128]{2,1,0:T(8,128)S(1)}, u32[]{:S(2)}, u32[]{:S(2)}) async-start(f32[32,8,128]{2,1,0:T(8,128)} %bitcast.11), calls=%async_computation.2 | async-start | bytes 262144 | tf_op jit(solution)/shard_map/all_to_all | solution.py:360
  74.6 21.3 %all-to-all-start.2 = ((bf16[8,128,128]{2,1,0:T(8,128)(2,1)}), bf16[8,128,128]{2,1,0:T(8,128)(2,1)S(1)}, u32[]{:S(2)}, u32[]{:S(2)}) async-start(bf16[8,128,128]{2,1,0:T(8,128)(2,1)} %near_sum.1), calls=%async_computation.3 | async-start | bytes 524288 | tf_op jit(solution)/shard_map/all_to_all | solution.py:367
  78.0 11.5 %collective-permute-start.1 = (bf16[96,256]{1,0:T(8,128)(2,1)S(1)}, bf16[96,256]{1,0:T(8,128)(2,1)S(1)}, u32[]{:S(2)}, u32[]{:S(2)}) collective-permute-start(bf16[96,256]{1,0:T(8,128)(2,1)S(1)} %copy-done.28), channel_id=1, source_target_pairs={{8,0},{16,8},{24,16},{32,24},{40,32},{48,40},{56,48},{64,56},{72,6... | collective-permute-start | bytes 147464 | tf_op jit(solution)/shard_map/ppermute | solution.py:308
  83.9 5.7 %collective-permute-start.2 = (f32[1,256]{1,0:T(1,128)}, f32[1,256]{1,0:T(1,128)S(1)}, u32[]{:S(2)}, u32[]{:S(2)}) collective-permute-start(f32[1,256]{1,0:T(1,128)} %bitcast.12), channel_id=1, source_target_pairs={{8,0},{16,8},{24,16},{32,24},{40,32},{48,40},{56,48},{64,56},{72,6... | collective-permute-start | bytes 3080 | tf_op jit(solution)/shard_map/ppermute | solution.py:308
  89.6 0.7 copy-start.10
  90.3 0.7 copy-start.12
  (16 other events, 10.7 us)
Sparse Core Ops, SparseCore 0:
  9.8 28.8 all-gather.1
  49.7 34.0 reduce-scatter.1

commit v2 on v1

v2 whole, which is shorter than its diff:
```python
import jax
import jax.numpy as jnp
from jax import lax
from jax.experimental import pallas as pl
from jax.experimental.pallas import tpu as pltpu
from jax.sharding import PartitionSpec as P

K = 4
DMAX = 16
MARGIN = (K - 1) * DMAX
REACH = 2 * MARGIN
SEGS = 8
LANES = 128
XSIZE, YSIZE, ZSIZE = 4, 4, 8
F32 = jnp.float32
BF16 = jnp.bfloat16
DECAY, GAMMA, READ, SKIP, DIL, PARAMS = 8, 10, 12, 14, 15, 16


def spread_rows(row):
    return jnp.transpose(jnp.broadcast_to(row, (LANES, row.shape[1])))


def row_of(value, index):
    return value[index : index + 1]


def power(value, exponent):
    while exponent > 1:
        value = value * value
        exponent //= 2
    return value


def halves(count):
    return [(half, slice(half * LANES, (half + 1) * LANES)) for half in range(count // LANES)]


def params(par_ref, first, cols):
    return [par_ref[first + p : first + p + 1, cols] for p in range(2)]


def dilation(par_ref, which):
    return jnp.max(par_ref[DIL : DIL + 1, which * LANES : (which + 1) * LANES]).astype(jnp.int32)


def x_index():
    return lax.axis_index("seq") // ZSIZE


def y_index():
    return lax.axis_index("ch") // 2


def core_index():
    return lax.rem(lax.axis_index("ch"), 2)


def gather_inputs(
    sig_hbm, taps_hbm, dec_hbm, ret_hbm, ro_hbm, skip_hbm, cot_hbm, dil_hbm,
    par_ref, rb_ref, drv_ref, fhead_ref, shead_ref, cot_ref,
    sig_ref, taps_ref, dec_ref, ret_ref, ro_ref, skip_ref, dil_ref, ext_ref, first_ref, sems,
):
    pairs = (
        (sig_hbm, sig_ref), (taps_hbm, taps_ref), (dec_hbm, dec_ref),
        (ret_hbm, ret_ref), (ro_hbm, ro_ref), (skip_hbm, skip_ref), (cot_hbm, cot_ref),
        (dil_hbm, dil_ref),
    )
    copies = [pltpu.make_async_copy(a, b, sems.at[i]) for i, (a, b) in enumerate(pairs)]
    for copy in copies:
        copy.start()
    for copy in copies:
        copy.wait()
    rows, width = sig_ref.shape
    par_ref[0:K, :] = taps_ref[0]
    par_ref[K : 2 * K, :] = taps_ref[1]
    decays = dec_ref[...]
    par_ref[DECAY : DECAY + 2, :] = decays
    par_ref[GAMMA : GAMMA + 2, :] = jnp.sqrt(1.0 - decays * decays)
    par_ref[READ : READ + 2, :] = ro_ref[...]
    par_ref[SKIP : SKIP + 1, :] = skip_ref[...]
    for which in range(2):
        par_ref[DIL : DIL + 1, which * LANES : (which + 1) * LANES] = jnp.full(
            (1, LANES), dil_ref[which], jnp.int32
        ).astype(F32)
    rb_ref[...] = spread_rows(ret_ref[...])
    for half, cols in halves(width):
        ext_ref[...] = sig_ref[:, cols].astype(F32)
        shead_ref[half] = ext_ref[0:MARGIN, :]
        total = jnp.zeros((rows - MARGIN, LANES), F32)
        for k in range(K):
            total = total + taps_ref[0, k : k + 1, cols] * ext_ref[
                pl.ds(MARGIN - k * dil_ref[0], rows - MARGIN), :
            ]
        first_ref[...] = total
        fhead_ref[half] = first_ref[0:MARGIN, :]
        total = jnp.zeros((rows - REACH, LANES), F32)
        for k in range(K):
            total = total + taps_ref[1, k : k + 1, cols] * first_ref[
                pl.ds(MARGIN - k * dil_ref[1], rows - REACH), :
            ]
        drv_ref[half, 0:REACH, :] = jnp.zeros((REACH, LANES), F32)
        drv_ref[half, REACH:rows, :] = total


def forward_local(
    halo_ref, par_ref, rb_ref, drvin_ref, fhead_ref, shead_ref,
    drv_ref, ends_ref, segh_ref, segp_ref,
    ext_ref, first_ref,
):
    rows = rb_ref.shape[0]
    width = par_ref.shape[1]
    steps = rows // SEGS
    first_gap, second_gap = dilation(par_ref, 0), dilation(par_ref, 1)
    for half, cols in halves(width):
        ext_ref[0:REACH, :] = halo_ref[:, cols].astype(F32)
        ext_ref[REACH : REACH + MARGIN, :] = shead_ref[half]
        total = jnp.zeros((REACH, LANES), F32)
        for k in range(K):
            total = total + par_ref[k : k + 1, cols] * ext_ref[
                pl.ds(MARGIN - k * first_gap, REACH), :
            ]
        first_ref[0:REACH, :] = total
        first_ref[REACH : REACH + MARGIN, :] = fhead_ref[half]
        total = jnp.zeros((REACH, LANES), F32)
        for k in range(K):
            total = total + par_ref[K + k : K + k + 1, cols] * first_ref[
                pl.ds(MARGIN - k * second_gap, REACH), :
            ]
        drv_ref[half, 0:REACH, :] = total
        decay, gamma = params(par_ref, DECAY, cols), params(par_ref, GAMMA, cols)
        state = [jnp.zeros((SEGS, LANES), F32) for _ in range(2)]
        kept = jnp.ones((SEGS, LANES), F32)
        for i in range(steps):
            r = rb_ref[pl.ds(i, SEGS, stride=steps), :]
            u = drv_ref[half, pl.ds(i, SEGS, stride=steps), :]
            kept = kept * r
            for p in range(2):
                state[p] = (decay[p] * r) * state[p] + gamma[p] * u
        for p in range(2):
            seg = kept * power(decay[p], steps)
            segh_ref[half, p] = state[p]
            segp_ref[half, p] = seg
            end = row_of(state[p], 0)
            for s in range(1, SEGS):
                end = row_of(seg, s) * end + row_of(state[p], s)
            ends_ref[2 * p + half : 2 * p + half + 1, :] = end


def decays_of(par_ref, rows):
    parts = [par_ref[DECAY + p : DECAY + p + 1, cols] for p in range(2) for _, cols in halves(2 * LANES)]
    return power(jnp.concatenate(parts, axis=0), rows)


def forward_final(
    got_ref, drv_ref, segh_ref, segp_ref, par_ref, rb_ref, near_ref, far_ref,
    mixed_ref, w0_ref, w1_ref, w2_ref, w3_ref, rprod_ref,
    mix_ref,
):
    rows, width = mixed_ref.shape
    steps = rows // SEGS
    me = lax.axis_index("seq")
    count = got_ref.shape[0]
    kept = jnp.concatenate(
        [got_ref[i, 2, 0:1, :] * got_ref[i, 2, 1:2, :] for i in range(count)], axis=0
    )
    gap = LANES // 2
    while gap:
        kept = kept * pltpu.roll(kept, gap, axis=1)
        gap //= 2
    rprod_ref[...] = kept
    whole = decays_of(par_ref, rows)
    entering = jnp.zeros((4, LANES), F32)
    for i in range(count - 1):
        longer = (whole * rprod_ref[i : i + 1, :]) * entering + got_ref[i, 0]
        entering = jnp.where(i < me, longer, entering)
    for half, cols in halves(width):
        decay, gamma = params(par_ref, DECAY, cols), params(par_ref, GAMMA, cols)
        readout = params(par_ref, READ, cols)
        skip = par_ref[SKIP : SKIP + 1, cols]
        state = []
        for p in range(2):
            here = row_of(entering, 2 * p + half)
            starts = [here]
            for s in range(SEGS - 1):
                here = segp_ref[half, p, s : s + 1, :] * here + segh_ref[half, p, s : s + 1, :]
                starts.append(here)
            state.append(jnp.concatenate(starts, axis=0))
        for i in range(steps):
            r = rb_ref[pl.ds(i, SEGS, stride=steps), :]
            u = drv_ref[half, pl.ds(i, SEGS, stride=steps), :]
            for p in range(2):
                state[p] = (decay[p] * r) * state[p] + gamma[p] * u
            mix_ref[half, pl.ds(i, SEGS, stride=steps), :] = (
                readout[0] * state[0] + readout[1] * state[1] + skip * u
            )
        mixed_ref[:, cols] = mix_ref[half].astype(BF16)
    flipped = jnp.transpose(
        jnp.concatenate([mix_ref[half] for half, _ in halves(width)], axis=1)
    ).astype(BF16)
    core = core_index()
    mine = pl.ds(pl.multiple_of(core * width, width), width)
    other = pl.ds(pl.multiple_of((1 - core) * width, width), width)
    for d, part in ((1, w1_ref), (2, w2_ref), (3, w3_ref), (0, w0_ref)):
        at = lax.rem(y_index() - x_index() - d + 2 * YSIZE, YSIZE)
        for cols, source in ((mine, near_ref), (other, far_ref)):
            part[:, cols] = jnp.dot(
                flipped, source[at], preferred_element_type=F32
            ).astype(part.dtype)


def project(mixed_ref, wout_ref, send_ref):
    width = mixed_ref.shape[1]
    for d in range(YSIZE):
        block = 2 * lax.rem(y_index() + d, YSIZE) + 1 - core_index()
        start = pl.multiple_of(block * width, width)
        send_ref[d] = jnp.dot(
            mixed_ref[...], wout_ref[:, pl.ds(start, width)], preferred_element_type=F32
        ).astype(BF16)


def pair_sum(mixed_ref, wout_ref, got_ref, own_ref, a_ref, b_ref, c_ref):
    width = mixed_ref.shape[1]
    for d, out_ref in ((1, a_ref), (2, b_ref), (3, c_ref), (0, own_ref)):
        block = 2 * lax.rem(y_index() + d, YSIZE) + core_index()
        start = pl.multiple_of(block * width, width)
        total = got_ref[d].astype(F32) + jnp.dot(
            mixed_ref[...], wout_ref[:, pl.ds(start, width)], preferred_element_type=F32
        )
        out_ref[...] = total.astype(out_ref.dtype)


def finish_output(sig_ref, own_ref, a_ref, b_ref, c_ref, out_ref):
    total = (own_ref[...] + a_ref[...].astype(F32)) + (
        b_ref[...].astype(F32) + c_ref[...].astype(F32)
    )
    out_ref[...] = (sig_ref[...].astype(F32) + total).astype(BF16)


def pack(own_ref, a_ref, b_ref, c_ref, out_ref):
    for d, source in enumerate((own_ref, a_ref, b_ref, c_ref)):
        out_ref[d] = source[...]


def backward_local(
    near_ref, far_ref, wout_ref, segp_ref, par_ref, rb_ref, ends_ref, ret_ref,
    gm_ref, pay_ref, segw_ref, halo_ref,
    gd_ref, tile_ref,
):
    rows = rb_ref.shape[0]
    width = par_ref.shape[1]
    steps = rows // SEGS
    core = core_index()
    grad_mixed = jnp.zeros((rows, width), F32)
    for source, which in ((near_ref, core), (far_ref, 1 - core)):
        for d in range(YSIZE):
            first = 2 * lax.rem(y_index() - d + YSIZE, YSIZE)
            start = pl.multiple_of((first + which) * width, width)
            grad_mixed = grad_mixed + lax.dot_general(
                source[d], wout_ref[:, pl.ds(start, width)], (((1,), (1,)), ((), ())),
                preferred_element_type=F32,
            )
    for half, cols in halves(width):
        gm_ref[half] = grad_mixed[:, cols]
        decay, gamma = params(par_ref, DECAY, cols), params(par_ref, GAMMA, cols)
        readout = params(par_ref, READ, cols)
        skip = par_ref[SKIP : SKIP + 1, cols]
        passed = [jnp.zeros((SEGS, LANES), F32) for _ in range(2)]
        for i in reversed(range(steps)):
            r = rb_ref[pl.ds(i, SEGS, stride=steps), :]
            g = gm_ref[half, pl.ds(i, SEGS, stride=steps), :]
            for p in range(2):
                passed[p] = (decay[p] * r) * (readout[p] * g + passed[p])
        inits = []
        for p in range(2):
            segw_ref[half, p] = passed[p]
            here = jnp.zeros((1, LANES), F32)
            starts = [here]
            for s in reversed(range(1, SEGS)):
                here = row_of(passed[p], s) + segp_ref[half, p, s : s + 1, :] * here
                starts.append(here)
            tile_ref[1, 2 * p + half : 2 * p + half + 1, :] = (
                row_of(passed[p], 0) + segp_ref[half, p, 0:1, :] * here
            )
            inits.append(jnp.concatenate(starts[::-1], axis=0))
        for i in reversed(range(steps)):
            r = rb_ref[pl.ds(i, SEGS, stride=steps), :]
            g = gm_ref[half, pl.ds(i, SEGS, stride=steps), :]
            total = None
            for p in range(2):
                grad_state = readout[p] * g + inits[p]
                inits[p] = (decay[p] * r) * grad_state
                term = gamma[p] * grad_state
                total = term if total is None else total + term
            gd_ref[pl.ds(i, SEGS, stride=steps), :] = skip * g + total
        halo_ref[:, cols] = gd_ref[0:REACH, :].astype(BF16)
    tile_ref[0] = ends_ref[...]
    for half, cols in halves(width):
        tile_ref[2, half : half + 1, :] = ret_ref[0:1, cols]
    tile_ref[2, 2:4, :] = jnp.ones((2, LANES), F32)
    tile = tile_ref[...]
    for copy in range(pay_ref.shape[0]):
        pay_ref[copy] = tile


def backward_final(
    got_ref, rprod_ref, gm_ref, segw_ref, segp_ref, halo_ref, rb_ref, par_ref, cot_ref,
    out_ref,
    rn_ref, ahead_ref, far_ref, first_ref,
):
    rows, width = cot_ref.shape
    steps = rows // SEGS
    me = lax.axis_index("seq")
    count = rprod_ref.shape[0]
    first_gap, second_gap = dilation(par_ref, 0), dilation(par_ref, 1)
    after = jnp.minimum(me + 1, count - 1)
    for part in range(rows // LANES):
        rn_ref[part * LANES : (part + 1) * LANES, :] = spread_rows(
            got_ref[after, 2, part : part + 1, :]
        )
    whole = decays_of(par_ref, rows)
    arriving = jnp.zeros((4, LANES), F32)
    beyond = jnp.zeros((4, LANES), F32)
    for i in reversed(range(1, count)):
        longer = (whole * rprod_ref[i : i + 1, :]) * arriving + got_ref[i, 1]
        beyond = jnp.where(i > me + 1, longer, beyond)
        arriving = jnp.where(i > me, longer, arriving)
    kept = jnp.ones((SEGS, LANES), F32)
    for i in range(steps):
        kept = kept * rn_ref[pl.ds(i, SEGS, stride=steps), :]
    for half, cols in halves(width):
        decay, gamma = params(par_ref, DECAY, cols), params(par_ref, GAMMA, cols)
        readout = params(par_ref, READ, cols)
        skip = par_ref[SKIP : SKIP + 1, cols]
        here_at, far_at = [], []
        for p in range(2):
            here = row_of(arriving, 2 * p + half)
            far = row_of(beyond, 2 * p + half)
            seg = kept * power(decay[p], steps)
            starts, fars = [here], [far]
            for s in reversed(range(1, SEGS)):
                here = segw_ref[half, p, s : s + 1, :] + segp_ref[half, p, s : s + 1, :] * here
                far = row_of(seg, s) * far
                starts.append(here)
                fars.append(far)
            here_at.append(jnp.concatenate(starts[::-1], axis=0))
            far_at.append(jnp.concatenate(fars[::-1], axis=0))
        for i in reversed(range(steps)):
            r = rb_ref[pl.ds(i, SEGS, stride=steps), :]
            rn = rn_ref[pl.ds(i, SEGS, stride=steps), :]
            g = gm_ref[half, pl.ds(i, SEGS, stride=steps), :]
            total = far_total = None
            for p in range(2):
                grad_state = readout[p] * g + here_at[p]
                here_at[p] = (decay[p] * r) * grad_state
                term = gamma[p] * grad_state
                total = term if total is None else total + term
                term = gamma[p] * far_at[p]
                far_total = term if far_total is None else far_total + term
                far_at[p] = (decay[p] * rn) * far_at[p]
            ahead_ref[pl.ds(i, SEGS, stride=steps), :] = skip * g + total
            far_ref[pl.ds(i, SEGS, stride=steps), :] = far_total
        ahead_ref[rows : rows + REACH, :] = halo_ref[:, cols].astype(F32) + far_ref[0:REACH, :]
        total = jnp.zeros((rows + MARGIN, LANES), F32)
        for k in range(K):
            total = total + par_ref[K + k : K + k + 1, cols] * ahead_ref[
                pl.ds(k * second_gap, rows + MARGIN), :
            ]
        first_ref[...] = total
        total = jnp.zeros((rows, LANES), F32)
        for k in range(K):
            total = total + par_ref[k : k + 1, cols] * first_ref[pl.ds(k * first_gap, rows), :]
        out_ref[:, cols] = (cot_ref[:, cols].astype(F32) + total).astype(BF16)


def near_sum(a_ref, b_ref, c_ref, d_ref, out_ref):
    total = (a_ref[...].astype(F32) + b_ref[...].astype(F32)) + (
        c_ref[...].astype(F32) + d_ref[...].astype(F32)
    )
    rows, width = total.shape
    wide = width // ZSIZE
    for z in range(ZSIZE):
        piece = total[:, z * wide : (z + 1) * wide]
        out_ref[z] = jnp.concatenate([piece[: rows // 2], piece[rows // 2 :]], axis=1).astype(BF16)


def far_sum(in_ref, out_ref):
    total = in_ref[0].astype(F32)
    for z in range(1, ZSIZE):
        total = total + in_ref[z].astype(F32)
    flipped = jnp.transpose(total)
    wide = flipped.shape[0] // 2
    out_ref[...] = jnp.concatenate([flipped[:wide], flipped[wide:]], axis=1)


def vmem(shape, dtype=F32):
    return pltpu.VMEM(shape, dtype)


def call(kernel, outs, scratch=(), smem=(), hbm=(), aliases=None, cost=1):
    def run(*args, after=()):
        used = len(args)
        args = tuple(
            pltpu.with_memory_space_constraint(arg, pltpu.HBM) if i in hbm else arg
            for i, arg in enumerate(args)
        ) + tuple(after)

        def body(*refs):
            kernel(*refs[:used], *refs[len(args) :])

        def space(i):
            return pltpu.SMEM if i in smem else pltpu.HBM if i in hbm else pl.ANY if i >= used else pltpu.VMEM

        return pl.pallas_call(
            body,
            out_shape=tuple(jax.ShapeDtypeStruct(shape, dtype) for shape, dtype in outs),
            in_specs=[pl.BlockSpec(memory_space=space(i)) for i in range(len(args))],
            out_specs=tuple(pl.BlockSpec(memory_space=pltpu.VMEM) for _ in outs),
            scratch_shapes=list(scratch),
            input_output_aliases=aliases or {},
            compiler_params=pltpu.CompilerParams(vmem_limit_bytes=16 * 2**20),
            cost_estimate=pl.CostEstimate(
                flops=0, bytes_accessed=cost * 3_500_000, transcendentals=0
            ),
            name=kernel.__name__,
        )(*args)

    return run


def shifted(block, distance):
    devices = range(lax.axis_size("seq"))
    return lax.ppermute(
        block, "seq", [(i - distance, i) for i in devices if i - distance in devices]
    )


def along_x(block, distance):
    size = XSIZE * ZSIZE
    return lax.ppermute(
        block, "seq", [(i, (i + distance * ZSIZE) % size) for i in range(size)]
    )


def along_y(block, distance):
    size = 2 * YSIZE
    return lax.ppermute(block, "ch", [(i, (i + 2 * distance) % size) for i in range(size)])


def other_core(block):
    return lax.ppermute(block, "ch", [(i, i ^ 1) for i in range(2 * YSIZE)])


def per_device(
    signal, conv_taps, dilations, decays, retention, readout, skip_gain, w_out, cotangent
):
    rows, width = signal.shape
    count = XSIZE * ZSIZE
    nh = width // LANES
    ret = retention.reshape(1, rows)
    skip = skip_gain.reshape(1, width)
    square = (rows, width)
    tall = ((nh, rows, LANES), F32)
    head = ((nh, MARGIN, LANES), F32)
    seg = ((nh, 2, SEGS, LANES), F32)

    halo = shifted(signal[rows - REACH :], 1)
    from_y = [along_y(cotangent, d) for d in range(1, YSIZE)]
    par, rb, driven, fhead, shead, own_cot = call(
        gather_inputs,
        [((PARAMS, width), F32), ((rows, LANES), F32), tall, head, head, (square, BF16)],
        [
            vmem(square, BF16), vmem((2, K, width)), vmem((2, width)), vmem((1, rows)),
            vmem((2, width)), vmem((1, width)), pltpu.SMEM((2,), jnp.int32), vmem((rows, LANES)),
            vmem((rows - MARGIN, LANES)), pltpu.SemaphoreType.DMA((8,)),
        ],
        hbm=range(8), cost=20,
    )(signal, conv_taps, decays, ret, readout, skip, cotangent, dilations)

    driven, ends, segh, segp = call(
        forward_local, [tall, ((4, LANES), F32), seg, seg],
        [vmem((REACH + MARGIN, LANES)), vmem((REACH + MARGIN, LANES))],
        aliases={3: 0}, cost=20,
    )(halo, par, rb, driven, fhead, shead)

    (near,) = call(pack, [((YSIZE,) + square, BF16)])(own_cot, *from_y, after=(segh,))
    far = other_core(near)
    grad_mixed, payload, segw, bhalo = call(
        backward_local, [tall, ((count, 3, 4, LANES), F32), seg, ((REACH, width), BF16)],
        [vmem((rows, LANES)), vmem((3, 4, LANES))], cost=20,
    )(near, far, w_out, segp, par, rb, ends, ret)
    got = lax.all_to_all(payload, "seq", 0, 0, tiled=True)
    later = shifted(bhalo, -1)

    mixed, w0, w1, w2, w3, rprod = call(
        forward_final,
        [(square, BF16)] + [((width, 2 * width), BF16)] * 4 + [((count, LANES), F32)],
        [vmem((nh, rows, LANES))], cost=20,
    )(got, driven, segh, segp, par, rb, near, far, after=(later,))
    w1, w2, w3 = along_x(w1, 1), along_x(w2, 2), along_x(w3, 3)

    (send,) = call(project, [((YSIZE,) + square, BF16)], cost=20)(mixed, w_out)
    pair = other_core(send)
    (grad_signal,) = call(
        backward_final, [(square, BF16)],
        [
            vmem((rows, LANES)), vmem((rows + REACH, LANES)), vmem((rows, LANES)),
            vmem((rows + MARGIN, LANES)),
        ],
        cost=1,
    )(got, rprod, grad_mixed, segw, segp, later, rb, par, own_cot, after=(send,))


    groups = [[x * ZSIZE + z for z in range(ZSIZE)] for x in range(XSIZE)]
    wide = 2 * width // ZSIZE
    (sums,) = call(near_sum, [((ZSIZE, width // 2, 2 * wide), BF16)], cost=20)(
        w0, w1, w2, w3,
        after=(pltpu.with_memory_space_constraint(grad_signal, pltpu.HBM),),
    )
    own, p1, p2, p3 = call(pair_sum, [(square, F32)] + [(square, BF16)] * 3)(
        mixed, w_out, pair, after=(sums,)
    )
    p1, p2, p3 = along_y(p1, 1), along_y(p2, 2), along_y(p3, 3)
    (output,) = call(finish_output, [(square, BF16)])(signal, own, p1, p2, p3)

    sums = lax.all_to_all(sums, "seq", 0, 0, axis_index_groups=groups, tiled=True)
    (grad_w_out,) = call(far_sum, [((wide, width), F32)])(sums)

    return (output, grad_signal, grad_w_out.T)


def solution(mesh):
    return jax.shard_map(
        per_device,
        mesh=mesh,
        in_specs=(
            P("seq", "ch"),
            P(None, None, "ch"),
            P(),
            P(None, "ch"),
            P("seq"),
            P(None, "ch"),
            P("ch"),
            P("ch", None),
            P("seq", "ch"),
        ),
        out_specs=(P("seq", "ch"), P("seq", "ch"), P("ch", "seq")),
        check_vma=False,
    )
```

time: 106 us -> 76 us (0.72)
  local copies, waits for them, and re-layouts: 17.8 us -> 2.4 us
  between operations: 14.2 us -> 0.76 us
  Pallas kernels: 7.66 us -> 9.68 us
  matrix products: 1.78 us -> 0 us
  other arithmetic: 1.63 us -> 0 us
    unnamed x59 -> x10, local copies, waits for them, and re-layouts: 17 us -> 1.59 us
    ppermute x0 -> x8, starting transfers between devices: none -> 9.74 us  [the longest x6 9.55 us: along_y(): lax.ppermute(block, 'ch', [(i, (i + 2 * distance) % size) for i in range(...]
    ppermute x0 -> x8, waiting for transfers between devices: none -> 7.46 us  [the longest x6 5.56 us: along_y(): lax.ppermute(block, 'ch', [(i, (i + 2 * distance) % size) for i in range(...]
    all_to_all x2 -> x1, waiting for transfers between devices: 8.27 us -> 1.16 us  [per_device(): lax.all_to_all(sums, 'seq', 0, 0, axis_index_groups=groups, tiled=True)]
    ppermute x3, waiting for transfers between devices: 0.01 us -> 7.09 us  [along_x(): lax.ppermute(block, 'seq', [(i, (i + distance * ZSIZE) % size) for i in r...]
    all_to_all x1, waiting for transfers between devices: 9.14 us -> 3.23 us  [per_device(): got = lax.all_to_all(payload, 'seq', 0, 0, tiled=True)]
    ppermute x3 -> x2, starting transfers between devices: 13 us -> 8.39 us  [shifted(): lax.ppermute(block, 'seq', [(i - distance, i) for i in devices if i - dis...]
    all_to_all x2 -> x1, starting transfers between devices: 9.55 us -> 5.15 us  [per_device(): lax.all_to_all(sums, 'seq', 0, 0, axis_index_groups=groups, tiled=True)]
  transfers between devices with their start and end apart: 11 -> 15, of which waited for: 4 -> 10; matrix products, arithmetic and copies ran while one was open for 1% -> 1% of each run, Pallas kernels for 6% -> 8%
where the time goes in v2:
time: 76 us; the launch traced here: 75.5 us
  starting transfers between devices  36.4 us (48%)
  waiting for transfers between devices  26.3 us (35%)
  Pallas kernels  9.68 us (13%)
  local copies, waits for them, and re-layouts  2.4 us (3%)
  between operations  0.76 us (1%)
    pallas_call x11, Pallas kernels, run(): pl.pallas_call(body, out_shape=tuple((jax.ShapeDtypeStruct(shape, dtype)...  9.68 us
    ppermute x6, starting transfers between devices, along_y(): lax.ppermute(block, 'ch', [(i, (i + 2 * distance) % size) for i in range(...  9.55 us
    all_to_all x1, starting transfers between devices, per_device(): got = lax.all_to_all(payload, 'seq', 0, 0, tiled=True)  9.01 us
    ppermute x2, starting transfers between devices, shifted(): lax.ppermute(block, 'seq', [(i - distance, i) for i in devices if i - dis...  8.39 us
    ppermute x2, waiting for transfers between devices, shifted(): lax.ppermute(block, 'seq', [(i - distance, i) for i in devices if i - dis...  7.34 us
    ppermute x3, waiting for transfers between devices, along_x(): lax.ppermute(block, 'seq', [(i, (i + distance * ZSIZE) % size) for i in r...  7.09 us
    ppermute x6, waiting for transfers between devices, along_y(): lax.ppermute(block, 'ch', [(i, (i + 2 * distance) % size) for i in range(...  5.56 us
    all_to_all x1, starting transfers between devices, per_device(): lax.all_to_all(sums, 'seq', 0, 0, axis_index_groups=groups, tiled=True)  5.15 us
  transfers between devices with their start and end apart: 15, of which 10 were waited for; matrix products, arithmetic and copies ran while one was open for 1% of the time, Pallas kernels for 8%

profile of v2, /device:TPU:2, one launch (start us, length us, event | category | flops | bytes accessed | tf_op | source)
XLA Modules:
  0.0 75.5 jit_solution(5326296460937883153)
XLA Ops:
  0.6 1.7 %collective-permute-start = (bf16[256,256]{1,0:T(8,128)(2,1)}, bf16[256,256]{1,0:T(8,128)(2,1)S(1)}, u32[]{:S(2)}, u32[]{:S(2)}) collective-permute-start(bf16[256,256]{1,0:T(8,128)(2,1)} %refs_6_.1), channel_id=1, source_target_pairs={{0,2},{1,3},{2,4},{3,5},{4,6},{5,7},{6,0},{7,1},{8,10},{9,11},{10,... | collective-permute-start | bytes 393224 | tf_op jit(solution)/shard_map/ppermute | solution.py:447
  2.3 1.7 %collective-permute-start.2 = (bf16[256,256]{1,0:T(8,128)(2,1)}, bf16[256,256]{1,0:T(8,128)(2,1)S(1)}, u32[]{:S(2)}, u32[]{:S(2)}) collective-permute-start(bf16[256,256]{1,0:T(8,128)(2,1)} %refs_6_.1), channel_id=1, source_target_pairs={{0,6},{1,7},{2,0},{3,1},{4,2},{5,3},{6,4},{7,5},{8,14},{9,15},{10,... | collective-permute-start | bytes 393224 | tf_op jit(solution)/shard_map/ppermute | solution.py:447
  4.0 2.0 %collective-permute-start.1 = (bf16[256,256]{1,0:T(8,128)(2,1)}, bf16[256,256]{1,0:T(8,128)(2,1)S(1)}, u32[]{:S(2)}, u32[]{:S(2)}) collective-permute-start(bf16[256,256]{1,0:T(8,128)(2,1)} %refs_6_.1), channel_id=1, source_target_pairs={{0,4},{1,5},{2,6},{3,7},{4,0},{5,1},{6,2},{7,3},{8,12},{9,13},{10,... | collective-permute-start | bytes 393224 | tf_op jit(solution)/shard_map/ppermute | solution.py:447
  6.7 3.8 %collective-permute-start.3 = (bf16[96,256]{1,0:T(8,128)(2,1)S(1)}, bf16[96,256]{1,0:T(8,128)(2,1)S(1)}, u32[]{:S(2)}, u32[]{:S(2)}) collective-permute-start(bf16[96,256]{1,0:T(8,128)(2,1)S(1)} %slice.3), channel_id=1, source_target_pairs={{0,8},{8,16},{16,24},{24,32},{32,40},{40,48},{48,56},{56,64},{64,7... | collective-permute-start | bytes 147464 | tf_op jit(solution)/shard_map/ppermute | solution.py:433
  10.6 1.3 %gather_inputs.1 = (f32[16,256]{1,0:T(8,128)S(1)}, f32[256,128]{1,0:T(8,128)S(1)}, f32[2,256,128]{2,1,0:T(8,128)S(1)}, f32[2,48,128]{2,1,0:T(8,128)S(1)}, f32[2,...) custom-call(bf16[256,256]{1,0:T(8,128)(2,1)} %refs_0_.3, f32[2,4,256]{2,1,0:T(4,128)} %refs_1_.3, f32[2,256]{1,0:T(2,128)} %refs_2_.2, ...), custom_call_target="tpu_custom_call" | custom-call | bytes 70000000 | tf_op jit(solution)/shard_map/gather_inputs/pallas_call | solution.py:414
  11.8 4.7 %collective-permute-done.3.refs_0_ = bf16[96,256]{1,0:T(8,128)(2,1)S(1)} collective-permute-done((bf16[96,256]{1,0:T(8,128)(2,1)S(1)}, bf16[96,256]{1,0:T(8,128)(2,1)S(1)}, u32[]{:S(2)}, u32[]{:S(2)}) %collective-permute-start.3) | collective-permute-done | bytes 49184 | tf_op jit(solution)/shard_map/ppermute | solution.py:433
  17.2 1.9 %collective-permute-done.4.refs_1_.refs_7_ = bf16[4,256,256]{2,1,0:T(8,128)(2,1)S(1)} collective-permute-done((bf16[4,256,256]{2,1,0:T(8,128)(2,1)S(1)}, bf16[4,256,256]{2,1,0:T(8,128)(2,1)S(1)}, u32[]{:S(2)}, u32[]{:S(2)}) %collective-permute-start.4) | collective-permute-done | bytes 524320 | tf_op jit(solution)/shard_map/ppermute | solution.py:451
  19.7 1.7 %backward_local.1 = (f32[2,256,128]{2,1,0:T(8,128)S(1)}, f32[32,3,4,128]{3,2,1,0:T(4,128)}, f32[2,2,8,128]{3,2,1,0:T(8,128)S(1)}, bf16[96,256]{1,0:T(8,128)(2,1)S(1)}) custom-call(bf16[4,256,256]{2,1,0:T(8,128)(2,1)S(1)} %pack.1.refs_0_.refs_6_, bf16[4,256,256]{2,1,0:T(8,128)(2,1)S(1)} %collective-permute-done.4.refs_1_.refs_7_, ...), custom_call_target="tpu_custom_call" | custom-call | bytes 70000000 | tf_op jit(solution)/shard_map/backward_local/pallas_call | solution.py:414
  22.1 9.0 %all-to-all-start = ((f32[32,3,4,128]{3,2,1,0:T(4,128)}), f32[32,3,4,128]{3,2,1,0:T(4,128)S(1)}, u32[]{:S(2)}, u32[]{:S(2)}) async-start(f32[32,3,4,128]{3,2,1,0:T(4,128)} %get-tuple-element.36), calls=%async_computation | async-start | bytes 393216 | tf_op jit(solution)/shard_map/all_to_all | solution.py:492
  31.1 4.6 %collective-permute-start.5 = (bf16[96,256]{1,0:T(8,128)(2,1)S(1)}, bf16[96,256]{1,0:T(8,128)(2,1)S(1)}, u32[]{:S(2)}, u32[]{:S(2)}) collective-permute-start(bf16[96,256]{1,0:T(8,128)(2,1)S(1)} %get-tuple-element.38), channel_id=1, source_target_pairs={{8,0},{16,8},{24,16},{32,24},{40,32},{48,40},{56,48},{64,56},{72,6... | collective-permute-start | bytes 147464 | tf_op jit(solution)/shard_map/ppermute | solution.py:433
  35.7 2.7 %collective-permute-done.5.refs_8_.refs_5_ = bf16[96,256]{1,0:T(8,128)(2,1)S(1)} collective-permute-done((bf16[96,256]{1,0:T(8,128)(2,1)S(1)}, bf16[96,256]{1,0:T(8,128)(2,1)S(1)}, u32[]{:S(2)}, u32[]{:S(2)}) %collective-permute-start.5) | collective-permute-done | bytes 49184 | tf_op jit(solution)/shard_map/ppermute | solution.py:433
  38.4 3.2 %all-to-all-done.refs_0_ = f32[32,3,4,128]{3,2,1,0:T(4,128)S(1)} async-done(((f32[32,3,4,128]{3,2,1,0:T(4,128)}), f32[32,3,4,128]{3,2,1,0:T(4,128)S(1)}, u32[]{:S(2)}, u32[]{:S(2)}) %all-to-all-start) | async-done | bytes 196640 | tf_op jit(solution)/shard_map/all_to_all | solution.py:492
  41.6 1.5 %forward_final.1 = (bf16[256,256]{1,0:T(8,128)(2,1)S(1)}, bf16[256,512]{1,0:T(8,128)(2,1)S(1)}, bf16[256,512]{1,0:T(8,128)(2,1)S(1)}, bf16[256,512]{1,0:T(8,128)...) custom-call(f32[32,3,4,128]{3,2,1,0:T(4,128)S(1)} %all-to-all-done.refs_0_, ...), custom_call_target="tpu_custom_call" | custom-call | bytes 70000000 | tf_op jit(solution)/shard_map/forward_final/pallas_call | solution.py:414
  43.1 1.0 %collective-permute-start.7 = (bf16[256,512]{1,0:T(8,128)(2,1)S(1)}, bf16[256,512]{1,0:T(8,128)(2,1)S(1)}, u32[]{:S(2)}, u32[]{:S(2)}) collective-permute-start(bf16[256,512]{1,0:T(8,128)(2,1)S(1)} %get-tuple-element.41), channel_id=1, source_target_pairs={{0,64},{8,72},{16,80},{24,88},{32,96},{40,104},{48,112},{56,120},{... | collective-permute-start | bytes 786440 | tf_op jit(solution)/shard_map/ppermute | solution.py:440
  44.1 2.5 %collective-permute-start.8 = (bf16[256,512]{1,0:T(8,128)(2,1)S(1)}, bf16[256,512]{1,0:T(8,128)(2,1)S(1)}, u32[]{:S(2)}, u32[]{:S(2)}) collective-permute-start(bf16[256,512]{1,0:T(8,128)(2,1)S(1)} %get-tuple-element.42), channel_id=1, source_target_pairs={{0,128},{8,136},{16,144},{24,152},{32,160},{40,168},{48,176},{56,1... | collective-permute-start | bytes 786440 | tf_op jit(solution)/shard_map/ppermute | solution.py:440
  47.9 1.7 %backward_final.1.refs_4_ = bf16[256,256]{1,0:T(8,128)(2,1)} custom-call(f32[32,3,4,128]{3,2,1,0:T(4,128)S(1)} %all-to-all-done.refs_0_, f32[32,128]{1,0:T(8,128)S(1)} %get-tuple-element.44.refs_1_, f32[2,256,128]{2,1,0:T(8,128)S(1)} %get-tuple-element.45.refs_2_, f32[2,2,8,128]{3,2,1,0:T(8,128)S(1)} %copy-done.3, ...), custom_call_target="tpu_custom_call" | custom-call | bytes 3500000 | tf_op jit(solution)/shard_map/backward_final/pallas_call | solution.py:414
  49.6 2.2 %collective-permute-done.7.refs_1_ = bf16[256,512]{1,0:T(8,128)(2,1)S(1)} collective-permute-done((bf16[256,512]{1,0:T(8,128)(2,1)S(1)}, bf16[256,512]{1,0:T(8,128)(2,1)S(1)}, u32[]{:S(2)}, u32[]{:S(2)}) %collective-permute-start.7) | collective-permute-done | bytes 262176 | tf_op jit(solution)/shard_map/ppermute | solution.py:440
  51.7 2.3 %collective-permute-done.8.refs_2_ = bf16[256,512]{1,0:T(8,128)(2,1)S(1)} collective-permute-done((bf16[256,512]{1,0:T(8,128)(2,1)S(1)}, bf16[256,512]{1,0:T(8,128)(2,1)S(1)}, u32[]{:S(2)}, u32[]{:S(2)}) %collective-permute-start.8) | collective-permute-done | bytes 262176 | tf_op jit(solution)/shard_map/ppermute | solution.py:440
  54.0 2.7 %collective-permute-done.9.refs_3_ = bf16[256,512]{1,0:T(8,128)(2,1)S(1)} collective-permute-done((bf16[256,512]{1,0:T(8,128)(2,1)S(1)}, bf16[256,512]{1,0:T(8,128)(2,1)S(1)}, u32[]{:S(2)}, u32[]{:S(2)}) %collective-permute-start.9) | collective-permute-done | bytes 262176 | tf_op jit(solution)/shard_map/ppermute | solution.py:440
  57.6 5.1 %all-to-all-start.1 = ((bf16[8,128,128]{2,1,0:T(8,128)(2,1)}), bf16[8,128,128]{2,1,0:T(8,128)(2,1)S(1)}, u32[]{:S(2)}, u32[]{:S(2)}) async-start(bf16[8,128,128]{2,1,0:T(8,128)(2,1)} %near_sum.1.refs_3_), calls=%async_computation.1 | async-start | bytes 524288 | tf_op jit(solution)/shard_map/all_to_all | solution.py:526
  63.8 1.8 %collective-permute-start.11 = (bf16[256,256]{1,0:T(8,128)(2,1)S(1)}, bf16[256,256]{1,0:T(8,128)(2,1)S(1)}, u32[]{:S(2)}, u32[]{:S(2)}) collective-permute-start(bf16[256,256]{1,0:T(8,128)(2,1)S(1)} %get-tuple-element.49), channel_id=1, source_target_pairs={{0,4},{1,5},{2,6},{3,7},{4,0},{5,1},{6,2},{7,3},{8,12},{9,13},{10,... | collective-permute-start | bytes 393224 | tf_op jit(solution)/shard_map/ppermute | solution.py:447
  65.7 1.7 %collective-permute-start.12 = (bf16[256,256]{1,0:T(8,128)(2,1)S(1)}, bf16[256,256]{1,0:T(8,128)(2,1)S(1)}, u32[]{:S(2)}, u32[]{:S(2)}) collective-permute-start(bf16[256,256]{1,0:T(8,128)(2,1)S(1)} %get-tuple-element.50), channel_id=1, source_target_pairs={{0,6},{1,7},{2,0},{3,1},{4,2},{5,3},{6,4},{7,5},{8,14},{9,15},{10,... | collective-permute-start | bytes 393224 | tf_op jit(solution)/shard_map/ppermute | solution.py:447
  67.3 5.0 %collective-permute-done.10.refs_2_ = bf16[256,256]{1,0:T(8,128)(2,1)S(1)} collective-permute-done((bf16[256,256]{1,0:T(8,128)(2,1)S(1)}, bf16[256,256]{1,0:T(8,128)(2,1)S(1)}, u32[]{:S(2)}, u32[]{:S(2)}) %collective-permute-start.10) | collective-permute-done | bytes 131104 | tf_op jit(solution)/shard_map/ppermute | solution.py:447
  73.6 1.2 %all-to-all-done.1.refs_0_ = bf16[8,128,128]{2,1,0:T(8,128)(2,1)S(1)} async-done(((bf16[8,128,128]{2,1,0:T(8,128)(2,1)}), bf16[8,128,128]{2,1,0:T(8,128)(2,1)S(1)}, u32[]{:S(2)}, u32[]{:S(2)}) %all-to-all-start.1) | async-done | bytes 262176 | tf_op jit(solution)/shard_map/all_to_all | solution.py:526
  (28 shorter events, 8.0 us)
Async XLA Ops:
  0.6 18.4 %copy-start = (bf16[256,2048]{1,0:T(8,128)(2,1)S(1)}, bf16[256,2048]{1,0:T(8,128)(2,1)}, u32[]{:S(2)}) copy-start(bf16[256,2048]{1,0:T(8,128)(2,1)} %refs_1_.5) | copy-start | bytes 3145732
  0.6 16.3 %collective-permute-start = (bf16[256,256]{1,0:T(8,128)(2,1)}, bf16[256,256]{1,0:T(8,128)(2,1)S(1)}, u32[]{:S(2)}, u32[]{:S(2)}) collective-permute-start(bf16[256,256]{1,0:T(8,128)(2,1)} %refs_6_.1), channel_id=1, source_target_pairs={{0,2},{1,3},{2,4},{3,5},{4,6},{5,7},{6,0},{7,1},{8,10},{9,11},{10,... | collective-permute-start | bytes 393224 | tf_op jit(solution)/shard_map/ppermute | solution.py:447
  2.3 14.7 %collective-permute-start.2 = (bf16[256,256]{1,0:T(8,128)(2,1)}, bf16[256,256]{1,0:T(8,128)(2,1)S(1)}, u32[]{:S(2)}, u32[]{:S(2)}) collective-permute-start(bf16[256,256]{1,0:T(8,128)(2,1)} %refs_6_.1), channel_id=1, source_target_pairs={{0,6},{1,7},{2,0},{3,1},{4,2},{5,3},{6,4},{7,5},{8,14},{9,15},{10,... | collective-permute-start | bytes 393224 | tf_op jit(solution)/shard_map/ppermute | solution.py:447
  4.0 13.0 %collective-permute-start.1 = (bf16[256,256]{1,0:T(8,128)(2,1)}, bf16[256,256]{1,0:T(8,128)(2,1)S(1)}, u32[]{:S(2)}, u32[]{:S(2)}) collective-permute-start(bf16[256,256]{1,0:T(8,128)(2,1)} %refs_6_.1), channel_id=1, source_target_pairs={{0,4},{1,5},{2,6},{3,7},{4,0},{5,1},{6,2},{7,3},{8,12},{9,13},{10,... | collective-permute-start | bytes 393224 | tf_op jit(solution)/shard_map/ppermute | solution.py:447
  6.7 9.8 %collective-permute-start.3 = (bf16[96,256]{1,0:T(8,128)(2,1)S(1)}, bf16[96,256]{1,0:T(8,128)(2,1)S(1)}, u32[]{:S(2)}, u32[]{:S(2)}) collective-permute-start(bf16[96,256]{1,0:T(8,128)(2,1)S(1)} %slice.3), channel_id=1, source_target_pairs={{0,8},{8,16},{16,24},{24,32},{32,40},{40,48},{48,56},{56,64},{64,7... | collective-permute-start | bytes 147464 | tf_op jit(solution)/shard_map/ppermute | solution.py:433
  17.1 2.0 %collective-permute-start.4 = (bf16[4,256,256]{2,1,0:T(8,128)(2,1)S(1)}, bf16[4,256,256]{2,1,0:T(8,128)(2,1)S(1)}, u32[]{:S(2)}, u32[]{:S(2)}) collective-permute-start(bf16[4,256,256]{2,1,0:T(8,128)(2,1)S(1)} %pack.1.refs_0_.refs_6_), channel_id=1, source_target_pairs={{0,1},{1,0},{2,3},{3,2},{4,5},{5,4},{6,7},{7,6},{8,9},{9,8},{10,11... | collective-permute-start | bytes 1572872 | tf_op jit(solution)/shard_map/ppermute | solution.py:451
  19.1 0.7 copy-start.4
  21.5 0.6 copy-start.2
  22.1 19.5 %all-to-all-start = ((f32[32,3,4,128]{3,2,1,0:T(4,128)}), f32[32,3,4,128]{3,2,1,0:T(4,128)S(1)}, u32[]{:S(2)}, u32[]{:S(2)}) async-start(f32[32,3,4,128]{3,2,1,0:T(4,128)} %get-tuple-element.36), calls=%async_computation | async-start | bytes 393216 | tf_op jit(solution)/shard_map/all_to_all | solution.py:492
  31.1 7.2 %collective-permute-start.5 = (bf16[96,256]{1,0:T(8,128)(2,1)S(1)}, bf16[96,256]{1,0:T(8,128)(2,1)S(1)}, u32[]{:S(2)}, u32[]{:S(2)}) collective-permute-start(bf16[96,256]{1,0:T(8,128)(2,1)S(1)} %get-tuple-element.38), channel_id=1, source_target_pairs={{8,0},{16,8},{24,16},{32,24},{40,32},{48,40},{56,48},{64,56},{72,6... | collective-permute-start | bytes 147464 | tf_op jit(solution)/shard_map/ppermute | solution.py:433
  43.1 8.7 %collective-permute-start.7 = (bf16[256,512]{1,0:T(8,128)(2,1)S(1)}, bf16[256,512]{1,0:T(8,128)(2,1)S(1)}, u32[]{:S(2)}, u32[]{:S(2)}) collective-permute-start(bf16[256,512]{1,0:T(8,128)(2,1)S(1)} %get-tuple-element.41), channel_id=1, source_target_pairs={{0,64},{8,72},{16,80},{24,88},{32,96},{40,104},{48,112},{56,120},{... | collective-permute-start | bytes 786440 | tf_op jit(solution)/shard_map/ppermute | solution.py:440
  44.1 9.9 %collective-permute-start.8 = (bf16[256,512]{1,0:T(8,128)(2,1)S(1)}, bf16[256,512]{1,0:T(8,128)(2,1)S(1)}, u32[]{:S(2)}, u32[]{:S(2)}) collective-permute-start(bf16[256,512]{1,0:T(8,128)(2,1)S(1)} %get-tuple-element.42), channel_id=1, source_target_pairs={{0,128},{8,136},{16,144},{24,152},{32,160},{40,168},{48,176},{56,1... | collective-permute-start | bytes 786440 | tf_op jit(solution)/shard_map/ppermute | solution.py:440
  46.6 10.1 %collective-permute-start.9 = (bf16[256,512]{1,0:T(8,128)(2,1)S(1)}, bf16[256,512]{1,0:T(8,128)(2,1)S(1)}, u32[]{:S(2)}, u32[]{:S(2)}) collective-permute-start(bf16[256,512]{1,0:T(8,128)(2,1)S(1)} %get-tuple-element.43), channel_id=1, source_target_pairs={{0,192},{8,200},{16,208},{24,216},{32,224},{40,232},{48,240},{56,2... | collective-permute-start | bytes 786440 | tf_op jit(solution)/shard_map/ppermute | solution.py:440
  47.2 0.7 copy-start.3
  47.5 15.3 %collective-permute-start.6 = (bf16[4,256,256]{2,1,0:T(8,128)(2,1)S(1)}, bf16[4,256,256]{2,1,0:T(8,128)(2,1)S(1)}, u32[]{:S(2)}, u32[]{:S(2)}) collective-permute-start(bf16[4,256,256]{2,1,0:T(8,128)(2,1)S(1)} %project.1.refs_9_), channel_id=1, source_target_pairs={{0,1},{1,0},{2,3},{3,2},{4,5},{5,4},{6,7},{7,6},{8,9},{9,8},{10,11... | collective-permute-start | bytes 1572872 | tf_op jit(solution)/shard_map/ppermute | solution.py:451
  57.6 17.2 %all-to-all-start.1 = ((bf16[8,128,128]{2,1,0:T(8,128)(2,1)}), bf16[8,128,128]{2,1,0:T(8,128)(2,1)S(1)}, u32[]{:S(2)}, u32[]{:S(2)}) async-start(bf16[8,128,128]{2,1,0:T(8,128)(2,1)} %near_sum.1.refs_3_), calls=%async_computation.1 | async-start | bytes 524288 | tf_op jit(solution)/shard_map/all_to_all | solution.py:526
  62.7 10.2 %copy-start.1 = (bf16[256,256]{1,0:T(8,128)(2,1)S(1)}, bf16[256,256]{1,0:T(8,128)(2,1)}, u32[]{:S(2)}) copy-start(bf16[256,256]{1,0:T(8,128)(2,1)} %refs_0_.3) | copy-start | bytes 393220
  63.1 9.2 %collective-permute-start.10 = (bf16[256,256]{1,0:T(8,128)(2,1)S(1)}, bf16[256,256]{1,0:T(8,128)(2,1)S(1)}, u32[]{:S(2)}, u32[]{:S(2)}) collective-permute-start(bf16[256,256]{1,0:T(8,128)(2,1)S(1)} %get-tuple-element.48), channel_id=1, source_target_pairs={{0,2},{1,3},{2,4},{3,5},{4,6},{5,7},{6,0},{7,1},{8,10},{9,11},{10,... | collective-permute-start | bytes 393224 | tf_op jit(solution)/shard_map/ppermute | solution.py:447
  63.8 8.5 %collective-permute-start.11 = (bf16[256,256]{1,0:T(8,128)(2,1)S(1)}, bf16[256,256]{1,0:T(8,128)(2,1)S(1)}, u32[]{:S(2)}, u32[]{:S(2)}) collective-permute-start(bf16[256,256]{1,0:T(8,128)(2,1)S(1)} %get-tuple-element.49), channel_id=1, source_target_pairs={{0,4},{1,5},{2,6},{3,7},{4,0},{5,1},{6,2},{7,3},{8,12},{9,13},{10,... | collective-permute-start | bytes 393224 | tf_op jit(solution)/shard_map/ppermute | solution.py:447
  65.7 7.2 %collective-permute-start.12 = (bf16[256,256]{1,0:T(8,128)(2,1)S(1)}, bf16[256,256]{1,0:T(8,128)(2,1)S(1)}, u32[]{:S(2)}, u32[]{:S(2)}) collective-permute-start(bf16[256,256]{1,0:T(8,128)(2,1)S(1)} %get-tuple-element.50), channel_id=1, source_target_pairs={{0,6},{1,7},{2,0},{3,1},{4,2},{5,3},{6,4},{7,5},{8,14},{9,15},{10,... | collective-permute-start | bytes 393224 | tf_op jit(solution)/shard_map/ppermute | solution.py:447

commit v3 on v2

--- a/solution.py
+++ b/solution.py
@@ -14,7 +14,7 @@
 XSIZE, YSIZE, ZSIZE = 4, 4, 8
 F32 = jnp.float32
 BF16 = jnp.bfloat16
-DECAY, GAMMA, READ, SKIP, DIL, PARAMS = 8, 10, 12, 14, 15, 16
+DECAY, GAMMA, READ, SKIP, DIL, KEPT, PARAMS = 8, 10, 12, 14, 15, 16, 24
 
 
 def spread_rows(row):
@@ -79,6 +79,7 @@
     par_ref[GAMMA : GAMMA + 2, :] = jnp.sqrt(1.0 - decays * decays)
     par_ref[READ : READ + 2, :] = ro_ref[...]
     par_ref[SKIP : SKIP + 1, :] = skip_ref[...]
+    par_ref[KEPT:PARAMS, :] = jnp.broadcast_to(ret_ref[...], (PARAMS - KEPT, width))
     for which in range(2):
         par_ref[DIL : DIL + 1, which * LANES : (which + 1) * LANES] = jnp.full(
             (1, LANES), dil_ref[which], jnp.int32
@@ -153,8 +154,8 @@
 
 
 def forward_final(
-    got_ref, drv_ref, segh_ref, segp_ref, par_ref, rb_ref, near_ref, far_ref,
-    mixed_ref, w0_ref, w1_ref, w2_ref, w3_ref, rprod_ref,
+    got_ref, drv_ref, segh_ref, segp_ref, par_ref, rb_ref,
+    mixed_ref, rprod_ref,
     mix_ref,
 ):
     rows, width = mixed_ref.shape
@@ -195,18 +196,6 @@
                 readout[0] * state[0] + readout[1] * state[1] + skip * u
             )
         mixed_ref[:, cols] = mix_ref[half].astype(BF16)
-    flipped = jnp.transpose(
-        jnp.concatenate([mix_ref[half] for half, _ in halves(width)], axis=1)
-    ).astype(BF16)
-    core = core_index()
-    mine = pl.ds(pl.multiple_of(core * width, width), width)
-    other = pl.ds(pl.multiple_of((1 - core) * width, width), width)
-    for d, part in ((1, w1_ref), (2, w2_ref), (3, w3_ref), (0, w0_ref)):
-        at = lax.rem(y_index() - x_index() - d + 2 * YSIZE, YSIZE)
-        for cols, source in ((mine, near_ref), (other, far_ref)):
-            part[:, cols] = jnp.dot(
-                flipped, source[at], preferred_element_type=F32
-            ).astype(part.dtype)
 
 
 def project(mixed_ref, wout_ref, send_ref):
@@ -237,15 +226,27 @@
     out_ref[...] = (sig_ref[...].astype(F32) + total).astype(BF16)
 
 
-def pack(own_ref, a_ref, b_ref, c_ref, out_ref):
+def facing(distance):
+    return lax.rem(y_index() - x_index() - distance + 2 * YSIZE, YSIZE)
+
+
+def pack(own_ref, a_ref, b_ref, c_ref, out_ref, s1_ref, s2_ref, s3_ref):
     for d, source in enumerate((own_ref, a_ref, b_ref, c_ref)):
         out_ref[d] = source[...]
+    for d, send_ref in ((1, s1_ref), (2, s2_ref), (3, s3_ref)):
+        send_ref[...] = out_ref[facing(d)]
+
+
+def stack(near_ref, a_ref, b_ref, c_ref, out_ref):
+    width = out_ref.shape[0]
+    for d, block in enumerate((near_ref[facing(0)], a_ref[...], b_ref[...], c_ref[...])):
+        out_ref[:, d * width : (d + 1) * width] = jnp.transpose(block.astype(F32)).astype(BF16)
 
 
 def backward_local(
-    near_ref, far_ref, wout_ref, segp_ref, par_ref, rb_ref, ends_ref, ret_ref,
-    gm_ref, pay_ref, segw_ref, halo_ref,
-    gd_ref, tile_ref,
+    near_ref, far_ref, wout_ref, segp_ref, par_ref, rb_ref, ends_ref,
+    gm_ref, pay_ref,
+    tile_ref,
 ):
     rows = rb_ref.shape[0]
     width = par_ref.shape[1]
@@ -260,51 +261,65 @@
                 source[d], wout_ref[:, pl.ds(start, width)], (((1,), (1,)), ((), ())),
                 preferred_element_type=F32,
             )
+    tile_ref[0] = ends_ref[...]
+    tile_ref[2, 2:4, :] = jnp.ones((2, LANES), F32)
     for half, cols in halves(width):
-        gm_ref[half] = grad_mixed[:, cols]
-        decay, gamma = params(par_ref, DECAY, cols), params(par_ref, GAMMA, cols)
-        readout = params(par_ref, READ, cols)
-        skip = par_ref[SKIP : SKIP + 1, cols]
+        gm_ref[half, 0:rows, :] = grad_mixed[:, cols]
+        tile_ref[2, half : half + 1, :] = par_ref[KEPT : KEPT + 1, cols]
+        decay, readout = params(par_ref, DECAY, cols), params(par_ref, READ, cols)
         passed = [jnp.zeros((SEGS, LANES), F32) for _ in range(2)]
         for i in reversed(range(steps)):
             r = rb_ref[pl.ds(i, SEGS, stride=steps), :]
             g = gm_ref[half, pl.ds(i, SEGS, stride=steps), :]
             for p in range(2):
                 passed[p] = (decay[p] * r) * (readout[p] * g + passed[p])
-        inits = []
         for p in range(2):
-            segw_ref[half, p] = passed[p]
+            gm_ref[half, rows + p * SEGS : rows + (p + 1) * SEGS, :] = passed[p]
+            here = jnp.zeros((1, LANES), F32)
+            for s in reversed(range(SEGS)):
+                here = row_of(passed[p], s) + segp_ref[half, p, s : s + 1, :] * here
+            tile_ref[1, 2 * p + half : 2 * p + half + 1, :] = here
+    tile = tile_ref[...]
+    for copy in range(pay_ref.shape[0]):
+        pay_ref[copy] = tile
+
+
+def backward_sends(
+    gm_ref, segp_ref, par_ref, rb_ref,
+    halo_ref,
+    gd_ref,
+):
+    rows = rb_ref.shape[0]
+    width = par_ref.shape[1]
+    steps = rows // SEGS
+    for half, cols in halves(width):
+        decay, gamma = params(par_ref, DECAY, cols), params(par_ref, GAMMA, cols)
+        readout = params(par_ref, READ, cols)
+        skip = par_ref[SKIP : SKIP + 1, cols]
+        passed = []
+        for p in range(2):
+            segw = gm_ref[half, rows + p * SEGS : rows + (p + 1) * SEGS, :]
             here = jnp.zeros((1, LANES), F32)
             starts = [here]
             for s in reversed(range(1, SEGS)):
-                here = row_of(passed[p], s) + segp_ref[half, p, s : s + 1, :] * here
+                here = row_of(segw, s) + segp_ref[half, p, s : s + 1, :] * here
                 starts.append(here)
-            tile_ref[1, 2 * p + half : 2 * p + half + 1, :] = (
-                row_of(passed[p], 0) + segp_ref[half, p, 0:1, :] * here
-            )
-            inits.append(jnp.concatenate(starts[::-1], axis=0))
+            passed.append(jnp.concatenate(starts[::-1], axis=0))
         for i in reversed(range(steps)):
             r = rb_ref[pl.ds(i, SEGS, stride=steps), :]
             g = gm_ref[half, pl.ds(i, SEGS, stride=steps), :]
             total = None
             for p in range(2):
-                grad_state = readout[p] * g + inits[p]
-                inits[p] = (decay[p] * r) * grad_state
+                grad_state = readout[p] * g + passed[p]
+                passed[p] = (decay[p] * r) * grad_state
                 term = gamma[p] * grad_state
                 total = term if total is None else total + term
             gd_ref[pl.ds(i, SEGS, stride=steps), :] = skip * g + total
         halo_ref[:, cols] = gd_ref[0:REACH, :].astype(BF16)
-    tile_ref[0] = ends_ref[...]
-    for half, cols in halves(width):
-        tile_ref[2, half : half + 1, :] = ret_ref[0:1, cols]
-    tile_ref[2, 2:4, :] = jnp.ones((2, LANES), F32)
-    tile = tile_ref[...]
-    for copy in range(pay_ref.shape[0]):
-        pay_ref[copy] = tile
 
 
 def backward_final(
-    got_ref, rprod_ref, gm_ref, segw_ref, segp_ref, halo_ref, rb_ref, par_ref, cot_ref,
+    got_ref, rprod_ref, gm_ref, segp_ref, halo_ref, rb_ref, par_ref, cot_ref,
     out_ref,
     rn_ref, ahead_ref, far_ref, first_ref,
 ):
@@ -339,7 +354,8 @@
             seg = kept * power(decay[p], steps)
             starts, fars = [here], [far]
             for s in reversed(range(1, SEGS)):
-                here = segw_ref[half, p, s : s + 1, :] + segp_ref[half, p, s : s + 1, :] * here
+                segw = gm_ref[half, rows + p * SEGS + s : rows + p * SEGS + s + 1, :]
+                here = segw + segp_ref[half, p, s : s + 1, :] * here
                 far = row_of(seg, s) * far
                 starts.append(here)
                 fars.append(far)
@@ -373,24 +389,20 @@
         out_ref[:, cols] = (cot_ref[:, cols].astype(F32) + total).astype(BF16)
 
 
-def near_sum(a_ref, b_ref, c_ref, d_ref, out_ref):
-    total = (a_ref[...].astype(F32) + b_ref[...].astype(F32)) + (
-        c_ref[...].astype(F32) + d_ref[...].astype(F32)
-    )
-    rows, width = total.shape
-    wide = width // ZSIZE
-    for z in range(ZSIZE):
-        piece = total[:, z * wide : (z + 1) * wide]
-        out_ref[z] = jnp.concatenate([piece[: rows // 2], piece[rows // 2 :]], axis=1).astype(BF16)
+def weight_pieces(f0_ref, f1_ref, f2_ref, f3_ref, own_ref, other_ref, out_ref):
+    mixed = jnp.concatenate([f0_ref[...], f1_ref[...], f2_ref[...], f3_ref[...]], axis=0)
+    wide = out_ref.shape[1]
+    for source, core in ((own_ref, core_index()), (other_ref, 1 - core_index())):
+        total = jnp.dot(source[...], mixed, preferred_element_type=F32).astype(BF16)
+        for z in range(ZSIZE // 2):
+            out_ref[core * (ZSIZE // 2) + z] = total[z * wide : (z + 1) * wide]
 
 
 def far_sum(in_ref, out_ref):
     total = in_ref[0].astype(F32)
     for z in range(1, ZSIZE):
         total = total + in_ref[z].astype(F32)
-    flipped = jnp.transpose(total)
-    wide = flipped.shape[0] // 2
-    out_ref[...] = jnp.concatenate([flipped[:wide], flipped[wide:]], axis=1)
+    out_ref[...] = total
 
 
 def vmem(shape, dtype=F32):
@@ -483,24 +495,34 @@
         aliases={3: 0}, cost=20,
     )(halo, par, rb, driven, fhead, shead)
 
-    (near,) = call(pack, [((YSIZE,) + square, BF16)])(own_cot, *from_y, after=(segh,))
+    near, c1, c2, c3 = call(pack, [((YSIZE,) + square, BF16)] + [(square, BF16)] * 3)(
+        own_cot, *from_y, after=(segh,)
+    )
+    c1, c2, c3 = along_x(c1, 1), along_x(c2, 2), along_x(c3, 3)
     far = other_core(near)
-    grad_mixed, payload, segw, bhalo = call(
-        backward_local, [tall, ((count, 3, 4, LANES), F32), seg, ((REACH, width), BF16)],
-        [vmem((rows, LANES)), vmem((3, 4, LANES))], cost=20,
-    )(near, far, w_out, segp, par, rb, ends, ret)
+    grad_mixed, payload = call(
+        backward_local,
+        [((nh, rows + 2 * SEGS, LANES), F32), ((count, 3, 4, LANES), F32)],
+        [vmem((3, 4, LANES))], cost=20,
+    )(near, far, w_out, segp, par, rb, ends)
     got = lax.all_to_all(payload, "seq", 0, 0, tiled=True)
+
+    (chip,) = call(stack, [((width, XSIZE * rows), BF16)])(near, c1, c2, c3, after=(payload,))
+    chip_far = other_core(chip)
+    (bhalo,) = call(
+        backward_sends, [((REACH, width), BF16)], [vmem((rows, LANES))], cost=20,
+    )(grad_mixed, segp, par, rb, after=(chip,))
     later = shifted(bhalo, -1)
 
-    mixed, w0, w1, w2, w3, rprod = call(
-        forward_final,
-        [(square, BF16)] + [((width, 2 * width), BF16)] * 4 + [((count, LANES), F32)],
+    mixed, rprod = call(
+        forward_final, [(square, BF16), ((count, LANES), F32)],
         [vmem((nh, rows, LANES))], cost=20,
-    )(got, driven, segh, segp, par, rb, near, far, after=(later,))
-    w1, w2, w3 = along_x(w1, 1), along_x(w2, 2), along_x(w3, 3)
+    )(got, driven, segh, segp, par, rb, after=(later, chip))
+    f1, f2, f3 = along_x(mixed, 1), along_x(mixed, 2), along_x(mixed, 3)
 
     (send,) = call(project, [((YSIZE,) + square, BF16)], cost=20)(mixed, w_out)
     pair = other_core(send)
+
     (grad_signal,) = call(
         backward_final, [(square, BF16)],
         [
@@ -508,24 +530,23 @@
             vmem((rows + MARGIN, LANES)),
         ],
         cost=1,
-    )(got, rprod, grad_mixed, segw, segp, later, rb, par, own_cot, after=(send,))
-
-
+    )(got, rprod, grad_mixed, segp, later, rb, par, own_cot, after=(send,))
     groups = [[x * ZSIZE + z for z in range(ZSIZE)] for x in range(XSIZE)]
     wide = 2 * width // ZSIZE
-    (sums,) = call(near_sum, [((ZSIZE, width // 2, 2 * wide), BF16)], cost=20)(
-        w0, w1, w2, w3,
-        after=(pltpu.with_memory_space_constraint(grad_signal, pltpu.HBM),),
-    )
+    (sums,) = call(weight_pieces, [((ZSIZE, wide, width), BF16)], cost=20)(
+        mixed, f1, f2, f3, chip, chip_far, after=(pltpu.with_memory_space_constraint(grad_signal, pltpu.HBM),)
+    )
+    pieces = lax.all_to_all(sums, "seq", 0, 0, axis_index_groups=groups, tiled=True)
+
     own, p1, p2, p3 = call(pair_sum, [(square, F32)] + [(square, BF16)] * 3)(
         mixed, w_out, pair, after=(sums,)
     )
     p1, p2, p3 = along_y(p1, 1), along_y(p2, 2), along_y(p3, 3)
-    (output,) = call(finish_output, [(square, BF16)])(signal, own, p1, p2, p3)
-
-    sums = lax.all_to_all(sums, "seq", 0, 0, axis_index_groups=groups, tiled=True)
-    (grad_w_out,) = call(far_sum, [((wide, width), F32)])(sums)
-
+
+    (output,) = call(finish_output, [(square, BF16)])(
+        signal, own, p1, p2, p3
+    )
+    (grad_w_out,) = call(far_sum, [((wide, width), F32)])(pieces)
     return (output, grad_signal, grad_w_out.T)
 
 

time: 76 us -> 74.1 us (0.975)
  waiting for transfers between devices: 26.3 us -> 20.9 us
  Pallas kernels: 9.68 us -> 11.9 us
  starting transfers between devices: 36.4 us -> 38.5 us
  local copies, waits for them, and re-layouts: 2.4 us -> 0.81 us
    all_to_all x1, waiting for transfers between devices: 1.16 us -> 6.81 us  [per_device(): lax.all_to_all(sums, 'seq', 0, 0, axis_index_groups=groups, tiled=True)]
    ppermute x6, waiting for transfers between devices: 5.56 us -> 0.02 us  [along_y(): lax.ppermute(block, 'ch', [(i, (i + 2 * distance) % size) for i in range(...]
    ppermute x3 -> x6, starting transfers between devices: 4.11 us -> 9.23 us  [along_x(): lax.ppermute(block, 'seq', [(i, (i + distance * ZSIZE) % size) for i in r...]
    pallas_call x11 -> x13, Pallas kernels: 9.68 us -> 11.9 us  [run(): pl.pallas_call(body, out_shape=tuple((jax.ShapeDtypeStruct(shape, dtype)...]
    ppermute x3 -> x6, waiting for transfers between devices: 7.09 us -> 4.84 us  [along_x(): lax.ppermute(block, 'seq', [(i, (i + distance * ZSIZE) % size) for i in r...]
    ppermute x2 -> x3, waiting for transfers between devices: 1.9 us -> 0.01 us  [other_core(): return lax.ppermute(block, 'ch', [(i, i ^ 1) for i in range(2 * YSIZE)])]
    all_to_all x1, starting transfers between devices: 9.01 us -> 7.19 us  [per_device(): got = lax.all_to_all(payload, 'seq', 0, 0, tiled=True)]
    unnamed x10 -> x4, local copies, waits for them, and re-layouts: 1.59 us -> 0.01 us
  transfers between devices with their start and end apart: 15 -> 19, of which waited for: 10 -> 7; matrix products, arithmetic and copies ran while one was open for 1% -> 1% of each run, Pallas kernels for 8% -> 15%
where the time goes in v3:
time: 74.1 us; the launch traced here: 73 us
  starting transfers between devices  38.5 us (52%)
  waiting for transfers between devices  20.9 us (28%)
  Pallas kernels  11.9 us (16%)
  local copies, waits for them, and re-layouts  0.81 us (1%)
  between operations  0.8 us (1%)
    pallas_call x13, Pallas kernels, run(): pl.pallas_call(body, out_shape=tuple((jax.ShapeDtypeStruct(shape, dtype)...  11.9 us
    ppermute x6, starting transfers between devices, along_y(): lax.ppermute(block, 'ch', [(i, (i + 2 * distance) % size) for i in range(...  9.44 us
    ppermute x6, starting transfers between devices, along_x(): lax.ppermute(block, 'seq', [(i, (i + distance * ZSIZE) % size) for i in r...  9.23 us
    ppermute x2, starting transfers between devices, shifted(): lax.ppermute(block, 'seq', [(i - distance, i) for i in devices if i - dis...  8.39 us
    all_to_all x1, starting transfers between devices, per_device(): got = lax.all_to_all(payload, 'seq', 0, 0, tiled=True)  7.19 us
    all_to_all x1, waiting for transfers between devices, per_device(): lax.all_to_all(sums, 'seq', 0, 0, axis_index_groups=groups, tiled=True)  6.81 us
    ppermute x2, waiting for transfers between devices, shifted(): lax.ppermute(block, 'seq', [(i - distance, i) for i in devices if i - dis...  6.41 us
    ppermute x6, waiting for transfers between devices, along_x(): lax.ppermute(block, 'seq', [(i, (i + distance * ZSIZE) % size) for i in r...  4.84 us
  transfers between devices with their start and end apart: 19, of which 7 were waited for; matrix products, arithmetic and copies ran while one was open for 1% of the time, Pallas kernels for 15%

profile of v3, /device:TPU:2, one launch (start us, length us, event | category | flops | bytes accessed | tf_op | source)
XLA Modules:
  0.0 73.0 jit_solution(10678855218268278745)
XLA Ops:
  0.6 1.7 %collective-permute-start = (bf16[256,256]{1,0:T(8,128)(2,1)}, bf16[256,256]{1,0:T(8,128)(2,1)S(1)}, u32[]{:S(2)}, u32[]{:S(2)}) collective-permute-start(bf16[256,256]{1,0:T(8,128)(2,1)} %refs_6_.1), channel_id=1, source_target_pairs={{0,2},{1,3},{2,4},{3,5},{4,6},{5,7},{6,0},{7,1},{8,10},{9,11},{10,... | collective-permute-start | bytes 393224 | tf_op jit(solution)/shard_map/ppermute | solution.py:459
  2.3 2.9 %collective-permute-start.1 = (bf16[256,256]{1,0:T(8,128)(2,1)}, bf16[256,256]{1,0:T(8,128)(2,1)S(1)}, u32[]{:S(2)}, u32[]{:S(2)}) collective-permute-start(bf16[256,256]{1,0:T(8,128)(2,1)} %refs_6_.1), channel_id=1, source_target_pairs={{0,4},{1,5},{2,6},{3,7},{4,0},{5,1},{6,2},{7,3},{8,12},{9,13},{10,... | collective-permute-start | bytes 393224 | tf_op jit(solution)/shard_map/ppermute | solution.py:459
  5.2 1.3 %collective-permute-start.2 = (bf16[256,256]{1,0:T(8,128)(2,1)}, bf16[256,256]{1,0:T(8,128)(2,1)S(1)}, u32[]{:S(2)}, u32[]{:S(2)}) collective-permute-start(bf16[256,256]{1,0:T(8,128)(2,1)} %refs_6_.1), channel_id=1, source_target_pairs={{0,6},{1,7},{2,0},{3,1},{4,2},{5,3},{6,4},{7,5},{8,14},{9,15},{10,... | collective-permute-start | bytes 393224 | tf_op jit(solution)/shard_map/ppermute | solution.py:459
  7.3 3.8 %collective-permute-start.3 = (bf16[96,256]{1,0:T(8,128)(2,1)S(1)}, bf16[96,256]{1,0:T(8,128)(2,1)S(1)}, u32[]{:S(2)}, u32[]{:S(2)}) collective-permute-start(bf16[96,256]{1,0:T(8,128)(2,1)S(1)} %slice.3), channel_id=1, source_target_pairs={{0,8},{8,16},{16,24},{24,32},{32,40},{40,48},{48,56},{56,64},{64,7... | collective-permute-start | bytes 147464 | tf_op jit(solution)/shard_map/ppermute | solution.py:445
  11.2 1.3 %gather_inputs.1 = (f32[24,256]{1,0:T(8,128)S(1)}, f32[256,128]{1,0:T(8,128)S(1)}, f32[2,256,128]{2,1,0:T(8,128)S(1)}, f32[2,48,128]{2,1,0:T(8,128)S(1)}, f32[2,...) custom-call(bf16[256,256]{1,0:T(8,128)(2,1)} %refs_0_.3, f32[2,4,256]{2,1,0:T(4,128)} %refs_1_.3, f32[2,256]{1,0:T(2,128)} %refs_2_.2, ...), custom_call_target="tpu_custom_call" | custom-call | bytes 70000000 | tf_op jit(solution)/shard_map/gather_inputs/pallas_call | solution.py:426
  12.5 4.7 %collective-permute-done.3.refs_0_ = bf16[96,256]{1,0:T(8,128)(2,1)S(1)} collective-permute-done((bf16[96,256]{1,0:T(8,128)(2,1)S(1)}, bf16[96,256]{1,0:T(8,128)(2,1)S(1)}, u32[]{:S(2)}, u32[]{:S(2)}) %collective-permute-start.3) | collective-permute-done | bytes 49184 | tf_op jit(solution)/shard_map/ppermute | solution.py:445
  17.8 1.6 %collective-permute-start.5 = (bf16[256,256]{1,0:T(8,128)(2,1)S(1)}, bf16[256,256]{1,0:T(8,128)(2,1)S(1)}, u32[]{:S(2)}, u32[]{:S(2)}) collective-permute-start(bf16[256,256]{1,0:T(8,128)(2,1)S(1)} %get-tuple-element.38), channel_id=1, source_target_pairs={{0,64},{8,72},{16,80},{24,88},{32,96},{40,104},{48,112},{56,120},{... | collective-permute-start | bytes 393224 | tf_op jit(solution)/shard_map/ppermute | solution.py:452
  19.4 1.0 %collective-permute-start.6 = (bf16[256,256]{1,0:T(8,128)(2,1)S(1)}, bf16[256,256]{1,0:T(8,128)(2,1)S(1)}, u32[]{:S(2)}, u32[]{:S(2)}) collective-permute-start(bf16[256,256]{1,0:T(8,128)(2,1)S(1)} %get-tuple-element.39), channel_id=1, source_target_pairs={{0,128},{8,136},{16,144},{24,152},{32,160},{40,168},{48,176},{56,1... | collective-permute-start | bytes 393224 | tf_op jit(solution)/shard_map/ppermute | solution.py:452
  20.4 2.5 %collective-permute-start.7 = (bf16[256,256]{1,0:T(8,128)(2,1)S(1)}, bf16[256,256]{1,0:T(8,128)(2,1)S(1)}, u32[]{:S(2)}, u32[]{:S(2)}) collective-permute-start(bf16[256,256]{1,0:T(8,128)(2,1)S(1)} %get-tuple-element.40), channel_id=1, source_target_pairs={{0,192},{8,200},{16,208},{24,216},{32,224},{40,232},{48,240},{56,2... | collective-permute-start | bytes 393224 | tf_op jit(solution)/shard_map/ppermute | solution.py:452
  22.9 1.6 %backward_local.1 = (f32[2,272,128]{2,1,0:T(8,128)S(1)}, f32[32,3,4,128]{3,2,1,0:T(4,128)}) custom-call(bf16[4,256,256]{2,1,0:T(8,128)(2,1)S(1)} %get-tuple-element.32.refs_0_, bf16[4,256,256]{2,1,0:T(8,128)(2,1)S(1)} %collective-permute-done.4.refs_1_, bf16[256,2048]{1,0:T(8,128)(2,1)S(1)} %copy-done, ...), custom_call_target="tpu_custom_call" | custom-call | bytes 70000000 | tf_op jit(solution)/shard_map/backward_local/pallas_call | solution.py:426
  24.5 7.2 %all-to-all-start = ((f32[32,3,4,128]{3,2,1,0:T(4,128)}), f32[32,3,4,128]{3,2,1,0:T(4,128)S(1)}, u32[]{:S(2)}, u32[]{:S(2)}) async-start(f32[32,3,4,128]{3,2,1,0:T(4,128)} %get-tuple-element.35.refs_4_), calls=%async_computation | async-start | bytes 393216 | tf_op jit(solution)/shard_map/all_to_all | solution.py:508
  32.4 4.6 %collective-permute-start.8 = (bf16[96,256]{1,0:T(8,128)(2,1)S(1)}, bf16[96,256]{1,0:T(8,128)(2,1)S(1)}, u32[]{:S(2)}, u32[]{:S(2)}) collective-permute-start(bf16[96,256]{1,0:T(8,128)(2,1)S(1)} %backward_sends.1), channel_id=1, source_target_pairs={{8,0},{16,8},{24,16},{32,24},{40,32},{48,40},{56,48},{64,56},{72,6... | collective-permute-start | bytes 147464 | tf_op jit(solution)/shard_map/ppermute | solution.py:445
  37.0 1.7 %collective-permute-done.8.refs_6_.refs_4_ = bf16[96,256]{1,0:T(8,128)(2,1)S(1)} collective-permute-done((bf16[96,256]{1,0:T(8,128)(2,1)S(1)}, bf16[96,256]{1,0:T(8,128)(2,1)S(1)}, u32[]{:S(2)}, u32[]{:S(2)}) %collective-permute-start.8) | collective-permute-done | bytes 49184 | tf_op jit(solution)/shard_map/ppermute | solution.py:445
  38.7 2.8 %all-to-all-done.refs_0_ = f32[32,3,4,128]{3,2,1,0:T(4,128)S(1)} async-done(((f32[32,3,4,128]{3,2,1,0:T(4,128)}), f32[32,3,4,128]{3,2,1,0:T(4,128)S(1)}, u32[]{:S(2)}, u32[]{:S(2)}) %all-to-all-start) | async-done | bytes 196640 | tf_op jit(solution)/shard_map/all_to_all | solution.py:508
  41.6 1.0 %forward_final.1 = (bf16[256,256]{1,0:T(8,128)(2,1)S(1)}, f32[32,128]{1,0:T(8,128)S(1)}) custom-call(f32[32,3,4,128]{3,2,1,0:T(4,128)S(1)} %all-to-all-done.refs_0_, f32[2,256,128]{2,1,0:T(8,128)S(1)} %get-tuple-element.36.refs_1_, f32[2,2,8,128]{3,2,1,0:T(8,128)S(1)} %get-tuple-element.31.refs_4_.refs_2_, ...), custom_call_target="tpu_custom_call" | custom-call | bytes 70000000 | tf_op jit(solution)/shard_map/forward_final/pallas_call | solution.py:426
  43.8 2.8 %collective-permute-start.11 = (bf16[256,256]{1,0:T(8,128)(2,1)S(1)}, bf16[256,256]{1,0:T(8,128)(2,1)S(1)}, u32[]{:S(2)}, u32[]{:S(2)}) collective-permute-start(bf16[256,256]{1,0:T(8,128)(2,1)S(1)} %get-tuple-element.41.refs_0_), channel_id=1, source_target_pairs={{0,128},{8,136},{16,144},{24,152},{32,160},{40,168},{48,176},{56,1... | collective-permute-start | bytes 393224 | tf_op jit(solution)/shard_map/ppermute | solution.py:452
  47.1 1.7 %backward_final.1.refs_6_ = bf16[256,256]{1,0:T(8,128)(2,1)} custom-call(f32[32,3,4,128]{3,2,1,0:T(4,128)S(1)} %all-to-all-done.refs_0_, f32[32,128]{1,0:T(8,128)S(1)} %get-tuple-element.42.refs_1_, f32[2,272,128]{2,1,0:T(8,128)S(1)} %get-tuple-element.37.refs_0_.refs_2_, f32[2,2,8,128]{3,2,1,0:T(8,128)S(1)} %get-tuple-element.33.refs_3_.refs_1_, ...), custom_call_target="tpu_custom_call" | custom-call | bytes 3500000 | tf_op jit(solution)/shard_map/backward_final/pallas_call | solution.py:426
  49.4 2.2 %collective-permute-done.11.refs_2_ = bf16[256,256]{1,0:T(8,128)(2,1)S(1)} collective-permute-done((bf16[256,256]{1,0:T(8,128)(2,1)S(1)}, bf16[256,256]{1,0:T(8,128)(2,1)S(1)}, u32[]{:S(2)}, u32[]{:S(2)}) %collective-permute-start.11) | collective-permute-done | bytes 131104 | tf_op jit(solution)/shard_map/ppermute | solution.py:452
  51.6 2.0 %collective-permute-done.12.refs_3_ = bf16[256,256]{1,0:T(8,128)(2,1)S(1)} collective-permute-done((bf16[256,256]{1,0:T(8,128)(2,1)S(1)}, bf16[256,256]{1,0:T(8,128)(2,1)S(1)}, u32[]{:S(2)}, u32[]{:S(2)}) %collective-permute-start.12) | collective-permute-done | bytes 131104 | tf_op jit(solution)/shard_map/ppermute | solution.py:452
  53.7 2.2 %weight_pieces.1.refs_3_ = bf16[8,64,256]{2,1,0:T(8,128)(2,1)} custom-call(bf16[256,256]{1,0:T(8,128)(2,1)S(1)} %get-tuple-element.41.refs_0_, bf16[256,256]{1,0:T(8,128)(2,1)S(1)} %collective-permute-done.10.refs_1_, bf16[256,256]{1,0:T(8,128)(2,1)S(1)} %collective-permute-done.11.refs_2_, bf16[256,256]{1,0:T(8,128)(2,1)S(1)} %collective-permute-done.12.refs_3_, ...), custom_call_target="tpu_custom_call" | custom-call | bytes 70000000 | tf_op jit(solution)/shard_map/weight_pieces/pallas_call | solution.py:426
  55.9 4.0 %all-to-all-start.1 = ((bf16[8,64,256]{2,1,0:T(8,128)(2,1)}), bf16[8,64,256]{2,1,0:T(8,128)(2,1)S(1)}, u32[]{:S(2)}, u32[]{:S(2)}) async-start(bf16[8,64,256]{2,1,0:T(8,128)(2,1)} %weight_pieces.1.refs_3_), calls=%async_computation.1 | async-start | bytes 524288 | tf_op jit(solution)/shard_map/all_to_all | solution.py:539
  59.8 1.3 %pair_sum.1 = (f32[256,256]{1,0:T(8,128)S(1)}, bf16[256,256]{1,0:T(8,128)(2,1)S(1)}, bf16[256,256]{1,0:T(8,128)(2,1)S(1)}, bf16[256,256]{1,0:T(8,128)(2,1)S(1)}) custom-call(bf16[256,256]{1,0:T(8,128)(2,1)S(1)} %get-tuple-element.41.refs_0_, bf16[256,2048]{1,0:T(8,128)(2,1)S(1)} %copy-done, bf16[4,256,256]{2,1,0:T(8,128)(2,1)} %collective-permute-done.9.refs_2_, ...), custom_call_target="tpu_custom_call" | custom-call | bytes 3500000 | tf_op jit(solution)/shard_map/pair_sum/pallas_call | solution.py:426
  62.7 2.0 %collective-permute-start.16 = (bf16[256,256]{1,0:T(8,128)(2,1)S(1)}, bf16[256,256]{1,0:T(8,128)(2,1)S(1)}, u32[]{:S(2)}, u32[]{:S(2)}) collective-permute-start(bf16[256,256]{1,0:T(8,128)(2,1)S(1)} %get-tuple-element.46), channel_id=1, source_target_pairs={{0,6},{1,7},{2,0},{3,1},{4,2},{5,3},{6,4},{7,5},{8,14},{9,15},{10,... | collective-permute-start | bytes 393224 | tf_op jit(solution)/shard_map/ppermute | solution.py:459
  64.7 6.8 %all-to-all-done.1.refs_0_ = bf16[8,64,256]{2,1,0:T(8,128)(2,1)S(1)} async-done(((bf16[8,64,256]{2,1,0:T(8,128)(2,1)}), bf16[8,64,256]{2,1,0:T(8,128)(2,1)S(1)}, u32[]{:S(2)}, u32[]{:S(2)}) %all-to-all-start.1) | async-done | bytes 262176 | tf_op jit(solution)/shard_map/all_to_all | solution.py:539
  (32 shorter events, 7.4 us)
Async XLA Ops:
  0.6 22.3 %copy-start = (bf16[256,2048]{1,0:T(8,128)(2,1)S(1)}, bf16[256,2048]{1,0:T(8,128)(2,1)}, u32[]{:S(2)}) copy-start(bf16[256,2048]{1,0:T(8,128)(2,1)} %refs_1_.5) | copy-start | bytes 3145732
  0.6 17.0 %collective-permute-start = (bf16[256,256]{1,0:T(8,128)(2,1)}, bf16[256,256]{1,0:T(8,128)(2,1)S(1)}, u32[]{:S(2)}, u32[]{:S(2)}) collective-permute-start(bf16[256,256]{1,0:T(8,128)(2,1)} %refs_6_.1), channel_id=1, source_target_pairs={{0,2},{1,3},{2,4},{3,5},{4,6},{5,7},{6,0},{7,1},{8,10},{9,11},{10,... | collective-permute-start | bytes 393224 | tf_op jit(solution)/shard_map/ppermute | solution.py:459
  2.3 15.3 %collective-permute-start.1 = (bf16[256,256]{1,0:T(8,128)(2,1)}, bf16[256,256]{1,0:T(8,128)(2,1)S(1)}, u32[]{:S(2)}, u32[]{:S(2)}) collective-permute-start(bf16[256,256]{1,0:T(8,128)(2,1)} %refs_6_.1), channel_id=1, source_target_pairs={{0,4},{1,5},{2,6},{3,7},{4,0},{5,1},{6,2},{7,3},{8,12},{9,13},{10,... | collective-permute-start | bytes 393224 | tf_op jit(solution)/shard_map/ppermute | solution.py:459
  5.2 12.4 %collective-permute-start.2 = (bf16[256,256]{1,0:T(8,128)(2,1)}, bf16[256,256]{1,0:T(8,128)(2,1)S(1)}, u32[]{:S(2)}, u32[]{:S(2)}) collective-permute-start(bf16[256,256]{1,0:T(8,128)(2,1)} %refs_6_.1), channel_id=1, source_target_pairs={{0,6},{1,7},{2,0},{3,1},{4,2},{5,3},{6,4},{7,5},{8,14},{9,15},{10,... | collective-permute-start | bytes 393224 | tf_op jit(solution)/shard_map/ppermute | solution.py:459
  7.3 9.8 %collective-permute-start.3 = (bf16[96,256]{1,0:T(8,128)(2,1)S(1)}, bf16[96,256]{1,0:T(8,128)(2,1)S(1)}, u32[]{:S(2)}, u32[]{:S(2)}) collective-permute-start(bf16[96,256]{1,0:T(8,128)(2,1)S(1)} %slice.3), channel_id=1, source_target_pairs={{0,8},{8,16},{16,24},{24,32},{32,40},{40,48},{48,56},{56,64},{64,7... | collective-permute-start | bytes 147464 | tf_op jit(solution)/shard_map/ppermute | solution.py:445
  17.7 5.2 %collective-permute-start.4 = (bf16[4,256,256]{2,1,0:T(8,128)(2,1)S(1)}, bf16[4,256,256]{2,1,0:T(8,128)(2,1)S(1)}, u32[]{:S(2)}, u32[]{:S(2)}) collective-permute-start(bf16[4,256,256]{2,1,0:T(8,128)(2,1)S(1)} %get-tuple-element.32.refs_0_), channel_id=1, source_target_pairs={{0,1},{1,0},{2,3},{3,2},{4,5},{5,4},{6,7},{7,6},{8,9},{9,8},{10,11... | collective-permute-start | bytes 1572872 | tf_op jit(solution)/shard_map/ppermute | solution.py:463
  17.8 13.9 %collective-permute-start.5 = (bf16[256,256]{1,0:T(8,128)(2,1)S(1)}, bf16[256,256]{1,0:T(8,128)(2,1)S(1)}, u32[]{:S(2)}, u32[]{:S(2)}) collective-permute-start(bf16[256,256]{1,0:T(8,128)(2,1)S(1)} %get-tuple-element.38), channel_id=1, source_target_pairs={{0,64},{8,72},{16,80},{24,88},{32,96},{40,104},{48,112},{56,120},{... | collective-permute-start | bytes 393224 | tf_op jit(solution)/shard_map/ppermute | solution.py:452
  19.4 12.3 %collective-permute-start.6 = (bf16[256,256]{1,0:T(8,128)(2,1)S(1)}, bf16[256,256]{1,0:T(8,128)(2,1)S(1)}, u32[]{:S(2)}, u32[]{:S(2)}) collective-permute-start(bf16[256,256]{1,0:T(8,128)(2,1)S(1)} %get-tuple-element.39), channel_id=1, source_target_pairs={{0,128},{8,136},{16,144},{24,152},{32,160},{40,168},{48,176},{56,1... | collective-permute-start | bytes 393224 | tf_op jit(solution)/shard_map/ppermute | solution.py:452
  20.4 11.3 %collective-permute-start.7 = (bf16[256,256]{1,0:T(8,128)(2,1)S(1)}, bf16[256,256]{1,0:T(8,128)(2,1)S(1)}, u32[]{:S(2)}, u32[]{:S(2)}) collective-permute-start(bf16[256,256]{1,0:T(8,128)(2,1)S(1)} %get-tuple-element.40), channel_id=1, source_target_pairs={{0,192},{8,200},{16,208},{24,216},{32,224},{40,232},{48,240},{56,2... | collective-permute-start | bytes 393224 | tf_op jit(solution)/shard_map/ppermute | solution.py:452
  24.5 17.1 %all-to-all-start = ((f32[32,3,4,128]{3,2,1,0:T(4,128)}), f32[32,3,4,128]{3,2,1,0:T(4,128)S(1)}, u32[]{:S(2)}, u32[]{:S(2)}) async-start(f32[32,3,4,128]{3,2,1,0:T(4,128)} %get-tuple-element.35.refs_4_), calls=%async_computation | async-start | bytes 393216 | tf_op jit(solution)/shard_map/all_to_all | solution.py:508
  31.9 21.7 %collective-permute-start.13 = (bf16[256,1024]{1,0:T(8,128)(2,1)S(1)}, bf16[256,1024]{1,0:T(8,128)(2,1)}, u32[]{:S(2)}, u32[]{:S(2)}) collective-permute-start(bf16[256,1024]{1,0:T(8,128)(2,1)S(1)} %stack.1.refs_4_.refs_7_), channel_id=1, source_target_pairs={{0,1},{1,0},{2,3},{3,2},{4,5},{5,4},{6,7},{7,6},{8,9},{9,8},{10,11... | collective-permute-start | bytes 1572872 | tf_op jit(solution)/shard_map/ppermute | solution.py:463
  32.4 6.3 %collective-permute-start.8 = (bf16[96,256]{1,0:T(8,128)(2,1)S(1)}, bf16[96,256]{1,0:T(8,128)(2,1)S(1)}, u32[]{:S(2)}, u32[]{:S(2)}) collective-permute-start(bf16[96,256]{1,0:T(8,128)(2,1)S(1)} %backward_sends.1), channel_id=1, source_target_pairs={{8,0},{16,8},{24,16},{32,24},{40,32},{48,40},{56,48},{64,56},{72,6... | collective-permute-start | bytes 147464 | tf_op jit(solution)/shard_map/ppermute | solution.py:445
  42.9 16.9 %collective-permute-start.9 = (bf16[4,256,256]{2,1,0:T(8,128)(2,1)S(1)}, bf16[4,256,256]{2,1,0:T(8,128)(2,1)}, u32[]{:S(2)}, u32[]{:S(2)}) collective-permute-start(bf16[4,256,256]{2,1,0:T(8,128)(2,1)S(1)} %project.1.refs_8_), channel_id=1, source_target_pairs={{0,1},{1,0},{2,3},{3,2},{4,5},{5,4},{6,7},{7,6},{8,9},{9,8},{10,11... | collective-permute-start | bytes 1572872 | tf_op jit(solution)/shard_map/ppermute | solution.py:463
  43.0 6.4 %collective-permute-start.10 = (bf16[256,256]{1,0:T(8,128)(2,1)S(1)}, bf16[256,256]{1,0:T(8,128)(2,1)S(1)}, u32[]{:S(2)}, u32[]{:S(2)}) collective-permute-start(bf16[256,256]{1,0:T(8,128)(2,1)S(1)} %get-tuple-element.41.refs_0_), channel_id=1, source_target_pairs={{0,64},{8,72},{16,80},{24,88},{32,96},{40,104},{48,112},{56,120},{... | collective-permute-start | bytes 393224 | tf_op jit(solution)/shard_map/ppermute | solution.py:452
  43.8 7.8 %collective-permute-start.11 = (bf16[256,256]{1,0:T(8,128)(2,1)S(1)}, bf16[256,256]{1,0:T(8,128)(2,1)S(1)}, u32[]{:S(2)}, u32[]{:S(2)}) collective-permute-start(bf16[256,256]{1,0:T(8,128)(2,1)S(1)} %get-tuple-element.41.refs_0_), channel_id=1, source_target_pairs={{0,128},{8,136},{16,144},{24,152},{32,160},{40,168},{48,176},{56,1... | collective-permute-start | bytes 393224 | tf_op jit(solution)/shard_map/ppermute | solution.py:452
  46.6 7.1 %collective-permute-start.12 = (bf16[256,256]{1,0:T(8,128)(2,1)S(1)}, bf16[256,256]{1,0:T(8,128)(2,1)S(1)}, u32[]{:S(2)}, u32[]{:S(2)}) collective-permute-start(bf16[256,256]{1,0:T(8,128)(2,1)S(1)} %get-tuple-element.41.refs_0_), channel_id=1, source_target_pairs={{0,192},{8,200},{16,208},{24,216},{32,224},{40,232},{48,240},{56,2... | collective-permute-start | bytes 393224 | tf_op jit(solution)/shard_map/ppermute | solution.py:452
  55.9 15.7 %all-to-all-start.1 = ((bf16[8,64,256]{2,1,0:T(8,128)(2,1)}), bf16[8,64,256]{2,1,0:T(8,128)(2,1)S(1)}, u32[]{:S(2)}, u32[]{:S(2)}) async-start(bf16[8,64,256]{2,1,0:T(8,128)(2,1)} %weight_pieces.1.refs_3_), calls=%async_computation.1 | async-start | bytes 524288 | tf_op jit(solution)/shard_map/all_to_all | solution.py:539
  61.2 11.0 %collective-permute-start.14 = (bf16[256,256]{1,0:T(8,128)(2,1)S(1)}, bf16[256,256]{1,0:T(8,128)(2,1)S(1)}, u32[]{:S(2)}, u32[]{:S(2)}) collective-permute-start(bf16[256,256]{1,0:T(8,128)(2,1)S(1)} %get-tuple-element.44), channel_id=1, source_target_pairs={{0,2},{1,3},{2,4},{3,5},{4,6},{5,7},{6,0},{7,1},{8,10},{9,11},{10,... | collective-permute-start | bytes 393224 | tf_op jit(solution)/shard_map/ppermute | solution.py:459
  61.9 10.3 %collective-permute-start.15 = (bf16[256,256]{1,0:T(8,128)(2,1)S(1)}, bf16[256,256]{1,0:T(8,128)(2,1)S(1)}, u32[]{:S(2)}, u32[]{:S(2)}) collective-permute-start(bf16[256,256]{1,0:T(8,128)(2,1)S(1)} %get-tuple-element.45), channel_id=1, source_target_pairs={{0,4},{1,5},{2,6},{3,7},{4,0},{5,1},{6,2},{7,3},{8,12},{9,13},{10,... | collective-permute-start | bytes 393224 | tf_op jit(solution)/shard_map/ppermute | solution.py:459
  62.7 9.5 %copy-start.1 = (bf16[256,256]{1,0:T(8,128)(2,1)S(1)}, bf16[256,256]{1,0:T(8,128)(2,1)}, u32[]{:S(2)}) copy-start(bf16[256,256]{1,0:T(8,128)(2,1)} %refs_0_.3) | copy-start | bytes 393220
  62.7 9.5 %collective-permute-start.16 = (bf16[256,256]{1,0:T(8,128)(2,1)S(1)}, bf16[256,256]{1,0:T(8,128)(2,1)S(1)}, u32[]{:S(2)}, u32[]{:S(2)}) collective-permute-start(bf16[256,256]{1,0:T(8,128)(2,1)S(1)} %get-tuple-element.46), channel_id=1, source_target_pairs={{0,6},{1,7},{2,0},{3,1},{4,2},{5,3},{6,4},{7,5},{8,14},{9,15},{10,... | collective-permute-start | bytes 393224 | tf_op jit(solution)/shard_map/ppermute | solution.py:459

commit v4 on v3

--- a/solution.py
+++ b/solution.py
@@ -230,16 +230,16 @@
     return lax.rem(y_index() - x_index() - distance + 2 * YSIZE, YSIZE)
 
 
-def pack(own_ref, a_ref, b_ref, c_ref, out_ref, s1_ref, s2_ref, s3_ref):
+def pack(own_ref, a_ref, b_ref, c_ref, out_ref, s0_ref, s1_ref, s2_ref, s3_ref):
     for d, source in enumerate((own_ref, a_ref, b_ref, c_ref)):
         out_ref[d] = source[...]
-    for d, send_ref in ((1, s1_ref), (2, s2_ref), (3, s3_ref)):
+    for d, send_ref in enumerate((s0_ref, s1_ref, s2_ref, s3_ref)):
         send_ref[...] = out_ref[facing(d)]
 
 
-def stack(near_ref, a_ref, b_ref, c_ref, out_ref):
+def stack(own_ref, a_ref, b_ref, c_ref, out_ref):
     width = out_ref.shape[0]
-    for d, block in enumerate((near_ref[facing(0)], a_ref[...], b_ref[...], c_ref[...])):
+    for d, block in enumerate((own_ref[...], a_ref[...], b_ref[...], c_ref[...])):
         out_ref[:, d * width : (d + 1) * width] = jnp.transpose(block.astype(F32)).astype(BF16)
 
 
@@ -477,7 +477,8 @@
     seg = ((nh, 2, SEGS, LANES), F32)
 
     halo = shifted(signal[rows - REACH :], 1)
-    from_y = [along_y(cotangent, d) for d in range(1, YSIZE)]
+    two, one, three = [along_y(cotangent, d) for d in (2, 1, 3)]
+    from_y = [one, two, three]
     par, rb, driven, fhead, shead, own_cot = call(
         gather_inputs,
         [((PARAMS, width), F32), ((rows, LANES), F32), tall, head, head, (square, BF16)],
@@ -495,10 +496,10 @@
         aliases={3: 0}, cost=20,
     )(halo, par, rb, driven, fhead, shead)
 
-    near, c1, c2, c3 = call(pack, [((YSIZE,) + square, BF16)] + [(square, BF16)] * 3)(
+    near, c0, c1, c2, c3 = call(pack, [((YSIZE,) + square, BF16)] + [(square, BF16)] * 4)(
         own_cot, *from_y, after=(segh,)
     )
-    c1, c2, c3 = along_x(c1, 1), along_x(c2, 2), along_x(c3, 3)
+    c2, c1, c3 = along_x(c2, 2), along_x(c1, 1), along_x(c3, 3)
     far = other_core(near)
     grad_mixed, payload = call(
         backward_local,
@@ -507,7 +508,7 @@
     )(near, far, w_out, segp, par, rb, ends)
     got = lax.all_to_all(payload, "seq", 0, 0, tiled=True)
 
-    (chip,) = call(stack, [((width, XSIZE * rows), BF16)])(near, c1, c2, c3, after=(payload,))
+    (chip,) = call(stack, [((width, XSIZE * rows), BF16)])(c0, c1, c2, c3, after=(payload,))
     chip_far = other_core(chip)
     (bhalo,) = call(
         backward_sends, [((REACH, width), BF16)], [vmem((rows, LANES))], cost=20,
@@ -518,7 +519,7 @@
         forward_final, [(square, BF16), ((count, LANES), F32)],
         [vmem((nh, rows, LANES))], cost=20,
     )(got, driven, segh, segp, par, rb, after=(later, chip))
-    f1, f2, f3 = along_x(mixed, 1), along_x(mixed, 2), along_x(mixed, 3)
+    f2, f1, f3 = along_x(mixed, 2), along_x(mixed, 1), along_x(mixed, 3)
 
     (send,) = call(project, [((YSIZE,) + square, BF16)], cost=20)(mixed, w_out)
     pair = other_core(send)
@@ -541,7 +542,7 @@
     own, p1, p2, p3 = call(pair_sum, [(square, F32)] + [(square, BF16)] * 3)(
         mixed, w_out, pair, after=(sums,)
     )
-    p1, p2, p3 = along_y(p1, 1), along_y(p2, 2), along_y(p3, 3)
+    p2, p1, p3 = along_y(p2, 2), along_y(p1, 1), along_y(p3, 3)
 
     (output,) = call(finish_output, [(square, BF16)])(
         signal, own, p1, p2, p3

time: 74.1 us -> 73.2 us (0.988)
  the two profiles are of different devices: /device:TPU:2 before, /device:TPU:1 now
where the time goes in v4:
time: 73.2 us; the launch traced here: 72.7 us
  starting transfers between devices  41.2 us (56%)
  waiting for transfers between devices  19 us (26%)
  Pallas kernels  10.9 us (15%)
  local copies, waits for them, and re-layouts  0.82 us (1%)
  between operations  0.8 us (1%)
    ppermute x6, starting transfers between devices, along_x(): lax.ppermute(block, 'seq', [(i, (i + distance * ZSIZE) % size) for i in r...  11.2 us
    pallas_call x13, Pallas kernels, run(): pl.pallas_call(body, out_shape=tuple((jax.ShapeDtypeStruct(shape, dtype)...  10.9 us
    ppermute x6, starting transfers between devices, along_y(): lax.ppermute(block, 'ch', [(i, (i + 2 * distance) % size) for i in range(...  8.7 us
    ppermute x6, waiting for transfers between devices, along_x(): lax.ppermute(block, 'seq', [(i, (i + distance * ZSIZE) % size) for i in r...  6.8 us
    ppermute x3, starting transfers between devices, other_core(): return lax.ppermute(block, 'ch', [(i, i ^ 1) for i in range(2 * YSIZE)])  6.54 us
    all_to_all x1, starting transfers between devices, per_device(): got = lax.all_to_all(payload, 'seq', 0, 0, tiled=True)  6 us
    all_to_all x1, waiting for transfers between devices, per_device(): lax.all_to_all(sums, 'seq', 0, 0, axis_index_groups=groups, tiled=True)  5.93 us
    ppermute x2, starting transfers between devices, shifted(): lax.ppermute(block, 'seq', [(i - distance, i) for i in devices if i - dis...  4.82 us
  transfers between devices with their start and end apart: 19, of which 6 were waited for; matrix products, arithmetic and copies ran while one was open for 1% of the time, Pallas kernels for 14%

profile of v4, /device:TPU:1, one launch (start us, length us, event | category | flops | bytes accessed | tf_op | source)
XLA Modules:
  0.0 72.7 jit_solution(15548193559962169707)
XLA Ops:
  0.6 2.2 %collective-permute-start = (bf16[256,256]{1,0:T(8,128)(2,1)}, bf16[256,256]{1,0:T(8,128)(2,1)S(1)}, u32[]{:S(2)}, u32[]{:S(2)}) collective-permute-start(bf16[256,256]{1,0:T(8,128)(2,1)} %refs_6_.1), channel_id=1, source_target_pairs={{0,2},{1,3},{2,4},{3,5},{4,6},{5,7},{6,0},{7,1},{8,10},{9,11},{10,... | collective-permute-start | bytes 393224 | tf_op jit(solution)/shard_map/ppermute | solution.py:459
  2.8 1.5 %collective-permute-start.2 = (bf16[256,256]{1,0:T(8,128)(2,1)}, bf16[256,256]{1,0:T(8,128)(2,1)S(1)}, u32[]{:S(2)}, u32[]{:S(2)}) collective-permute-start(bf16[256,256]{1,0:T(8,128)(2,1)} %refs_6_.1), channel_id=1, source_target_pairs={{0,6},{1,7},{2,0},{3,1},{4,2},{5,3},{6,4},{7,5},{8,14},{9,15},{10,... | collective-permute-start | bytes 393224 | tf_op jit(solution)/shard_map/ppermute | solution.py:459
  4.4 1.6 %collective-permute-start.1 = (bf16[256,256]{1,0:T(8,128)(2,1)}, bf16[256,256]{1,0:T(8,128)(2,1)S(1)}, u32[]{:S(2)}, u32[]{:S(2)}) collective-permute-start(bf16[256,256]{1,0:T(8,128)(2,1)} %refs_6_.1), channel_id=1, source_target_pairs={{0,4},{1,5},{2,6},{3,7},{4,0},{5,1},{6,2},{7,3},{8,12},{9,13},{10,... | collective-permute-start | bytes 393224 | tf_op jit(solution)/shard_map/ppermute | solution.py:459
  6.7 3.5 %collective-permute-start.3 = (bf16[96,256]{1,0:T(8,128)(2,1)S(1)}, bf16[96,256]{1,0:T(8,128)(2,1)S(1)}, u32[]{:S(2)}, u32[]{:S(2)}) collective-permute-start(bf16[96,256]{1,0:T(8,128)(2,1)S(1)} %slice.3), channel_id=1, source_target_pairs={{0,8},{8,16},{16,24},{24,32},{32,40},{40,48},{48,56},{56,64},{64,7... | collective-permute-start | bytes 147464 | tf_op jit(solution)/shard_map/ppermute | solution.py:445
  10.3 1.3 %gather_inputs.1 = (f32[24,256]{1,0:T(8,128)S(1)}, f32[256,128]{1,0:T(8,128)S(1)}, f32[2,256,128]{2,1,0:T(8,128)S(1)}, f32[2,48,128]{2,1,0:T(8,128)S(1)}, f32[2,...) custom-call(bf16[256,256]{1,0:T(8,128)(2,1)} %refs_0_.3, f32[2,4,256]{2,1,0:T(4,128)} %refs_1_.3, f32[2,256]{1,0:T(2,128)} %refs_2_.2, ...), custom_call_target="tpu_custom_call" | custom-call | bytes 70000000 | tf_op jit(solution)/shard_map/gather_inputs/pallas_call | solution.py:426
  12.1 2.3 %collective-permute-start.4 = (bf16[4,256,256]{2,1,0:T(8,128)(2,1)S(1)}, bf16[4,256,256]{2,1,0:T(8,128)(2,1)S(1)}, u32[]{:S(2)}, u32[]{:S(2)}) collective-permute-start(bf16[4,256,256]{2,1,0:T(8,128)(2,1)S(1)} %get-tuple-element.33.refs_0_), channel_id=1, source_target_pairs={{0,1},{1,0},{2,3},{3,2},{4,5},{5,4},{6,7},{7,6},{8,9},{9,8},{10,11... | collective-permute-start | bytes 1572872 | tf_op jit(solution)/shard_map/ppermute | solution.py:463
  14.4 5.5 %collective-permute-start.5 = (bf16[256,256]{1,0:T(8,128)(2,1)S(1)}, bf16[256,256]{1,0:T(8,128)(2,1)S(1)}, u32[]{:S(2)}, u32[]{:S(2)}) collective-permute-start(bf16[256,256]{1,0:T(8,128)(2,1)S(1)} %get-tuple-element.40), channel_id=1, source_target_pairs={{0,64},{8,72},{16,80},{24,88},{32,96},{40,104},{48,112},{56,120},{... | collective-permute-start | bytes 393224 | tf_op jit(solution)/shard_map/ppermute | solution.py:452
  19.9 2.7 %collective-permute-start.6 = (bf16[256,256]{1,0:T(8,128)(2,1)S(1)}, bf16[256,256]{1,0:T(8,128)(2,1)S(1)}, u32[]{:S(2)}, u32[]{:S(2)}) collective-permute-start(bf16[256,256]{1,0:T(8,128)(2,1)S(1)} %get-tuple-element.41), channel_id=1, source_target_pairs={{0,128},{8,136},{16,144},{24,152},{32,160},{40,168},{48,176},{56,1... | collective-permute-start | bytes 393224 | tf_op jit(solution)/shard_map/ppermute | solution.py:452
  23.5 1.6 %backward_local.1 = (f32[2,272,128]{2,1,0:T(8,128)S(1)}, f32[32,3,4,128]{3,2,1,0:T(4,128)}) custom-call(bf16[4,256,256]{2,1,0:T(8,128)(2,1)S(1)} %get-tuple-element.33.refs_0_, bf16[4,256,256]{2,1,0:T(8,128)(2,1)S(1)} %collective-permute-done.4.refs_1_, bf16[256,2048]{1,0:T(8,128)(2,1)S(1)} %copy-done, ...), custom_call_target="tpu_custom_call" | custom-call | bytes 70000000 | tf_op jit(solution)/shard_map/backward_local/pallas_call | solution.py:426
  25.1 6.0 %all-to-all-start = ((f32[32,3,4,128]{3,2,1,0:T(4,128)}), f32[32,3,4,128]{3,2,1,0:T(4,128)S(1)}, u32[]{:S(2)}, u32[]{:S(2)}) async-start(f32[32,3,4,128]{3,2,1,0:T(4,128)} %get-tuple-element.36.refs_4_), calls=%async_computation | async-start | bytes 393216 | tf_op jit(solution)/shard_map/all_to_all | solution.py:509
  31.3 1.3 %collective-permute-start.13 = (bf16[256,1024]{1,0:T(8,128)(2,1)S(1)}, bf16[256,1024]{1,0:T(8,128)(2,1)S(1)}, u32[]{:S(2)}, u32[]{:S(2)}) collective-permute-start(bf16[256,1024]{1,0:T(8,128)(2,1)S(1)} %stack.1.refs_4_.refs_7_), channel_id=1, source_target_pairs={{0,1},{1,0},{2,3},{3,2},{4,5},{5,4},{6,7},{7,6},{8,9},{9,8},{10,11... | collective-permute-start | bytes 1572872 | tf_op jit(solution)/shard_map/ppermute | solution.py:463
  33.0 1.3 %collective-permute-start.8 = (bf16[96,256]{1,0:T(8,128)(2,1)S(1)}, bf16[96,256]{1,0:T(8,128)(2,1)S(1)}, u32[]{:S(2)}, u32[]{:S(2)}) collective-permute-start(bf16[96,256]{1,0:T(8,128)(2,1)S(1)} %backward_sends.1), channel_id=1, source_target_pairs={{8,0},{16,8},{24,16},{32,24},{40,32},{48,40},{56,48},{64,56},{72,6... | collective-permute-start | bytes 147464 | tf_op jit(solution)/shard_map/ppermute | solution.py:445
  34.3 4.4 %collective-permute-done.8.refs_6_.refs_4_ = bf16[96,256]{1,0:T(8,128)(2,1)S(1)} collective-permute-done((bf16[96,256]{1,0:T(8,128)(2,1)S(1)}, bf16[96,256]{1,0:T(8,128)(2,1)S(1)}, u32[]{:S(2)}, u32[]{:S(2)}) %collective-permute-start.8) | collective-permute-done | bytes 49184 | tf_op jit(solution)/shard_map/ppermute | solution.py:445
  38.7 1.8 %all-to-all-done.refs_0_ = f32[32,3,4,128]{3,2,1,0:T(4,128)S(1)} async-done(((f32[32,3,4,128]{3,2,1,0:T(4,128)}), f32[32,3,4,128]{3,2,1,0:T(4,128)S(1)}, u32[]{:S(2)}, u32[]{:S(2)}) %all-to-all-start) | async-done | bytes 196640 | tf_op jit(solution)/shard_map/all_to_all | solution.py:509
  41.9 2.9 %collective-permute-start.9 = (bf16[4,256,256]{2,1,0:T(8,128)(2,1)S(1)}, bf16[4,256,256]{2,1,0:T(8,128)(2,1)}, u32[]{:S(2)}, u32[]{:S(2)}) collective-permute-start(bf16[4,256,256]{2,1,0:T(8,128)(2,1)S(1)} %project.1.refs_8_), channel_id=1, source_target_pairs={{0,1},{1,0},{2,3},{3,2},{4,5},{5,4},{6,7},{7,6},{8,9},{9,8},{10,11... | collective-permute-start | bytes 1572872 | tf_op jit(solution)/shard_map/ppermute | solution.py:463
  45.7 1.2 %collective-permute-start.11 = (bf16[256,256]{1,0:T(8,128)(2,1)S(1)}, bf16[256,256]{1,0:T(8,128)(2,1)S(1)}, u32[]{:S(2)}, u32[]{:S(2)}) collective-permute-start(bf16[256,256]{1,0:T(8,128)(2,1)S(1)} %get-tuple-element.43.refs_0_), channel_id=1, source_target_pairs={{0,128},{8,136},{16,144},{24,152},{32,160},{40,168},{48,176},{56,1... | collective-permute-start | bytes 393224 | tf_op jit(solution)/shard_map/ppermute | solution.py:452
  47.0 1.7 %backward_final.1.refs_6_ = bf16[256,256]{1,0:T(8,128)(2,1)} custom-call(f32[32,3,4,128]{3,2,1,0:T(4,128)S(1)} %all-to-all-done.refs_0_, f32[32,128]{1,0:T(8,128)S(1)} %get-tuple-element.44.refs_1_, f32[2,272,128]{2,1,0:T(8,128)S(1)} %get-tuple-element.38.refs_0_.refs_2_, f32[2,2,8,128]{3,2,1,0:T(8,128)S(1)} %get-tuple-element.34.refs_3_.refs_1_, ...), custom_call_target="tpu_custom_call" | custom-call | bytes 3500000 | tf_op jit(solution)/shard_map/backward_final/pallas_call | solution.py:426
  49.9 2.1 %collective-permute-done.11.refs_2_ = bf16[256,256]{1,0:T(8,128)(2,1)S(1)} collective-permute-done((bf16[256,256]{1,0:T(8,128)(2,1)S(1)}, bf16[256,256]{1,0:T(8,128)(2,1)S(1)}, u32[]{:S(2)}, u32[]{:S(2)}) %collective-permute-start.11) | collective-permute-done | bytes 131104 | tf_op jit(solution)/shard_map/ppermute | solution.py:452
  51.9 3.5 %collective-permute-done.10.refs_1_ = bf16[256,256]{1,0:T(8,128)(2,1)S(1)} collective-permute-done((bf16[256,256]{1,0:T(8,128)(2,1)S(1)}, bf16[256,256]{1,0:T(8,128)(2,1)S(1)}, u32[]{:S(2)}, u32[]{:S(2)}) %collective-permute-start.10) | collective-permute-done | bytes 131104 | tf_op jit(solution)/shard_map/ppermute | solution.py:452
  56.6 4.0 %all-to-all-start.1 = ((bf16[8,64,256]{2,1,0:T(8,128)(2,1)}), bf16[8,64,256]{2,1,0:T(8,128)(2,1)S(1)}, u32[]{:S(2)}, u32[]{:S(2)}) async-start(bf16[8,64,256]{2,1,0:T(8,128)(2,1)} %weight_pieces.1.refs_3_), calls=%async_computation.1 | async-start | bytes 524288 | tf_op jit(solution)/shard_map/all_to_all | solution.py:540
  60.6 1.3 %pair_sum.1 = (f32[256,256]{1,0:T(8,128)S(1)}, bf16[256,256]{1,0:T(8,128)(2,1)S(1)}, bf16[256,256]{1,0:T(8,128)(2,1)S(1)}, bf16[256,256]{1,0:T(8,128)(2,1)S(1)}) custom-call(bf16[256,256]{1,0:T(8,128)(2,1)S(1)} %get-tuple-element.43.refs_0_, bf16[256,2048]{1,0:T(8,128)(2,1)S(1)} %copy-done, bf16[4,256,256]{2,1,0:T(8,128)(2,1)} %collective-permute-done.9.refs_2_, ...), custom_call_target="tpu_custom_call" | custom-call | bytes 3500000 | tf_op jit(solution)/shard_map/pair_sum/pallas_call | solution.py:426
  62.4 1.6 %collective-permute-start.15 = (bf16[256,256]{1,0:T(8,128)(2,1)S(1)}, bf16[256,256]{1,0:T(8,128)(2,1)S(1)}, u32[]{:S(2)}, u32[]{:S(2)}) collective-permute-start(bf16[256,256]{1,0:T(8,128)(2,1)S(1)} %get-tuple-element.47), channel_id=1, source_target_pairs={{0,4},{1,5},{2,6},{3,7},{4,0},{5,1},{6,2},{7,3},{8,12},{9,13},{10,... | collective-permute-start | bytes 393224 | tf_op jit(solution)/shard_map/ppermute | solution.py:459
  64.0 1.4 %collective-permute-start.16 = (bf16[256,256]{1,0:T(8,128)(2,1)S(1)}, bf16[256,256]{1,0:T(8,128)(2,1)S(1)}, u32[]{:S(2)}, u32[]{:S(2)}) collective-permute-start(bf16[256,256]{1,0:T(8,128)(2,1)S(1)} %get-tuple-element.48), channel_id=1, source_target_pairs={{0,6},{1,7},{2,0},{3,1},{4,2},{5,3},{6,4},{7,5},{8,14},{9,15},{10,... | collective-permute-start | bytes 393224 | tf_op jit(solution)/shard_map/ppermute | solution.py:459
  65.4 5.9 %all-to-all-done.1.refs_0_ = bf16[8,64,256]{2,1,0:T(8,128)(2,1)S(1)} async-done(((bf16[8,64,256]{2,1,0:T(8,128)(2,1)}), bf16[8,64,256]{2,1,0:T(8,128)(2,1)S(1)}, u32[]{:S(2)}, u32[]{:S(2)}) %all-to-all-start.1) | async-done | bytes 262176 | tf_op jit(solution)/shard_map/all_to_all | solution.py:540
  (36 shorter events, 9.3 us)
Async XLA Ops:
  0.6 22.9 %copy-start = (bf16[256,2048]{1,0:T(8,128)(2,1)S(1)}, bf16[256,2048]{1,0:T(8,128)(2,1)}, u32[]{:S(2)}) copy-start(bf16[256,2048]{1,0:T(8,128)(2,1)} %refs_1_.5) | copy-start | bytes 3145732
  0.6 11.4 %collective-permute-start = (bf16[256,256]{1,0:T(8,128)(2,1)}, bf16[256,256]{1,0:T(8,128)(2,1)S(1)}, u32[]{:S(2)}, u32[]{:S(2)}) collective-permute-start(bf16[256,256]{1,0:T(8,128)(2,1)} %refs_6_.1), channel_id=1, source_target_pairs={{0,2},{1,3},{2,4},{3,5},{4,6},{5,7},{6,0},{7,1},{8,10},{9,11},{10,... | collective-permute-start | bytes 393224 | tf_op jit(solution)/shard_map/ppermute | solution.py:459
  2.8 9.2 %collective-permute-start.2 = (bf16[256,256]{1,0:T(8,128)(2,1)}, bf16[256,256]{1,0:T(8,128)(2,1)S(1)}, u32[]{:S(2)}, u32[]{:S(2)}) collective-permute-start(bf16[256,256]{1,0:T(8,128)(2,1)} %refs_6_.1), channel_id=1, source_target_pairs={{0,6},{1,7},{2,0},{3,1},{4,2},{5,3},{6,4},{7,5},{8,14},{9,15},{10,... | collective-permute-start | bytes 393224 | tf_op jit(solution)/shard_map/ppermute | solution.py:459
  4.4 7.7 %collective-permute-start.1 = (bf16[256,256]{1,0:T(8,128)(2,1)}, bf16[256,256]{1,0:T(8,128)(2,1)S(1)}, u32[]{:S(2)}, u32[]{:S(2)}) collective-permute-start(bf16[256,256]{1,0:T(8,128)(2,1)} %refs_6_.1), channel_id=1, source_target_pairs={{0,4},{1,5},{2,6},{3,7},{4,0},{5,1},{6,2},{7,3},{8,12},{9,13},{10,... | collective-permute-start | bytes 393224 | tf_op jit(solution)/shard_map/ppermute | solution.py:459
  6.7 4.8 %collective-permute-start.3 = (bf16[96,256]{1,0:T(8,128)(2,1)S(1)}, bf16[96,256]{1,0:T(8,128)(2,1)S(1)}, u32[]{:S(2)}, u32[]{:S(2)}) collective-permute-start(bf16[96,256]{1,0:T(8,128)(2,1)S(1)} %slice.3), channel_id=1, source_target_pairs={{0,8},{8,16},{16,24},{24,32},{32,40},{40,48},{48,56},{56,64},{64,7... | collective-permute-start | bytes 147464 | tf_op jit(solution)/shard_map/ppermute | solution.py:445
  12.1 11.4 %collective-permute-start.4 = (bf16[4,256,256]{2,1,0:T(8,128)(2,1)S(1)}, bf16[4,256,256]{2,1,0:T(8,128)(2,1)S(1)}, u32[]{:S(2)}, u32[]{:S(2)}) collective-permute-start(bf16[4,256,256]{2,1,0:T(8,128)(2,1)S(1)} %get-tuple-element.33.refs_0_), channel_id=1, source_target_pairs={{0,1},{1,0},{2,3},{3,2},{4,5},{5,4},{6,7},{7,6},{8,9},{9,8},{10,11... | collective-permute-start | bytes 1572872 | tf_op jit(solution)/shard_map/ppermute | solution.py:463
  14.4 16.6 %collective-permute-start.5 = (bf16[256,256]{1,0:T(8,128)(2,1)S(1)}, bf16[256,256]{1,0:T(8,128)(2,1)S(1)}, u32[]{:S(2)}, u32[]{:S(2)}) collective-permute-start(bf16[256,256]{1,0:T(8,128)(2,1)S(1)} %get-tuple-element.40), channel_id=1, source_target_pairs={{0,64},{8,72},{16,80},{24,88},{32,96},{40,104},{48,112},{56,120},{... | collective-permute-start | bytes 393224 | tf_op jit(solution)/shard_map/ppermute | solution.py:452
  19.9 11.2 %collective-permute-start.6 = (bf16[256,256]{1,0:T(8,128)(2,1)S(1)}, bf16[256,256]{1,0:T(8,128)(2,1)S(1)}, u32[]{:S(2)}, u32[]{:S(2)}) collective-permute-start(bf16[256,256]{1,0:T(8,128)(2,1)S(1)} %get-tuple-element.41), channel_id=1, source_target_pairs={{0,128},{8,136},{16,144},{24,152},{32,160},{40,168},{48,176},{56,1... | collective-permute-start | bytes 393224 | tf_op jit(solution)/shard_map/ppermute | solution.py:452
  22.7 8.5 %collective-permute-start.7 = (bf16[256,256]{1,0:T(8,128)(2,1)S(1)}, bf16[256,256]{1,0:T(8,128)(2,1)S(1)}, u32[]{:S(2)}, u32[]{:S(2)}) collective-permute-start(bf16[256,256]{1,0:T(8,128)(2,1)S(1)} %get-tuple-element.42), channel_id=1, source_target_pairs={{0,192},{8,200},{16,208},{24,216},{32,224},{40,232},{48,240},{56,2... | collective-permute-start | bytes 393224 | tf_op jit(solution)/shard_map/ppermute | solution.py:452
  25.1 15.4 %all-to-all-start = ((f32[32,3,4,128]{3,2,1,0:T(4,128)}), f32[32,3,4,128]{3,2,1,0:T(4,128)S(1)}, u32[]{:S(2)}, u32[]{:S(2)}) async-start(f32[32,3,4,128]{3,2,1,0:T(4,128)} %get-tuple-element.36.refs_4_), calls=%async_computation | async-start | bytes 393216 | tf_op jit(solution)/shard_map/all_to_all | solution.py:509
  31.3 24.1 %collective-permute-start.13 = (bf16[256,1024]{1,0:T(8,128)(2,1)S(1)}, bf16[256,1024]{1,0:T(8,128)(2,1)S(1)}, u32[]{:S(2)}, u32[]{:S(2)}) collective-permute-start(bf16[256,1024]{1,0:T(8,128)(2,1)S(1)} %stack.1.refs_4_.refs_7_), channel_id=1, source_target_pairs={{0,1},{1,0},{2,3},{3,2},{4,5},{5,4},{6,7},{7,6},{8,9},{9,8},{10,11... | collective-permute-start | bytes 1572872 | tf_op jit(solution)/shard_map/ppermute | solution.py:463
  33.0 5.7 %collective-permute-start.8 = (bf16[96,256]{1,0:T(8,128)(2,1)S(1)}, bf16[96,256]{1,0:T(8,128)(2,1)S(1)}, u32[]{:S(2)}, u32[]{:S(2)}) collective-permute-start(bf16[96,256]{1,0:T(8,128)(2,1)S(1)} %backward_sends.1), channel_id=1, source_target_pairs={{8,0},{16,8},{24,16},{32,24},{40,32},{48,40},{56,48},{64,56},{72,6... | collective-permute-start | bytes 147464 | tf_op jit(solution)/shard_map/ppermute | solution.py:445
  38.7 2.8 %copy-start.2 = (bf16[96,256]{1,0:T(8,128)(2,1)}, bf16[96,256]{1,0:T(8,128)(2,1)S(1)}, u32[]{:S(2)}) copy-start(bf16[96,256]{1,0:T(8,128)(2,1)S(1)} %collective-permute-done.8.refs_6_.refs_4_) | copy-start | bytes 147460
  41.5 5.4 %copy-start.3 = (bf16[96,256]{1,0:T(8,128)(2,1)S(1)}, bf16[96,256]{1,0:T(8,128)(2,1)}, u32[]{:S(2)}) copy-start(bf16[96,256]{1,0:T(8,128)(2,1)} %copy-done.2) | copy-start | bytes 147460
  41.9 18.7 %collective-permute-start.9 = (bf16[4,256,256]{2,1,0:T(8,128)(2,1)S(1)}, bf16[4,256,256]{2,1,0:T(8,128)(2,1)}, u32[]{:S(2)}, u32[]{:S(2)}) collective-permute-start(bf16[4,256,256]{2,1,0:T(8,128)(2,1)S(1)} %project.1.refs_8_), channel_id=1, source_target_pairs={{0,1},{1,0},{2,3},{3,2},{4,5},{5,4},{6,7},{7,6},{8,9},{9,8},{10,11... | collective-permute-start | bytes 1572872 | tf_op jit(solution)/shard_map/ppermute | solution.py:463
  44.8 5.1 %collective-permute-start.12 = (bf16[256,256]{1,0:T(8,128)(2,1)S(1)}, bf16[256,256]{1,0:T(8,128)(2,1)S(1)}, u32[]{:S(2)}, u32[]{:S(2)}) collective-permute-start(bf16[256,256]{1,0:T(8,128)(2,1)S(1)} %get-tuple-element.43.refs_0_), channel_id=1, source_target_pairs={{0,192},{8,200},{16,208},{24,216},{32,224},{40,232},{48,240},{56,2... | collective-permute-start | bytes 393224 | tf_op jit(solution)/shard_map/ppermute | solution.py:452
  45.7 6.2 %collective-permute-start.11 = (bf16[256,256]{1,0:T(8,128)(2,1)S(1)}, bf16[256,256]{1,0:T(8,128)(2,1)S(1)}, u32[]{:S(2)}, u32[]{:S(2)}) collective-permute-start(bf16[256,256]{1,0:T(8,128)(2,1)S(1)} %get-tuple-element.43.refs_0_), channel_id=1, source_target_pairs={{0,128},{8,136},{16,144},{24,152},{32,160},{40,168},{48,176},{56,1... | collective-permute-start | bytes 393224 | tf_op jit(solution)/shard_map/ppermute | solution.py:452
  47.0 8.5 %collective-permute-start.10 = (bf16[256,256]{1,0:T(8,128)(2,1)S(1)}, bf16[256,256]{1,0:T(8,128)(2,1)S(1)}, u32[]{:S(2)}, u32[]{:S(2)}) collective-permute-start(bf16[256,256]{1,0:T(8,128)(2,1)S(1)} %get-tuple-element.43.refs_0_), channel_id=1, source_target_pairs={{0,64},{8,72},{16,80},{24,88},{32,96},{40,104},{48,112},{56,120},{... | collective-permute-start | bytes 393224 | tf_op jit(solution)/shard_map/ppermute | solution.py:452
  56.6 14.7 %all-to-all-start.1 = ((bf16[8,64,256]{2,1,0:T(8,128)(2,1)}), bf16[8,64,256]{2,1,0:T(8,128)(2,1)S(1)}, u32[]{:S(2)}, u32[]{:S(2)}) async-start(bf16[8,64,256]{2,1,0:T(8,128)(2,1)} %weight_pieces.1.refs_3_), calls=%async_computation.1 | async-start | bytes 524288 | tf_op jit(solution)/shard_map/all_to_all | solution.py:540
  62.0 10.0 %collective-permute-start.14 = (bf16[256,256]{1,0:T(8,128)(2,1)S(1)}, bf16[256,256]{1,0:T(8,128)(2,1)S(1)}, u32[]{:S(2)}, u32[]{:S(2)}) collective-permute-start(bf16[256,256]{1,0:T(8,128)(2,1)S(1)} %get-tuple-element.46), channel_id=1, source_target_pairs={{0,2},{1,3},{2,4},{3,5},{4,6},{5,7},{6,0},{7,1},{8,10},{9,11},{10,... | collective-permute-start | bytes 393224 | tf_op jit(solution)/shard_map/ppermute | solution.py:459
  62.4 9.5 %collective-permute-start.15 = (bf16[256,256]{1,0:T(8,128)(2,1)S(1)}, bf16[256,256]{1,0:T(8,128)(2,1)S(1)}, u32[]{:S(2)}, u32[]{:S(2)}) collective-permute-start(bf16[256,256]{1,0:T(8,128)(2,1)S(1)} %get-tuple-element.47), channel_id=1, source_target_pairs={{0,4},{1,5},{2,6},{3,7},{4,0},{5,1},{6,2},{7,3},{8,12},{9,13},{10,... | collective-permute-start | bytes 393224 | tf_op jit(solution)/shard_map/ppermute | solution.py:459
  64.0 8.0 %copy-start.1 = (bf16[256,256]{1,0:T(8,128)(2,1)S(1)}, bf16[256,256]{1,0:T(8,128)(2,1)}, u32[]{:S(2)}) copy-start(bf16[256,256]{1,0:T(8,128)(2,1)} %refs_0_.3) | copy-start | bytes 393220
  64.0 8.0 %collective-permute-start.16 = (bf16[256,256]{1,0:T(8,128)(2,1)S(1)}, bf16[256,256]{1,0:T(8,128)(2,1)S(1)}, u32[]{:S(2)}, u32[]{:S(2)}) collective-permute-start(bf16[256,256]{1,0:T(8,128)(2,1)S(1)} %get-tuple-element.48), channel_id=1, source_target_pairs={{0,6},{1,7},{2,0},{3,1},{4,2},{5,3},{6,4},{7,5},{8,14},{9,15},{10,... | collective-permute-start | bytes 393224 | tf_op jit(solution)/shard_map/ppermute | solution.py:459

commit v5 on v4

--- a/solution.py
+++ b/solution.py
@@ -532,17 +532,18 @@
         ],
         cost=1,
     )(got, rprod, grad_mixed, segp, later, rb, par, own_cot, after=(send,))
+    own, p1, p2, p3 = call(pair_sum, [(square, F32)] + [(square, BF16)] * 3)(
+        mixed, w_out, pair,
+        after=(pltpu.with_memory_space_constraint(grad_signal, pltpu.HBM),),
+    )
+    p2, p1, p3 = along_y(p2, 2), along_y(p1, 1), along_y(p3, 3)
+
     groups = [[x * ZSIZE + z for z in range(ZSIZE)] for x in range(XSIZE)]
     wide = 2 * width // ZSIZE
     (sums,) = call(weight_pieces, [((ZSIZE, wide, width), BF16)], cost=20)(
-        mixed, f1, f2, f3, chip, chip_far, after=(pltpu.with_memory_space_constraint(grad_signal, pltpu.HBM),)
+        mixed, f1, f2, f3, chip, chip_far, after=(own,)
     )
     pieces = lax.all_to_all(sums, "seq", 0, 0, axis_index_groups=groups, tiled=True)
-
-    own, p1, p2, p3 = call(pair_sum, [(square, F32)] + [(square, BF16)] * 3)(
-        mixed, w_out, pair, after=(sums,)
-    )
-    p2, p1, p3 = along_y(p2, 2), along_y(p1, 1), along_y(p3, 3)
 
     (output,) = call(finish_output, [(square, BF16)])(
         signal, own, p1, p2, p3

time: 73.2 us -> 80.9 us (1.11)
  the two profiles are of different devices: /device:TPU:1 before, /device:TPU:8 now
where the time goes in v5:
time: 80.9 us; the launch traced here: 80.5 us
  starting transfers between devices  42.7 us (53%)
  waiting for transfers between devices  26.4 us (33%)
  Pallas kernels  9.87 us (12%)
  local copies, waits for them, and re-layouts  0.81 us (1%)
    all_to_all x1, starting transfers between devices, per_device(): got = lax.all_to_all(payload, 'seq', 0, 0, tiled=True)  12.9 us
    ppermute x6, waiting for transfers between devices, along_x(): lax.ppermute(block, 'seq', [(i, (i + distance * ZSIZE) % size) for i in r...  12.1 us
    ppermute x6, starting transfers between devices, along_x(): lax.ppermute(block, 'seq', [(i, (i + distance * ZSIZE) % size) for i in r...  10.1 us
    pallas_call x13, Pallas kernels, run(): pl.pallas_call(body, out_shape=tuple((jax.ShapeDtypeStruct(shape, dtype)...  9.87 us
    ppermute x6, starting transfers between devices, along_y(): lax.ppermute(block, 'ch', [(i, (i + 2 * distance) % size) for i in range(...  8.26 us
    ppermute x6, waiting for transfers between devices, along_y(): lax.ppermute(block, 'ch', [(i, (i + 2 * distance) % size) for i in range(...  5.96 us
    all_to_all x1, starting transfers between devices, per_device(): lax.all_to_all(sums, 'seq', 0, 0, axis_index_groups=groups, tiled=True)  5.6 us
    ppermute x2, waiting for transfers between devices, shifted(): lax.ppermute(block, 'seq', [(i - distance, i) for i in devices if i - dis...  5.13 us
  transfers between devices with their start and end apart: 19, of which 12 were waited for; matrix products, arithmetic and copies ran while one was open for 1% of the time, Pallas kernels for 6%

profile of v5, /device:TPU:8, one launch (start us, length us, event | category | flops | bytes accessed | tf_op | source)
XLA Modules:
  0.0 80.5 jit_solution(9341339792123947875)
XLA Ops:
  0.6 1.7 %collective-permute-start = (bf16[256,256]{1,0:T(8,128)(2,1)}, bf16[256,256]{1,0:T(8,128)(2,1)S(1)}, u32[]{:S(2)}, u32[]{:S(2)}) collective-permute-start(bf16[256,256]{1,0:T(8,128)(2,1)} %refs_6_.1), channel_id=1, source_target_pairs={{0,2},{1,3},{2,4},{3,5},{4,6},{5,7},{6,0},{7,1},{8,10},{9,11},{10,... | collective-permute-start | bytes 393224 | tf_op jit(solution)/shard_map/ppermute | solution.py:459
  3.0 2.0 %collective-permute-start.1 = (bf16[256,256]{1,0:T(8,128)(2,1)}, bf16[256,256]{1,0:T(8,128)(2,1)S(1)}, u32[]{:S(2)}, u32[]{:S(2)}) collective-permute-start(bf16[256,256]{1,0:T(8,128)(2,1)} %refs_6_.1), channel_id=1, source_target_pairs={{0,4},{1,5},{2,6},{3,7},{4,0},{5,1},{6,2},{7,3},{8,12},{9,13},{10,... | collective-permute-start | bytes 393224 | tf_op jit(solution)/shard_map/ppermute | solution.py:459
  5.8 3.8 %collective-permute-start.3 = (bf16[96,256]{1,0:T(8,128)(2,1)S(1)}, bf16[96,256]{1,0:T(8,128)(2,1)S(1)}, u32[]{:S(2)}, u32[]{:S(2)}) collective-permute-start(bf16[96,256]{1,0:T(8,128)(2,1)S(1)} %slice.3), channel_id=1, source_target_pairs={{0,8},{8,16},{16,24},{24,32},{32,40},{40,48},{48,56},{56,64},{64,7... | collective-permute-start | bytes 147464 | tf_op jit(solution)/shard_map/ppermute | solution.py:445
  12.1 1.9 %collective-permute-done.4.refs_1_ = bf16[4,256,256]{2,1,0:T(8,128)(2,1)S(1)} collective-permute-done((bf16[4,256,256]{2,1,0:T(8,128)(2,1)S(1)}, bf16[4,256,256]{2,1,0:T(8,128)(2,1)S(1)}, u32[]{:S(2)}, u32[]{:S(2)}) %collective-permute-start.4) | collective-permute-done | bytes 524320 | tf_op jit(solution)/shard_map/ppermute | solution.py:463
  14.0 1.6 %backward_local.1 = (f32[2,272,128]{2,1,0:T(8,128)S(1)}, f32[32,3,4,128]{3,2,1,0:T(4,128)}) custom-call(bf16[4,256,256]{2,1,0:T(8,128)(2,1)S(1)} %get-tuple-element.33.refs_0_, bf16[4,256,256]{2,1,0:T(8,128)(2,1)S(1)} %collective-permute-done.4.refs_1_, bf16[256,2048]{1,0:T(8,128)(2,1)S(1)} %copy-done, ...), custom_call_target="tpu_custom_call" | custom-call | bytes 70000000 | tf_op jit(solution)/shard_map/backward_local/pallas_call | solution.py:426
  15.5 12.9 %all-to-all-start = ((f32[32,3,4,128]{3,2,1,0:T(4,128)}), f32[32,3,4,128]{3,2,1,0:T(4,128)S(1)}, u32[]{:S(2)}, u32[]{:S(2)}) async-start(f32[32,3,4,128]{3,2,1,0:T(4,128)} %get-tuple-element.36.refs_4_), calls=%async_computation | async-start | bytes 393216 | tf_op jit(solution)/shard_map/all_to_all | solution.py:509
  28.5 1.9 %collective-permute-start.5 = (bf16[256,256]{1,0:T(8,128)(2,1)S(1)}, bf16[256,256]{1,0:T(8,128)(2,1)S(1)}, u32[]{:S(2)}, u32[]{:S(2)}) collective-permute-start(bf16[256,256]{1,0:T(8,128)(2,1)S(1)} %get-tuple-element.40), channel_id=1, source_target_pairs={{0,64},{8,72},{16,80},{24,88},{32,96},{40,104},{48,112},{56,120},{... | collective-permute-start | bytes 393224 | tf_op jit(solution)/shard_map/ppermute | solution.py:452
  30.4 2.7 %collective-permute-start.6 = (bf16[256,256]{1,0:T(8,128)(2,1)S(1)}, bf16[256,256]{1,0:T(8,128)(2,1)S(1)}, u32[]{:S(2)}, u32[]{:S(2)}) collective-permute-start(bf16[256,256]{1,0:T(8,128)(2,1)S(1)} %get-tuple-element.41), channel_id=1, source_target_pairs={{0,128},{8,136},{16,144},{24,152},{32,160},{40,168},{48,176},{56,1... | collective-permute-start | bytes 393224 | tf_op jit(solution)/shard_map/ppermute | solution.py:452
  33.1 1.4 %collective-permute-start.7 = (bf16[256,256]{1,0:T(8,128)(2,1)S(1)}, bf16[256,256]{1,0:T(8,128)(2,1)S(1)}, u32[]{:S(2)}, u32[]{:S(2)}) collective-permute-start(bf16[256,256]{1,0:T(8,128)(2,1)S(1)} %get-tuple-element.42), channel_id=1, source_target_pairs={{0,192},{8,200},{16,208},{24,216},{32,224},{40,232},{48,240},{56,2... | collective-permute-start | bytes 393224 | tf_op jit(solution)/shard_map/ppermute | solution.py:452
  34.5 1.8 %collective-permute-done.5.refs_1_ = bf16[256,256]{1,0:T(8,128)(2,1)S(1)} collective-permute-done((bf16[256,256]{1,0:T(8,128)(2,1)S(1)}, bf16[256,256]{1,0:T(8,128)(2,1)S(1)}, u32[]{:S(2)}, u32[]{:S(2)}) %collective-permute-start.5) | collective-permute-done | bytes 131104 | tf_op jit(solution)/shard_map/ppermute | solution.py:452
  36.3 4.6 %collective-permute-done.6.refs_2_ = bf16[256,256]{1,0:T(8,128)(2,1)S(1)} collective-permute-done((bf16[256,256]{1,0:T(8,128)(2,1)S(1)}, bf16[256,256]{1,0:T(8,128)(2,1)S(1)}, u32[]{:S(2)}, u32[]{:S(2)}) %collective-permute-start.6) | collective-permute-done | bytes 131104 | tf_op jit(solution)/shard_map/ppermute | solution.py:452
  42.7 4.7 %collective-permute-done.8.refs_6_.refs_4_ = bf16[96,256]{1,0:T(8,128)(2,1)S(1)} collective-permute-done((bf16[96,256]{1,0:T(8,128)(2,1)S(1)}, bf16[96,256]{1,0:T(8,128)(2,1)S(1)}, u32[]{:S(2)}, u32[]{:S(2)}) %collective-permute-start.8) | collective-permute-done | bytes 49184 | tf_op jit(solution)/shard_map/ppermute | solution.py:445
  49.4 2.3 %collective-permute-start.15 = (bf16[256,256]{1,0:T(8,128)(2,1)S(1)}, bf16[256,256]{1,0:T(8,128)(2,1)S(1)}, u32[]{:S(2)}, u32[]{:S(2)}) collective-permute-start(bf16[256,256]{1,0:T(8,128)(2,1)S(1)} %get-tuple-element.43.refs_0_), channel_id=1, source_target_pairs={{0,192},{8,200},{16,208},{24,216},{32,224},{40,232},{48,240},{56,2... | collective-permute-start | bytes 393224 | tf_op jit(solution)/shard_map/ppermute | solution.py:452
  51.7 1.5 %collective-permute-start.14 = (bf16[256,256]{1,0:T(8,128)(2,1)S(1)}, bf16[256,256]{1,0:T(8,128)(2,1)S(1)}, u32[]{:S(2)}, u32[]{:S(2)}) collective-permute-start(bf16[256,256]{1,0:T(8,128)(2,1)S(1)} %get-tuple-element.43.refs_0_), channel_id=1, source_target_pairs={{0,128},{8,136},{16,144},{24,152},{32,160},{40,168},{48,176},{56,1... | collective-permute-start | bytes 393224 | tf_op jit(solution)/shard_map/ppermute | solution.py:452
  53.4 1.7 %backward_final.1.refs_3_ = bf16[256,256]{1,0:T(8,128)(2,1)} custom-call(f32[32,3,4,128]{3,2,1,0:T(4,128)S(1)} %all-to-all-done.refs_0_, f32[32,128]{1,0:T(8,128)S(1)} %get-tuple-element.44.refs_1_, f32[2,272,128]{2,1,0:T(8,128)S(1)} %get-tuple-element.38.refs_0_.refs_2_, f32[2,2,8,128]{3,2,1,0:T(8,128)S(1)} %get-tuple-element.34.refs_3_.refs_1_, ...), custom_call_target="tpu_custom_call" | custom-call | bytes 3500000 | tf_op jit(solution)/shard_map/backward_final/pallas_call | solution.py:426
  55.4 2.1 %collective-permute-done.15.refs_3_ = bf16[256,256]{1,0:T(8,128)(2,1)S(1)} collective-permute-done((bf16[256,256]{1,0:T(8,128)(2,1)S(1)}, bf16[256,256]{1,0:T(8,128)(2,1)S(1)}, u32[]{:S(2)}, u32[]{:S(2)}) %collective-permute-start.15) | collective-permute-done | bytes 131104 | tf_op jit(solution)/shard_map/ppermute | solution.py:452
  57.5 2.0 %collective-permute-done.14.refs_2_ = bf16[256,256]{1,0:T(8,128)(2,1)S(1)} collective-permute-done((bf16[256,256]{1,0:T(8,128)(2,1)S(1)}, bf16[256,256]{1,0:T(8,128)(2,1)S(1)}, u32[]{:S(2)}, u32[]{:S(2)}) %collective-permute-start.14) | collective-permute-done | bytes 131104 | tf_op jit(solution)/shard_map/ppermute | solution.py:452
  59.6 1.6 %collective-permute-done.13.refs_1_ = bf16[256,256]{1,0:T(8,128)(2,1)S(1)} collective-permute-done((bf16[256,256]{1,0:T(8,128)(2,1)S(1)}, bf16[256,256]{1,0:T(8,128)(2,1)S(1)}, u32[]{:S(2)}, u32[]{:S(2)}) %collective-permute-start.13) | collective-permute-done | bytes 131104 | tf_op jit(solution)/shard_map/ppermute | solution.py:452
  62.4 5.6 %all-to-all-start.1 = ((bf16[8,64,256]{2,1,0:T(8,128)(2,1)}), bf16[8,64,256]{2,1,0:T(8,128)(2,1)S(1)}, u32[]{:S(2)}, u32[]{:S(2)}) async-start(bf16[8,64,256]{2,1,0:T(8,128)(2,1)} %weight_pieces.1), calls=%async_computation.1 | async-start | bytes 524288 | tf_op jit(solution)/shard_map/all_to_all | solution.py:546
  68.8 2.6 %collective-permute-start.11 = (bf16[256,256]{1,0:T(8,128)(2,1)S(1)}, bf16[256,256]{1,0:T(8,128)(2,1)S(1)}, u32[]{:S(2)}, u32[]{:S(2)}) collective-permute-start(bf16[256,256]{1,0:T(8,128)(2,1)S(1)} %get-tuple-element.47), channel_id=1, source_target_pairs={{0,4},{1,5},{2,6},{3,7},{4,0},{5,1},{6,2},{7,3},{8,12},{9,13},{10,... | collective-permute-start | bytes 393224 | tf_op jit(solution)/shard_map/ppermute | solution.py:459
  71.8 2.4 %collective-permute-done.10.refs_2_ = bf16[256,256]{1,0:T(8,128)(2,1)S(1)} collective-permute-done((bf16[256,256]{1,0:T(8,128)(2,1)S(1)}, bf16[256,256]{1,0:T(8,128)(2,1)S(1)}, u32[]{:S(2)}, u32[]{:S(2)}) %collective-permute-start.10) | collective-permute-done | bytes 131104 | tf_op jit(solution)/shard_map/ppermute | solution.py:459
  74.2 2.2 %collective-permute-done.11.refs_3_ = bf16[256,256]{1,0:T(8,128)(2,1)S(1)} collective-permute-done((bf16[256,256]{1,0:T(8,128)(2,1)S(1)}, bf16[256,256]{1,0:T(8,128)(2,1)S(1)}, u32[]{:S(2)}, u32[]{:S(2)}) %collective-permute-start.11) | collective-permute-done | bytes 131104 | tf_op jit(solution)/shard_map/ppermute | solution.py:459
  76.4 1.4 %collective-permute-done.12.refs_4_ = bf16[256,256]{1,0:T(8,128)(2,1)S(1)} collective-permute-done((bf16[256,256]{1,0:T(8,128)(2,1)S(1)}, bf16[256,256]{1,0:T(8,128)(2,1)S(1)}, u32[]{:S(2)}, u32[]{:S(2)}) %collective-permute-start.12) | collective-permute-done | bytes 131104 | tf_op jit(solution)/shard_map/ppermute | solution.py:459
  78.5 1.3 %all-to-all-done.1.refs_0_ = bf16[8,64,256]{2,1,0:T(8,128)(2,1)S(1)} async-done(((bf16[8,64,256]{2,1,0:T(8,128)(2,1)}), bf16[8,64,256]{2,1,0:T(8,128)(2,1)S(1)}, u32[]{:S(2)}, u32[]{:S(2)}) %all-to-all-start.1) | async-done | bytes 262176 | tf_op jit(solution)/shard_map/all_to_all | solution.py:546
  (32 shorter events, 12.1 us)
Async XLA Ops:
  0.6 13.3 %copy-start = (bf16[256,2048]{1,0:T(8,128)(2,1)S(1)}, bf16[256,2048]{1,0:T(8,128)(2,1)}, u32[]{:S(2)}) copy-start(bf16[256,2048]{1,0:T(8,128)(2,1)} %refs_1_.5) | copy-start | bytes 3145732
  0.6 11.2 %collective-permute-start = (bf16[256,256]{1,0:T(8,128)(2,1)}, bf16[256,256]{1,0:T(8,128)(2,1)S(1)}, u32[]{:S(2)}, u32[]{:S(2)}) collective-permute-start(bf16[256,256]{1,0:T(8,128)(2,1)} %refs_6_.1), channel_id=1, source_target_pairs={{0,2},{1,3},{2,4},{3,5},{4,6},{5,7},{6,0},{7,1},{8,10},{9,11},{10,... | collective-permute-start | bytes 393224 | tf_op jit(solution)/shard_map/ppermute | solution.py:459
  2.3 9.6 %collective-permute-start.2 = (bf16[256,256]{1,0:T(8,128)(2,1)}, bf16[256,256]{1,0:T(8,128)(2,1)S(1)}, u32[]{:S(2)}, u32[]{:S(2)}) collective-permute-start(bf16[256,256]{1,0:T(8,128)(2,1)} %refs_6_.1), channel_id=1, source_target_pairs={{0,6},{1,7},{2,0},{3,1},{4,2},{5,3},{6,4},{7,5},{8,14},{9,15},{10,... | collective-permute-start | bytes 393224 | tf_op jit(solution)/shard_map/ppermute | solution.py:459
  3.0 8.9 %collective-permute-start.1 = (bf16[256,256]{1,0:T(8,128)(2,1)}, bf16[256,256]{1,0:T(8,128)(2,1)S(1)}, u32[]{:S(2)}, u32[]{:S(2)}) collective-permute-start(bf16[256,256]{1,0:T(8,128)(2,1)} %refs_6_.1), channel_id=1, source_target_pairs={{0,4},{1,5},{2,6},{3,7},{4,0},{5,1},{6,2},{7,3},{8,12},{9,13},{10,... | collective-permute-start | bytes 393224 | tf_op jit(solution)/shard_map/ppermute | solution.py:459
  5.8 5.6 %collective-permute-start.3 = (bf16[96,256]{1,0:T(8,128)(2,1)S(1)}, bf16[96,256]{1,0:T(8,128)(2,1)S(1)}, u32[]{:S(2)}, u32[]{:S(2)}) collective-permute-start(bf16[96,256]{1,0:T(8,128)(2,1)S(1)} %slice.3), channel_id=1, source_target_pairs={{0,8},{8,16},{16,24},{24,32},{32,40},{40,48},{48,56},{56,64},{64,7... | collective-permute-start | bytes 147464 | tf_op jit(solution)/shard_map/ppermute | solution.py:445
  12.0 2.0 %collective-permute-start.4 = (bf16[4,256,256]{2,1,0:T(8,128)(2,1)S(1)}, bf16[4,256,256]{2,1,0:T(8,128)(2,1)S(1)}, u32[]{:S(2)}, u32[]{:S(2)}) collective-permute-start(bf16[4,256,256]{2,1,0:T(8,128)(2,1)S(1)} %get-tuple-element.33.refs_0_), channel_id=1, source_target_pairs={{0,1},{1,0},{2,3},{3,2},{4,5},{5,4},{6,7},{7,6},{8,9},{9,8},{10,11... | collective-permute-start | bytes 1572872 | tf_op jit(solution)/shard_map/ppermute | solution.py:463
  15.5 31.8 %all-to-all-start = ((f32[32,3,4,128]{3,2,1,0:T(4,128)}), f32[32,3,4,128]{3,2,1,0:T(4,128)S(1)}, u32[]{:S(2)}, u32[]{:S(2)}) async-start(f32[32,3,4,128]{3,2,1,0:T(4,128)} %get-tuple-element.36.refs_4_), calls=%async_computation | async-start | bytes 393216 | tf_op jit(solution)/shard_map/all_to_all | solution.py:509
  28.5 7.8 %collective-permute-start.5 = (bf16[256,256]{1,0:T(8,128)(2,1)S(1)}, bf16[256,256]{1,0:T(8,128)(2,1)S(1)}, u32[]{:S(2)}, u32[]{:S(2)}) collective-permute-start(bf16[256,256]{1,0:T(8,128)(2,1)S(1)} %get-tuple-element.40), channel_id=1, source_target_pairs={{0,64},{8,72},{16,80},{24,88},{32,96},{40,104},{48,112},{56,120},{... | collective-permute-start | bytes 393224 | tf_op jit(solution)/shard_map/ppermute | solution.py:452
  30.4 10.5 %collective-permute-start.6 = (bf16[256,256]{1,0:T(8,128)(2,1)S(1)}, bf16[256,256]{1,0:T(8,128)(2,1)S(1)}, u32[]{:S(2)}, u32[]{:S(2)}) collective-permute-start(bf16[256,256]{1,0:T(8,128)(2,1)S(1)} %get-tuple-element.41), channel_id=1, source_target_pairs={{0,128},{8,136},{16,144},{24,152},{32,160},{40,168},{48,176},{56,1... | collective-permute-start | bytes 393224 | tf_op jit(solution)/shard_map/ppermute | solution.py:452
  33.1 7.7 %collective-permute-start.7 = (bf16[256,256]{1,0:T(8,128)(2,1)S(1)}, bf16[256,256]{1,0:T(8,128)(2,1)S(1)}, u32[]{:S(2)}, u32[]{:S(2)}) collective-permute-start(bf16[256,256]{1,0:T(8,128)(2,1)S(1)} %get-tuple-element.42), channel_id=1, source_target_pairs={{0,192},{8,200},{16,208},{24,216},{32,224},{40,232},{48,240},{56,2... | collective-permute-start | bytes 393224 | tf_op jit(solution)/shard_map/ppermute | solution.py:452
  41.4 6.0 %collective-permute-start.8 = (bf16[96,256]{1,0:T(8,128)(2,1)S(1)}, bf16[96,256]{1,0:T(8,128)(2,1)S(1)}, u32[]{:S(2)}, u32[]{:S(2)}) collective-permute-start(bf16[96,256]{1,0:T(8,128)(2,1)S(1)} %backward_sends.1), channel_id=1, source_target_pairs={{8,0},{16,8},{24,16},{32,24},{40,32},{48,40},{56,48},{64,56},{72,6... | collective-permute-start | bytes 147464 | tf_op jit(solution)/shard_map/ppermute | solution.py:445
  48.8 6.3 %collective-permute-start.9 = (bf16[4,256,256]{2,1,0:T(8,128)(2,1)S(1)}, bf16[4,256,256]{2,1,0:T(8,128)(2,1)S(1)}, u32[]{:S(2)}, u32[]{:S(2)}) collective-permute-start(bf16[4,256,256]{2,1,0:T(8,128)(2,1)S(1)} %project.1.refs_8_), channel_id=1, source_target_pairs={{0,1},{1,0},{2,3},{3,2},{4,5},{5,4},{6,7},{7,6},{8,9},{9,8},{10,11... | collective-permute-start | bytes 1572872 | tf_op jit(solution)/shard_map/ppermute | solution.py:463
  48.9 12.3 %collective-permute-start.16 = (bf16[256,1024]{1,0:T(8,128)(2,1)S(1)}, bf16[256,1024]{1,0:T(8,128)(2,1)S(1)}, u32[]{:S(2)}, u32[]{:S(2)}) collective-permute-start(bf16[256,1024]{1,0:T(8,128)(2,1)S(1)} %stack.1.refs_4_.refs_7_), channel_id=1, source_target_pairs={{0,1},{1,0},{2,3},{3,2},{4,5},{5,4},{6,7},{7,6},{8,9},{9,8},{10,11... | collective-permute-start | bytes 1572872 | tf_op jit(solution)/shard_map/ppermute | solution.py:463
  49.4 8.2 %collective-permute-start.15 = (bf16[256,256]{1,0:T(8,128)(2,1)S(1)}, bf16[256,256]{1,0:T(8,128)(2,1)S(1)}, u32[]{:S(2)}, u32[]{:S(2)}) collective-permute-start(bf16[256,256]{1,0:T(8,128)(2,1)S(1)} %get-tuple-element.43.refs_0_), channel_id=1, source_target_pairs={{0,192},{8,200},{16,208},{24,216},{32,224},{40,232},{48,240},{56,2... | collective-permute-start | bytes 393224 | tf_op jit(solution)/shard_map/ppermute | solution.py:452
  51.7 7.9 %collective-permute-start.14 = (bf16[256,256]{1,0:T(8,128)(2,1)S(1)}, bf16[256,256]{1,0:T(8,128)(2,1)S(1)}, u32[]{:S(2)}, u32[]{:S(2)}) collective-permute-start(bf16[256,256]{1,0:T(8,128)(2,1)S(1)} %get-tuple-element.43.refs_0_), channel_id=1, source_target_pairs={{0,128},{8,136},{16,144},{24,152},{32,160},{40,168},{48,176},{56,1... | collective-permute-start | bytes 393224 | tf_op jit(solution)/shard_map/ppermute | solution.py:452
  53.1 8.1 %collective-permute-start.13 = (bf16[256,256]{1,0:T(8,128)(2,1)S(1)}, bf16[256,256]{1,0:T(8,128)(2,1)S(1)}, u32[]{:S(2)}, u32[]{:S(2)}) collective-permute-start(bf16[256,256]{1,0:T(8,128)(2,1)S(1)} %get-tuple-element.43.refs_0_), channel_id=1, source_target_pairs={{0,64},{8,72},{16,80},{24,88},{32,96},{40,104},{48,112},{56,120},{... | collective-permute-start | bytes 393224 | tf_op jit(solution)/shard_map/ppermute | solution.py:452
  62.4 15.4 %copy-start.1 = (bf16[256,256]{1,0:T(8,128)(2,1)S(1)}, bf16[256,256]{1,0:T(8,128)(2,1)}, u32[]{:S(2)}) copy-start(bf16[256,256]{1,0:T(8,128)(2,1)} %refs_0_.3) | copy-start | bytes 393220
  62.4 17.5 %all-to-all-start.1 = ((bf16[8,64,256]{2,1,0:T(8,128)(2,1)}), bf16[8,64,256]{2,1,0:T(8,128)(2,1)S(1)}, u32[]{:S(2)}, u32[]{:S(2)}) async-start(bf16[8,64,256]{2,1,0:T(8,128)(2,1)} %weight_pieces.1), calls=%async_computation.1 | async-start | bytes 524288 | tf_op jit(solution)/shard_map/all_to_all | solution.py:546
  68.0 6.2 %collective-permute-start.10 = (bf16[256,256]{1,0:T(8,128)(2,1)S(1)}, bf16[256,256]{1,0:T(8,128)(2,1)S(1)}, u32[]{:S(2)}, u32[]{:S(2)}) collective-permute-start(bf16[256,256]{1,0:T(8,128)(2,1)S(1)} %get-tuple-element.46), channel_id=1, source_target_pairs={{0,2},{1,3},{2,4},{3,5},{4,6},{5,7},{6,0},{7,1},{8,10},{9,11},{10,... | collective-permute-start | bytes 393224 | tf_op jit(solution)/shard_map/ppermute | solution.py:459
  68.8 7.6 %collective-permute-start.11 = (bf16[256,256]{1,0:T(8,128)(2,1)S(1)}, bf16[256,256]{1,0:T(8,128)(2,1)S(1)}, u32[]{:S(2)}, u32[]{:S(2)}) collective-permute-start(bf16[256,256]{1,0:T(8,128)(2,1)S(1)} %get-tuple-element.47), channel_id=1, source_target_pairs={{0,4},{1,5},{2,6},{3,7},{4,0},{5,1},{6,2},{7,3},{8,12},{9,13},{10,... | collective-permute-start | bytes 393224 | tf_op jit(solution)/shard_map/ppermute | solution.py:459
  71.4 6.4 %collective-permute-start.12 = (bf16[256,256]{1,0:T(8,128)(2,1)S(1)}, bf16[256,256]{1,0:T(8,128)(2,1)S(1)}, u32[]{:S(2)}, u32[]{:S(2)}) collective-permute-start(bf16[256,256]{1,0:T(8,128)(2,1)S(1)} %get-tuple-element.48), channel_id=1, source_target_pairs={{0,6},{1,7},{2,0},{3,1},{4,2},{5,3},{6,4},{7,5},{8,14},{9,15},{10,... | collective-permute-start | bytes 393224 | tf_op jit(solution)/shard_map/ppermute | solution.py:459
